TPU v7x, 128 devices: a whole 4x4x4 slice. The times are simulated.
128 devices in a mesh: chan: 64 (over z, y, x), dom: 2 (over core).
Axes of the slice: x: 4, y: 4, z: 4, core: 2. Of those that a mesh axis runs over, the one named last changes fastest.
Arguments:
- amplitudes: bfloat16 [128, 2048, 512], P('chan', None, 'dom'), may hold values from -6 to 6
- recouple: bfloat16 [128, 2048, 2048], P('chan'), may hold values from -0.125 to 0.125
- ladder_int: bfloat16 [128, 2048, 2048], P('chan'), may hold values from -0.125 to 0.125
- cycle_coupling: bfloat16 [128, 512, 512], P('chan', 'dom'), may hold values from -0.375 to 0.375
- drive: bfloat16 [128, 2048, 512], P('chan', None, 'dom'), may hold values from -6 to 6
- eps_part: float32 [128, 2048], P('chan'), may hold values from 0.5 to 2.5
- eps_hole: float32 [128, 512], P('chan', 'dom'), may hold values from -2.5 to -0.5
Outputs:
- new_amplitudes: bfloat16 [128, 2048, 512], P('chan', None, 'dom')
All inputs are finite; a program needn't handle non-finite values.
Results may differ from a plain program's by a relative error of at most 0.0052.
Values may be sent and summed in bfloat16 or wider, within the bound.
No kernel may reach another device: no remote copies, remote signals or barrier semaphores. Data moves between devices by JAX's collectives and lax.ppermute only.
A program may use at most 128 MiB of HBM per device.

v0:
```python
import jax
import jax.numpy as jnp
from jax import lax
from jax.sharding import PartitionSpec as P


def local(amplitudes, recouple, ladder_int, cycle_coupling, drive, eps_part, eps_hole):
    chan_count, row_count, col_count = amplitudes.shape
    peer_count = lax.axis_size("chan")
    seg_rows = row_count // peer_count
    recoupled = jnp.einsum(
        "cpq,cqh->cph", recouple, amplitudes, preferred_element_type=jnp.float32
    ).astype(jnp.bfloat16)
    ph_blocks = lax.all_to_all(
        recoupled.reshape(chan_count, peer_count, seg_rows, col_count),
        "chan",
        split_axis=1,
        concat_axis=1,
        tiled=True,
    )
    ph_blocks = ph_blocks.reshape(chan_count, row_count, col_count)
    pieces_sum = jnp.einsum(
        "cph,chk->cpk", ph_blocks, cycle_coupling, preferred_element_type=jnp.float32
    )
    cycle_term = lax.psum_scatter(pieces_sum, "dom", scatter_dimension=2, tiled=True).astype(
        jnp.bfloat16
    )
    returned = lax.all_to_all(
        cycle_term.reshape(chan_count, peer_count, seg_rows, col_count),
        "chan",
        split_axis=1,
        concat_axis=1,
        tiled=True,
    )
    returned = returned.reshape(chan_count, row_count, col_count)
    ladder = jnp.einsum("cpq,cqh->cph", ladder_int, amplitudes, preferred_element_type=jnp.float32)
    folded = jnp.einsum("cqp,cqh->cph", recouple, returned, preferred_element_type=jnp.float32)
    summed = ladder + folded + drive.astype(jnp.float32)
    denominator = eps_part[:, :, None] - eps_hole[:, None, :]
    return (summed / denominator).astype(jnp.bfloat16)


def solution(mesh):
    placed = (
        P("chan", None, "dom"),
        P("chan", None, None),
        P("chan", None, None),
        P("chan", "dom", None),
        P("chan", None, "dom"),
        P("chan", None),
        P("chan", "dom"),
    )
    return jax.shard_map(
        local, mesh=mesh, in_specs=placed, out_specs=P("chan", None, "dom"), check_vma=False
    )
```

profile of v0, /device:TPU:1, one launch (start us, length us, event | category | flops | bytes accessed | tf_op | source)
XLA Modules:
  0.0 146.8 jit_solution(12834870731059875166)
XLA Ops:
  6.5 0.0 copy-start
  6.5 0.0 reduce-scatter.2.cloned.1.call-start
  6.5 1.6 %copy-done = bf16[2,2048,256]{2,1,0:T(8,128)(2,1)S(1)} copy-done((bf16[2,2048,256]{2,1,0:T(8,128)(2,1)S(1)}, bf16[2,2048,256]{2,1,0:T(8,128)(2,1)}, u32[]{:S(2)}) %copy-start) | copy-done | bytes 2097176
  8.1 8.3 %convolution_convert_fusion = bf16[2,2048,256]{2,1,0:T(8,128)(2,1)S(1)} fusion(bf16[2,2048,2048]{2,1,0:T(8,128)(2,1)} %param.8, bf16[2,2048,256]{2,1,0:T(8,128)(2,1)S(1)} %copy-done), kind=kOutput, calls=%fused_computation.4 | convolution fusion | flops 4296015872 | bytes 20971520 | tf_op jit(solution)/shard_map/cpq,cqh->cph/dot_general | solution.py:11
  16.5 0.2 copy.12
  16.6 0.0 copy-start.2
  16.7 40.3 %all_to_all.10 = bf16[2,64,32,256]{3,2,0,1:T(8,128)(2,1)S(1)} all-to-all(bf16[2,64,32,256]{3,2,0,1:T(8,128)(2,1)S(1)} %copy.12), channel_id=1, replica_groups=mesh['chan'=64,'dom'=2] {'chan'}, dimensions={1} | all-to-all | bytes 4194304 | tf_op jit(solution)/shard_map/all_to_all | solution.py:14
  57.0 0.2 copy.13
  57.2 0.0 copy-done.2
  57.2 4.5 %fusion.4 = f32[2,2048,512]{2,1,0:T(8,128)} fusion(bf16[2,2048,256]{2,1,0:T(8,128)(2,1)S(1)} %bitcast.21, bf16[2,256,512]{2,1,0:T(8,128)(2,1)S(1)} %copy-done.2), kind=kOutput, calls=%fused_computation.6 | convolution fusion | flops 1073741824 | bytes 11010048 | tf_op jit(solution)/shard_map/cph,chk->cpk/dot_general | solution.py:22
  61.7 0.0 reduce-scatter.2.cloned.1.call-update
  61.7 18.7 %reduce-scatter.2.cloned.1.call-done = f32[2,2048,256]{2,1,0:T(8,128)} async-done(((f32[2,2048,512]{2,1,0:T(8,128)}), f32[2,2048,256]{2,1,0:T(8,128)}) %reduce-scatter.2.cloned.1.call-update) | async-done | bytes 4194320 | tf_op jit(solution)/shard_map/reduce_scatter | solution.py:25
  80.4 2.4 %convert_element_type.13 = bf16[2,2048,256]{2,1,0:T(8,128)(2,1)S(1)} convert(f32[2,2048,256]{2,1,0:T(8,128)} %reduce-scatter.2.cloned.1.call-done) | non-fusion elementwise | flops 1048576 | bytes 6291456 | tf_op jit(solution)/shard_map/convert_element_type | solution.py:25
  82.8 1.6 %copy.14 = bf16[2,64,32,256]{3,2,0,1:T(8,128)(2,1)} copy(bf16[2,64,32,256]{3,2,1,0:T(8,128)(2,1)S(1)} %bitcast.20) | data formatting | bytes 4194304 | tf_op jit(solution)/shard_map/reshape | solution.py:29
  84.4 10.6 %all-to-all-start.1 = ((bf16[2,64,32,256]{3,2,0,1:T(8,128)(2,1)}), bf16[2,64,32,256]{3,2,0,1:T(8,128)(2,1)}, u32[]{:S(2)}, u32[]{:S(2)}) async-start(bf16[2,64,32,256]{3,2,0,1:T(8,128)(2,1)} %copy.14), calls=%async_computation.2 | async-start | bytes 4194304 | tf_op jit(solution)/shard_map/all_to_all | solution.py:28
  95.0 10.1 %fusion.3 = f32[2,2048,256]{2,1,0:T(8,128)} fusion(bf16[2,2048,2048]{2,1,0:T(8,128)(2,1)} %param.9, bf16[2,2048,256]{2,1,0:T(8,128)(2,1)S(1)} %copy-done), kind=kOutput, calls=%fused_computation.5 | convolution fusion | flops 4294967296 | bytes 23068672 | tf_op jit(solution)/shard_map/cpq,cqh->cph/dot_general | solution.py:36
  105.0 0.0 copy-start.3
  105.0 0.0 copy-start.4
  105.1 18.7 %all-to-all-done.1 = bf16[2,64,32,256]{3,2,0,1:T(8,128)(2,1)} async-done(((bf16[2,64,32,256]{3,2,0,1:T(8,128)(2,1)}), bf16[2,64,32,256]{3,2,0,1:T(8,128)(2,1)}, u32[]{:S(2)}, u32[]{:S(2)}) %all-to-all-start.1) | async-done | bytes 2097184 | tf_op jit(solution)/shard_map/all_to_all | solution.py:28
  123.7 3.2 %copy.15 = bf16[2,64,32,256]{3,2,1,0:T(8,128)(2,1)} copy(bf16[2,64,32,256]{3,2,0,1:T(8,128)(2,1)} %all-to-all-done.1) | data formatting | bytes 4194304 | tf_op jit(solution)/shard_map/all_to_all | solution.py:28
  126.9 0.0 copy-done.3
  126.9 0.0 copy-done.4
  126.9 0.0 copy-start.1
  126.9 13.0 %fusion.2 = bf16[2,2048,256]{2,1,0:T(8,128)(2,1)} fusion(f32[2,2048,256]{2,1,0:T(8,128)} %fusion.3, bf16[2,2048,256]{2,1,0:T(8,128)(2,1)} %param.11, bf16[2,2048,256]{2,1,0:T(8,128)(2,1)} %bitcast.22, bf16[2,2048,2048]{2,1,0:T(8,128)(2,1)} %param.8, f32[2,256]{1,0:T(2,128)S(1)} %copy-done.4, f32[2,2048]{1,0:T(2,128)S(1)} %copy-done.3), kind=kOutput, calls=%fused_computation.3 | convolution fusion | flops 4301258752 | bytes 27281408 | tf_op jit(solution)/shard_map/cqp,cqh->cph/dot_general | solution.py:37
  139.9 0.0 copy-done.1
Async XLA Ops:
  6.5 1.6 %copy-start = (bf16[2,2048,256]{2,1,0:T(8,128)(2,1)S(1)}, bf16[2,2048,256]{2,1,0:T(8,128)(2,1)}, u32[]{:S(2)}) copy-start(bf16[2,2048,256]{2,1,0:T(8,128)(2,1)} %param.7) | copy-start | bytes 6291460
  6.5 73.9 %reduce-scatter.2.cloned.1.call-start = ((), (), s32[]{:S(2)}) async-start(), calls=%async_computation.3 | async-start | bytes 12582912 | tf_op jit(solution)/shard_map/reduce_scatter | solution.py:25
  16.6 40.6 %copy-start.2 = (bf16[2,256,512]{2,1,0:T(8,128)(2,1)S(1)}, bf16[2,256,512]{2,1,0:T(8,128)(2,1)}, u32[]{:S(2)}) copy-start(bf16[2,256,512]{2,1,0:T(8,128)(2,1)} %param.10) | copy-start | bytes 1572868
  84.4 39.3 %all-to-all-start.1 = ((bf16[2,64,32,256]{3,2,0,1:T(8,128)(2,1)}), bf16[2,64,32,256]{3,2,0,1:T(8,128)(2,1)}, u32[]{:S(2)}, u32[]{:S(2)}) async-start(bf16[2,64,32,256]{3,2,0,1:T(8,128)(2,1)} %copy.14), calls=%async_computation.2 | async-start | bytes 4194304 | tf_op jit(solution)/shard_map/all_to_all | solution.py:28
  105.0 21.8 %copy-start.3 = (f32[2,2048]{1,0:T(2,128)S(1)}, f32[2,2048]{1,0:T(2,128)}, u32[]{:S(2)}) copy-start(f32[2,2048]{1,0:T(2,128)} %param.12) | copy-start | bytes 49156
  105.0 21.9 %copy-start.4 = (f32[2,256]{1,0:T(2,128)S(1)}, f32[2,256]{1,0:T(2,128)}, u32[]{:S(2)}) copy-start(f32[2,256]{1,0:T(2,128)} %param.13) | copy-start | bytes 6148
  126.9 13.0 %copy-start.1 = (bf16[2,2048,256]{2,1,0:T(8,128)(2,1)S(1)}, bf16[2,2048,256]{2,1,0:T(8,128)(2,1)}, u32[]{:S(2)}) copy-start(bf16[2,2048,256]{2,1,0:T(8,128)(2,1)} %param.7) | copy-start | bytes 6291460
Sparse Core Ops, SparseCore 0:
  61.9 18.5 reduce-scatter.1
where the time goes:
time: 148 us; the launch traced here: 147 us
  blocking collectives  40.3 us (27%)
  waiting for transfers between devices  37.4 us (25%)
  matrix products  35.9 us (24%)
  between operations  13.4 us (9%)
  starting transfers between devices  10.6 us (7%)
  local copies, waits for them, and re-layouts  6.7 us (5%)
  other arithmetic  2.39 us (2%)
    all_to_all x1, blocking collectives, local(): lax.all_to_all(recoupled.reshape(chan_count, peer_count, seg_rows, col_co...  40.3 us
    reduce_scatter x1, waiting for transfers between devices, local(): lax.psum_scatter(pieces_sum, 'dom', scatter_dimension=2, tiled=True)  18.7 us
    all_to_all x1, waiting for transfers between devices, local(): lax.all_to_all(cycle_term.reshape(chan_count, peer_count, seg_rows, col_c...  18.7 us
    dot_general x1, matrix products, local(): jnp.einsum('cqp,cqh->cph', recouple, returned, preferred_element_type=jnp...  13 us
    all_to_all x1, starting transfers between devices, local(): lax.all_to_all(cycle_term.reshape(chan_count, peer_count, seg_rows, col_c...  10.6 us
    dot_general x1, matrix products, local(): jnp.einsum('cpq,cqh->cph', ladder_int, amplitudes, preferred_element_type...  10.1 us
    dot_general x1, matrix products, local(): jnp.einsum('cpq,cqh->cph', recouple, amplitudes, preferred_element_type=j...  8.33 us
    dot_general x1, matrix products, local(): jnp.einsum('cph,chk->cpk', ph_blocks, cycle_coupling, preferred_element_t...  4.49 us
  transfers between devices with their start and end apart: 2, of which 2 were waited for; matrix products, arithmetic and copies ran while one was open for 7% of the time, Pallas kernels for 0%

commit v1 on v0

v1 whole, which is shorter than its diff:
```python
import itertools

import jax
import jax.numpy as jnp
from jax import lax
from jax.experimental import pallas as pl
from jax.experimental.pallas import tpu as pltpu
from jax.sharding import PartitionSpec as P

RING = ((0, 0), (0, 1), (1, 1), (1, 0))
PLACE = {bits: at for at, bits in enumerate(RING)}
BF, F32 = jnp.bfloat16, jnp.float32
WIDE = 48 * 1024 * 1024


def chip(bits):
    return (PLACE[bits[0]] * 4 + PLACE[bits[1]]) * 4 + PLACE[bits[2]]


def bits_of(core, moved, kept):
    return [(m, k) if core == 0 else (k, m) for m, k in zip(moved, kept)]


THREE = list(itertools.product((0, 1), repeat=3))
GROUPS = [
    [chip(bits_of(core, moved, kept)) * 2 + core for moved in THREE]
    for core in range(2)
    for kept in THREE
]


def flips(axis):
    pairs = []
    for core, moved, kept in itertools.product(range(2), THREE, THREE):
        other = [k ^ (a == axis) for a, k in enumerate(kept)]
        pairs.append(
            (
                chip(bits_of(core, moved, kept)) * 2 + core,
                chip(bits_of(core, moved, other)) * 2 + core,
            )
        )
    return pairs


FLIPS = [flips(axis) for axis in range(3)]
BOTH = ("chan", "dom")


def swap(array):
    return lax.ppermute(array, "dom", [(0, 1), (1, 0)])


def over(array, axis):
    return lax.ppermute(array, BOTH, FLIPS[axis])


def segment(core, moved, kept):
    at = 0
    for shift in (2, 1, 0):
        m, k = (moved >> shift) & 1, (kept >> shift) & 1
        at = at * 4 + 2 * jnp.where(core == 0, m, k) + (m ^ k)
    return at


def dot(a, b):
    return jnp.dot(a, b, preferred_element_type=F32)


def params():
    return pltpu.CompilerParams(vmem_limit_bytes=WIDE)


def cost(flops, moved):
    return pl.CostEstimate(flops=flops, bytes_accessed=moved, transcendentals=0)


def row_specs(rows, width):
    return [
        pl.BlockSpec((1, rows, width), lambda m, sc, k=k: (sc[0], segment(sc[0], m, k), 0))
        for k in range(8)
    ]


def recoupled_kernel(sc, *refs):
    own, oth, out = refs[8:]
    rows = jnp.concatenate([ref[0] for ref in refs[:8]], axis=0)
    half = own.shape[2]
    out[0, :, :half] = dot(rows, own[0]).astype(BF)
    out[0, :, half:] = dot(rows, oth[...]).astype(BF)


def recoupled_call(sc, recouple, amplitudes, other):
    _, n, _ = recouple.shape
    half = amplitudes.shape[2]
    return pl.pallas_call(
        recoupled_kernel,
        grid_spec=pltpu.PrefetchScalarGridSpec(
            num_scalar_prefetch=1,
            grid=(8,),
            in_specs=row_specs(n // 64, n)
            + [
                pl.BlockSpec((1, n, half), lambda m, sc: (sc[0], 0, 0)),
                pl.BlockSpec((n, half), lambda m, sc: (0, 0)),
            ],
            out_specs=pl.BlockSpec((1, n // 8, 2 * half), lambda m, sc: (m, 0, 0)),
        ),
        out_shape=jax.ShapeDtypeStruct((8, n // 8, 2 * half), BF),
        compiler_params=params(),
        cost_estimate=cost(4 * n * n * half, 2 * n * n + 8 * n * half),
        name="recoupled",
    )(sc, *([recouple] * 8), amplitudes, other)


def turn_kernel(sc, *refs):
    rows = jnp.concatenate([ref[0] for ref in refs[:8]], axis=0)
    refs[8][...] = rows.T


def turn_call(sc, recouple):
    _, n, _ = recouple.shape
    return pl.pallas_call(
        turn_kernel,
        grid_spec=pltpu.PrefetchScalarGridSpec(
            num_scalar_prefetch=1,
            grid=(8,),
            in_specs=row_specs(n // 64, n),
            out_specs=pl.BlockSpec((n, n // 8), lambda m, sc: (0, m)),
        ),
        out_shape=jax.ShapeDtypeStruct((n, n), BF),
        compiler_params=params(),
        cost_estimate=cost(0, 4 * n * n),
        name="turned",
    )(sc, *([recouple] * 8))


def cycle_kernel(sc, x, c, out):
    rows, half = x.shape[0] * x.shape[2], c.shape[2] // 2
    lines = x[...].reshape(rows, x.shape[3])
    for side in range(2):
        at = pl.multiple_of((sc[0] ^ side) * half, half)
        got = dot(lines, c[0, :, pl.ds(at, half)]).astype(BF)
        out[:, :, :, side * half : (side + 1) * half] = got.reshape(x.shape[:3] + (half,))


def cycle_call(sc, blocks, couplings):
    _, _, rows, h = blocks.shape
    spec = pl.BlockSpec((8, 1, rows, h), lambda r, sc: (0, r ^ sc[1], 0, 0))
    return pl.pallas_call(
        cycle_kernel,
        grid_spec=pltpu.PrefetchScalarGridSpec(
            num_scalar_prefetch=1,
            grid=(8,),
            in_specs=[spec, pl.BlockSpec((1, h, h), lambda r, sc: (r, 0, 0))],
            out_specs=spec,
        ),
        out_shape=jax.ShapeDtypeStruct(blocks.shape, BF),
        compiler_params=params(),
        cost_estimate=cost(2 * 64 * rows * h * h, 256 * rows * h + 16 * h * h),
        name="cycle",
    )(sc, blocks, couplings)


def ladder_kernel(sc, l, own, oth, drive, drive_oth, out):
    half = own.shape[2]
    out[:, :half] = dot(l[0], own[0]) + drive[0].astype(F32)
    out[:, half:] = dot(l[0], oth[...]) + drive_oth[...].astype(F32)


def ladder_call(sc, ladder_int, amplitudes, other, drive, drive_other):
    _, n, _ = ladder_int.shape
    half = amplitudes.shape[2]
    tile = n // 8
    return pl.pallas_call(
        ladder_kernel,
        grid_spec=pltpu.PrefetchScalarGridSpec(
            num_scalar_prefetch=1,
            grid=(8,),
            in_specs=[
                pl.BlockSpec((1, tile, n), lambda i, sc: (sc[0], i, 0)),
                pl.BlockSpec((1, n, half), lambda i, sc: (sc[0], 0, 0)),
                pl.BlockSpec((n, half), lambda i, sc: (0, 0)),
                pl.BlockSpec((1, tile, half), lambda i, sc: (sc[0], i, 0)),
                pl.BlockSpec((tile, half), lambda i, sc: (i, 0)),
            ],
            out_specs=pl.BlockSpec((tile, 2 * half), lambda i, sc: (i, 0)),
        ),
        out_shape=jax.ShapeDtypeStruct((n, 2 * half), F32),
        compiler_params=params(),
        cost_estimate=cost(4 * n * n * half, 2 * n * n + 16 * n * half),
        name="ladder",
    )(sc, ladder_int, amplitudes, other, drive, drive_other)


def final_kernel(sc, turned, x, ladder, part, hole, out, out_oth):
    half = out.shape[2]
    for side, to in ((1, out_oth), (0, out)):
        at = slice(side * half, (side + 1) * half)
        total = dot(turned[...], x[:, at]) + ladder[:, at]
        got = (total / (part[...] - hole[:, at])).astype(BF)
        to[...] = got.reshape(to.shape)


def final_call(sc, turned, returned, ladder, part, hole):
    n, h = returned.shape
    tile, half = n // 8, h // 2
    return pl.pallas_call(
        final_kernel,
        grid_spec=pltpu.PrefetchScalarGridSpec(
            num_scalar_prefetch=1,
            grid=(8,),
            in_specs=[
                pl.BlockSpec((tile, n), lambda i, sc: (i, 0)),
                pl.BlockSpec((n, h), lambda i, sc: (0, 0)),
                pl.BlockSpec((tile, h), lambda i, sc: (i, 0)),
                pl.BlockSpec((tile, 1), lambda i, sc: (i, 0)),
                pl.BlockSpec((1, h), lambda i, sc: (0, 0)),
            ],
            out_specs=[
                pl.BlockSpec((1, tile, half), lambda i, sc: (sc[0], i, 0)),
                pl.BlockSpec((tile, half), lambda i, sc: (i, 0)),
            ],
        ),
        out_shape=[
            jax.ShapeDtypeStruct((2, n, half), BF),
            jax.ShapeDtypeStruct((n, half), BF),
        ],
        compiler_params=params(),
        cost_estimate=cost(2 * n * n * h, 2 * n * n + 8 * n * h),
        name="final",
    )(sc, turned, returned, ladder, part, hole)


def local(amplitudes, recouple, ladder_int, cycle_coupling, drive, eps_part, eps_hole):
    _, n, half = amplitudes.shape
    h, seg = 2 * half, n // 64
    core, here = lax.axis_index("dom"), lax.axis_index("chan")
    kept = 0
    for weight in (16, 4, 1):
        place = (here // weight) % 4
        high, low = place // 2, ((place + 1) // 2) % 2
        kept = 2 * kept + jnp.where(core == 0, low, high)
    sc = jnp.stack([core, kept]).astype(jnp.int32)

    def mine(array):
        return lax.dynamic_index_in_dim(array, core, 0, keepdims=False)

    def others(array):
        return swap(lax.dynamic_index_in_dim(array, 1 - core, 0, keepdims=False))

    amp_other = others(amplitudes)
    c0 = jnp.concatenate([mine(cycle_coupling), others(cycle_coupling)], axis=0)
    hole = jnp.concatenate([mine(eps_hole), others(eps_hole)])[None, :]
    part = mine(eps_part)[:, None]
    drive_other = others(drive)

    recoupled = recoupled_call(sc, recouple, amplitudes, amp_other)

    c4, c2, c1 = over(c0, 0), over(c0, 1), over(c0, 2)
    c6, c3, c5 = over(c4, 1), over(c2, 2), over(c1, 0)
    c7 = over(c6, 2)
    couplings = jnp.stack([c0, c1, c2, c3, c4, c5, c6, c7])

    def exchange(array):
        return lax.all_to_all(array, BOTH, 0, 0, axis_index_groups=GROUPS, tiled=True)

    blocks = exchange(recoupled).reshape(8, 8, seg, h)
    turned = turn_call(sc, recouple)
    ladder = ladder_call(sc, ladder_int, amplitudes, amp_other, drive, drive_other)
    cycle_term = cycle_call(sc, blocks, couplings)
    returned = exchange(cycle_term.reshape(8, 8 * seg, h)).reshape(n, h)
    out, out_other = final_call(sc, turned, returned, ladder, part, hole)
    return lax.dynamic_update_slice(out, swap(out_other)[None], (1 - core, 0, 0))


def solution(mesh):
    placed = (
        P("chan", None, "dom"),
        P("chan", None, None),
        P("chan", None, None),
        P("chan", "dom", None),
        P("chan", None, "dom"),
        P("chan", None),
        P("chan", "dom"),
    )
    return jax.shard_map(
        local, mesh=mesh, in_specs=placed, out_specs=P("chan", None, "dom"), check_vma=False
    )
```

time: 148 us -> 124 us (0.84)
  Pallas kernels: 0 us -> 50.2 us
  blocking collectives: 40.3 us -> 0 us
  matrix products: 35.9 us -> 0 us
  waiting for transfers between devices: 37.4 us -> 14.2 us
  starting transfers between devices: 10.6 us -> 31.3 us
  local copies, waits for them, and re-layouts: 6.7 us -> 23.9 us
  between operations: 13.4 us -> 0.12 us
    pallas_call x0 -> x5, Pallas kernels: none -> 50.2 us  [the longest x1 11.5 us: final_call(): pl.pallas_call(final_kernel, grid_spec=pltpu.PrefetchScalarGridSpec(num_s...]
    all_to_all x1 -> x0, blocking collectives: 40.3 us -> none  [local(): lax.all_to_all(recoupled.reshape(chan_count, peer_count, seg_rows, col_co...]
    dot_general x4 -> x0, matrix products: 35.9 us -> none  [the longest x1 13 us: local(): jnp.einsum('cqp,cqh->cph', recouple, returned, preferred_element_type=jnp...]
    ppermute x0 -> x12, starting transfers between devices: none -> 22.5 us  [the longest x7 16.9 us: over(): return lax.ppermute(array, BOTH, FLIPS[axis])]
    reduce_scatter x1 -> x0, waiting for transfers between devices: 18.7 us -> none  [local(): lax.psum_scatter(pieces_sum, 'dom', scatter_dimension=2, tiled=True)]
    all_to_all x1 -> x2, waiting for transfers between devices: 18.7 us -> 0.01 us  [exchange(): lax.all_to_all(array, BOTH, 0, 0, axis_index_groups=GROUPS, tiled=True)]
    ppermute x0 -> x12, waiting for transfers between devices: none -> 14.2 us  [the longest x7 10.4 us: over(): return lax.ppermute(array, BOTH, FLIPS[axis])]
    unnamed x10 -> x22, local copies, waits for them, and re-layouts: 1.61 us -> 14.8 us
  transfers between devices with their start and end apart: 2 -> 14, of which waited for: 2 -> 6; matrix products, arithmetic and copies ran while one was open for 7% -> 15% of each run, Pallas kernels for 0% -> 26%
where the time goes in v1:
time: 124 us; the launch traced here: 122 us
  Pallas kernels  50.2 us (40%)
  starting transfers between devices  31.3 us (25%)
  local copies, waits for them, and re-layouts  23.9 us (19%)
  waiting for transfers between devices  14.2 us (11%)
  other arithmetic  2.76 us (2%)
    ppermute x7, starting transfers between devices, over(): return lax.ppermute(array, BOTH, FLIPS[axis])  16.9 us
    unnamed x22, local copies, waits for them, and re-layouts  14.8 us
    pallas_call x1, Pallas kernels, final_call(): pl.pallas_call(final_kernel, grid_spec=pltpu.PrefetchScalarGridSpec(num_s...  11.5 us
    pallas_call x1, Pallas kernels, ladder_call(): pl.pallas_call(ladder_kernel, grid_spec=pltpu.PrefetchScalarGridSpec(num_...  11 us
    pallas_call x1, Pallas kernels, turn_call(): pl.pallas_call(turn_kernel, grid_spec=pltpu.PrefetchScalarGridSpec(num_sc...  10.9 us
    ppermute x7, waiting for transfers between devices, over(): return lax.ppermute(array, BOTH, FLIPS[axis])  10.4 us
    pallas_call x1, Pallas kernels, recoupled_call(): pl.pallas_call(recoupled_kernel, grid_spec=pltpu.PrefetchScalarGridSpec(n...  9.91 us
    all_to_all x2, starting transfers between devices, exchange(): lax.all_to_all(array, BOTH, 0, 0, axis_index_groups=GROUPS, tiled=True)  8.85 us
  transfers between devices with their start and end apart: 14, of which 6 were waited for; matrix products, arithmetic and copies ran while one was open for 15% of the time, Pallas kernels for 26%

profile of v1, /device:TPU:1, one launch (start us, length us, event | category | flops | bytes accessed | tf_op | source)
XLA Modules:
  0.0 122.5 jit_solution(13135515525845142703)
XLA Ops:
  0.0 0.0 copy-start
  0.0 0.0 copy-start.2
  0.0 2.4 %dynamic-slice_bitcast_fusion.1 = bf16[2048,256]{1,0:T(8,128)(2,1)} fusion(bf16[2,2048,256]{2,1,0:T(8,128)(2,1)} %own.1, s32[]{:T(128)S(6)} %select_n.95), kind=kLoop, calls=%fused_computation.2 | loop fusion | bytes 2097156 | tf_op jit(solution)/shard_map/jit(dynamic_index_in_dim)/squeeze | solution.py:248
  2.4 1.4 %collective-permute-start = (bf16[2048,256]{1,0:T(8,128)(2,1)}, bf16[2048,256]{1,0:T(8,128)(2,1)S(1)}, u32[]{:S(2)}, u32[]{:S(2)}) collective-permute-start(bf16[2048,256]{1,0:T(8,128)(2,1)} %dynamic-slice_bitcast_fusion.1), channel_id=1, source_target_pairs={{0,1},{1,0},{2,3},{3,2},{4,5},{5,4},{6,7},{7,6},{8,9},{9,8},{10,11... | collective-permute-start | bytes 3145736 | tf_op jit(solution)/shard_map/ppermute | solution.py:50
  3.8 1.1 dynamic-slice_bitcast_fusion.3
  4.9 0.1 collective-permute-start.1
  5.0 1.5 %collective-permute-done.1 = bf16[256,512]{1,0:T(8,128)(2,1)S(1)} collective-permute-done((bf16[256,512]{1,0:T(8,128)(2,1)S(1)}, bf16[256,512]{1,0:T(8,128)(2,1)S(1)}, u32[]{:S(2)}, u32[]{:S(2)}) %collective-permute-start.1) | collective-permute-done | bytes 262176 | tf_op jit(solution)/shard_map/ppermute | solution.py:50
  6.5 0.0 copy-start.6
  6.5 0.7 copy-done.6
  7.2 0.9 pad_maximum_fusion
  8.1 2.8 %collective-permute-start.3 = (bf16[512,512]{1,0:T(8,128)(2,1)}, bf16[512,512]{1,0:T(8,128)(2,1)}, u32[]{:S(2)}, u32[]{:S(2)}) collective-permute-start(bf16[512,512]{1,0:T(8,128)(2,1)} %pad_maximum_fusion), channel_id=1, source_target_pairs={{0,8},{2,10},{8,0},{10,2},{32,40},{34,42},{40,32},{42,34},{6,14},{... | collective-permute-start | bytes 1572872 | tf_op jit(solution)/shard_map/ppermute | solution.py:54
  10.9 3.8 %collective-permute-start.5 = (bf16[512,512]{1,0:T(8,128)(2,1)}, bf16[512,512]{1,0:T(8,128)(2,1)}, u32[]{:S(2)}, u32[]{:S(2)}) collective-permute-start(bf16[512,512]{1,0:T(8,128)(2,1)} %pad_maximum_fusion), channel_id=1, source_target_pairs={{0,32},{2,34},{8,40},{10,42},{32,0},{34,2},{40,8},{42,10},{6,38},{... | collective-permute-start | bytes 1572872 | tf_op jit(solution)/shard_map/ppermute | solution.py:54
  14.7 0.1 pad_add_fusion.sc
  14.8 2.5 %collective-permute-start.2 = (bf16[512,512]{1,0:T(8,128)(2,1)}, bf16[512,512]{1,0:T(8,128)(2,1)}, u32[]{:S(2)}, u32[]{:S(2)}) collective-permute-start(bf16[512,512]{1,0:T(8,128)(2,1)} %pad_maximum_fusion), channel_id=1, source_target_pairs={{0,2},{2,0},{8,10},{10,8},{32,34},{34,32},{40,42},{42,40},{6,4},{4... | collective-permute-start | bytes 1572872 | tf_op jit(solution)/shard_map/ppermute | solution.py:54
  17.3 0.6 collective-permute-done.3
  17.8 2.5 %collective-permute-start.4 = (bf16[512,512]{1,0:T(8,128)(2,1)}, bf16[512,512]{1,0:T(8,128)(2,1)}, u32[]{:S(2)}, u32[]{:S(2)}) collective-permute-start(bf16[512,512]{1,0:T(8,128)(2,1)} %collective-permute-done.3), channel_id=1, source_target_pairs={{0,2},{2,0},{8,10},{10,8},{32,34},{34,32},{40,42},{42,40},{6,4},{4... | collective-permute-start | bytes 1572872 | tf_op jit(solution)/shard_map/ppermute | solution.py:54
  20.3 1.3 %collective-permute-done.5 = bf16[512,512]{1,0:T(8,128)(2,1)} collective-permute-done((bf16[512,512]{1,0:T(8,128)(2,1)}, bf16[512,512]{1,0:T(8,128)(2,1)}, u32[]{:S(2)}, u32[]{:S(2)}) %collective-permute-start.5) | collective-permute-done | bytes 524320 | tf_op jit(solution)/shard_map/ppermute | solution.py:54
  21.6 1.4 %collective-permute-start.7 = (bf16[512,512]{1,0:T(8,128)(2,1)}, bf16[512,512]{1,0:T(8,128)(2,1)}, u32[]{:S(2)}, u32[]{:S(2)}) collective-permute-start(bf16[512,512]{1,0:T(8,128)(2,1)} %collective-permute-done.5), channel_id=1, source_target_pairs={{0,8},{2,10},{8,0},{10,2},{32,40},{34,42},{40,32},{42,34},{6,14},{... | collective-permute-start | bytes 1572872 | tf_op jit(solution)/shard_map/ppermute | solution.py:54
  23.0 0.0 collective-permute-done.refs_9_.oth
  23.0 0.0 copy-done.2
  23.0 9.9 %recoupled.1 = bf16[8,256,512]{2,1,0:T(8,128)(2,1)S(1)} custom-call(s32[2]{0:T(128)S(1)} %pad_add_fusion.sc, bf16[2,2048,2048]{2,1,0:T(8,128)(2,1)} %refs_7_.3, bf16[2,2048,2048]{2,1,0:T(8,128)(2,1)} %refs_7_.3, bf16[2,2048,2048]{2,1,0:T(8,128)(2,1)} %refs_7_.3, bf16[2,2048,2048]{2,1,0:T(8,128)(2,1)} %refs_7_.3, bf16[2,2048,2048]{2,1,0:T(8,128)(2,1)} %refs_7_.3, ...), custom_call_target="tpu_custom_call" | custom-call | flops 4294967296 | bytes 12582912 | tf_op jit(solution)/shard_map/recoupled/pallas_call | solution.py:95
  32.9 0.0 copy-start.3
  32.9 1.3 %copy-done.3 = bf16[8,256,512]{2,1,0:T(8,128)(2,1)} copy-done((bf16[8,256,512]{2,1,0:T(8,128)(2,1)}, bf16[8,256,512]{2,1,0:T(8,128)(2,1)S(1)}, u32[]{:S(2)}) %copy-start.3) | copy-done | bytes 2097176
  34.2 4.4 %all-to-all-start = ((bf16[8,256,512]{2,1,0:T(8,128)(2,1)}), bf16[8,256,512]{2,1,0:T(8,128)(2,1)}, u32[]{:S(2)}, u32[]{:S(2)}) async-start(bf16[8,256,512]{2,1,0:T(8,128)(2,1)} %copy-done.3), calls=%async_computation | async-start | bytes 4194304 | tf_op jit(solution)/shard_map/all_to_all | solution.py:264
  38.6 1.8 %bitcast_dynamic-update-slice_fusion.8 = bf16[8,512,512]{2,1,0:T(8,128)(2,1)} fusion(bf16[256,512]{1,0:T(8,128)(2,1)} %copy-done.6, bf16[256,512]{1,0:T(8,128)(2,1)S(1)} %get-tuple-element.9), kind=kLoop, calls=%fused_computation.11 | loop fusion | flops 1048575 | bytes 1048576
  40.4 0.0 collective-permute-done.2
  40.4 3.8 %collective-permute-start.6 = (bf16[512,512]{1,0:T(8,128)(2,1)}, bf16[512,512]{1,0:T(8,128)(2,1)S(1)}, u32[]{:S(2)}, u32[]{:S(2)}) collective-permute-start(bf16[512,512]{1,0:T(8,128)(2,1)} %collective-permute-done.2), channel_id=1, source_target_pairs={{0,32},{2,34},{8,40},{10,42},{32,0},{34,2},{40,8},{42,10},{6,38},{... | collective-permute-start | bytes 1572872 | tf_op jit(solution)/shard_map/ppermute | solution.py:54
  44.1 1.9 %bitcast_dynamic-update-slice_fusion.7 = bf16[8,512,512]{2,1,0:T(8,128)(2,1)} fusion(bf16[8,512,512]{2,1,0:T(8,128)(2,1)} %bitcast_dynamic-update-slice_fusion.8, bf16[512,512]{1,0:T(8,128)(2,1)} %collective-permute-done.2), kind=kLoop, calls=%fused_computation.10 | loop fusion | bytes 1048576
  46.1 1.9 %bitcast_dynamic-update-slice_fusion.6 = bf16[8,512,512]{2,1,0:T(8,128)(2,1)} fusion(bf16[8,512,512]{2,1,0:T(8,128)(2,1)} %bitcast_dynamic-update-slice_fusion.7, bf16[512,512]{1,0:T(8,128)(2,1)} %collective-permute-done.3), kind=kLoop, calls=%fused_computation.9 | loop fusion | bytes 1048576
  47.9 0.0 collective-permute-done.7
  48.0 0.2 collective-permute-start.8
  48.2 0.0 collective-permute-done.4
  48.2 1.9 %bitcast_dynamic-update-slice_fusion.5 = bf16[8,512,512]{2,1,0:T(8,128)(2,1)} fusion(bf16[8,512,512]{2,1,0:T(8,128)(2,1)} %bitcast_dynamic-update-slice_fusion.6, bf16[512,512]{1,0:T(8,128)(2,1)} %collective-permute-done.4), kind=kLoop, calls=%fused_computation.8 | loop fusion | bytes 1048576
  50.0 1.9 %bitcast_dynamic-update-slice_fusion.4 = bf16[8,512,512]{2,1,0:T(8,128)(2,1)} fusion(bf16[8,512,512]{2,1,0:T(8,128)(2,1)} %bitcast_dynamic-update-slice_fusion.5, bf16[512,512]{1,0:T(8,128)(2,1)} %collective-permute-done.5), kind=kLoop, calls=%fused_computation.7 | loop fusion | bytes 1048576
  51.9 7.8 %collective-permute-done.6 = bf16[512,512]{1,0:T(8,128)(2,1)S(1)} collective-permute-done((bf16[512,512]{1,0:T(8,128)(2,1)}, bf16[512,512]{1,0:T(8,128)(2,1)S(1)}, u32[]{:S(2)}, u32[]{:S(2)}) %collective-permute-start.6) | collective-permute-done | bytes 524320 | tf_op jit(solution)/shard_map/ppermute | solution.py:54
  59.7 0.8 bitcast_dynamic-update-slice_fusion.3
  60.6 1.9 %bitcast_dynamic-update-slice_fusion.2 = bf16[8,512,512]{2,1,0:T(8,128)(2,1)} fusion(bf16[8,512,512]{2,1,0:T(8,128)(2,1)} %bitcast_dynamic-update-slice_fusion.3, bf16[512,512]{1,0:T(8,128)(2,1)} %collective-permute-done.7), kind=kLoop, calls=%fused_computation.5 | loop fusion | bytes 1048576
  62.5 0.7 collective-permute-done.8
  63.1 0.8 bitcast_dynamic-update-slice_fusion.1.c
  63.9 0.0 all-to-all-done
  63.9 6.9 %cycle.1 = bf16[8,8,32,512]{3,2,1,0:T(8,128)(2,1)S(1)} custom-call(s32[2]{0:T(128)S(1)} %pad_add_fusion.sc, bf16[8,8,32,512]{3,2,1,0:T(8,128)(2,1)} %bitcast.3.x, bf16[8,512,512]{2,1,0:T(8,128)(2,1)} %bitcast_dynamic-update-slice_fusion.1.c), custom_call_target="tpu_custom_call" | custom-call | flops 1073741824 | bytes 8388608 | tf_op jit(solution)/shard_map/cycle/pallas_call | solution.py:148
  70.8 0.0 copy-start.4
  70.8 1.3 %copy-done.4 = bf16[8,8,32,512]{3,2,1,0:T(8,128)(2,1)} copy-done((bf16[8,8,32,512]{3,2,1,0:T(8,128)(2,1)}, bf16[8,8,32,512]{3,2,1,0:T(8,128)(2,1)S(1)}, u32[]{:S(2)}) %copy-start.4) | copy-done | bytes 2097176
  72.2 0.0 copy-start.7
  72.2 4.5 %all-to-all-start.1 = ((bf16[8,256,512]{2,1,0:T(8,128)(2,1)}), bf16[8,256,512]{2,1,0:T(8,128)(2,1)}, u32[]{:S(2)}, u32[]{:S(2)}) async-start(bf16[8,256,512]{2,1,0:T(8,128)(2,1)} %bitcast.36), calls=%async_computation.1 | async-start | bytes 4194304 | tf_op jit(solution)/shard_map/all_to_all | solution.py:264
  76.7 2.4 %dynamic-slice_bitcast_fusion = bf16[2048,256]{1,0:T(8,128)(2,1)} fusion(bf16[2,2048,256]{2,1,0:T(8,128)(2,1)} %drive.1, s32[]{:T(128)S(6)} %select_n.95), kind=kLoop, calls=%fused_computation.1 | loop fusion | bytes 2097156 | tf_op jit(solution)/shard_map/jit(dynamic_index_in_dim)/squeeze | solution.py:248
  79.0 3.5 %collective-permute-start.9 = (bf16[2048,256]{1,0:T(8,128)(2,1)}, bf16[2048,256]{1,0:T(8,128)(2,1)}, u32[]{:S(2)}, u32[]{:S(2)}) collective-permute-start(bf16[2048,256]{1,0:T(8,128)(2,1)} %dynamic-slice_bitcast_fusion), channel_id=1, source_target_pairs={{0,1},{1,0},{2,3},{3,2},{4,5},{5,4},{6,7},{7,6},{8,9},{9,8},{10,11... | collective-permute-start | bytes 3145736 | tf_op jit(solution)/shard_map/ppermute | solution.py:50
  82.5 0.0 copy-done.7
  82.6 0.1 collective-permute-start.10
  82.6 0.0 copy-done
  82.7 10.9 %turned.1 = bf16[2048,2048]{1,0:T(8,128)(2,1)} custom-call(s32[2]{0:T(128)S(1)} %pad_add_fusion.sc, bf16[2,2048,2048]{2,1,0:T(8,128)(2,1)} %refs_7_.3, bf16[2,2048,2048]{2,1,0:T(8,128)(2,1)} %refs_7_.3, bf16[2,2048,2048]{2,1,0:T(8,128)(2,1)} %refs_7_.3, bf16[2,2048,2048]{2,1,0:T(8,128)(2,1)} %refs_7_.3, bf16[2,2048,2048]{2,1,0:T(8,128)(2,1)} %refs_7_.3, ...), custom_call_target="tpu_custom_call" | custom-call | bytes 16777216 | tf_op jit(solution)/shard_map/turned/pallas_call | solution.py:121
  93.6 1.3 %copy.8.part = f32[2048,1]{1,0:T(8,128)} copy(f32[2048,1]{0,1:T(1,128)S(1)} %dynamic-slice_bitcast_fusion.4) | data formatting | bytes 16384 | tf_op jit(solution)/shard_map/broadcast_in_dim | solution.py:253
  94.9 0.0 collective-permute-done.10
  95.0 0.0 collective-permute-done.9.drive_oth
  95.0 11.0 %ladder.1 = f32[2048,512]{1,0:T(8,128)} custom-call(s32[2]{0:T(128)S(1)} %pad_add_fusion.sc, bf16[2,2048,2048]{2,1,0:T(8,128)(2,1)} %l.1, bf16[2,2048,256]{2,1,0:T(8,128)(2,1)S(1)} %copy-done.2, bf16[2048,256]{1,0:T(8,128)(2,1)S(1)} %collective-permute-done.refs_9_.oth, bf16[2,2048,256]{2,1,0:T(8,128)(2,1)} %drive.1, ...), custom_call_target="tpu_custom_call" | custom-call | flops 4294967296 | bytes 16777216 | tf_op jit(solution)/shard_map/ladder/pallas_call | solution.py:173
  105.9 0.0 all-to-all-done.1
  105.9 0.0 copy-start.5
  105.9 1.2 copy-done.5
  107.2 0.0 copy-start.1
  107.2 11.5 %final.1 = (bf16[2,2048,256]{2,1,0:T(8,128)(2,1)}, bf16[2048,256]{1,0:T(8,128)(2,1)S(1)}) custom-call(s32[2]{0:T(128)S(1)} %pad_add_fusion.sc, bf16[2048,2048]{1,0:T(8,128)(2,1)} %turned.1, bf16[2048,512]{1,0:T(8,128)(2,1)} %bitcast.15.x, f32[2048,512]{1,0:T(8,128)} %ladder.1, f32[2048,1]{1,0:T(8,128)S(1)} %copy-done.5, f32[1,512]{1,0:T(1,128)S(1)} %bitcast.37), custom_call_target="tpu_custom_call" | custom-call | flops 4294967296 | bytes 16777216 | tf_op jit(solution)/shard_map/final/pallas_call | solution.py:206
  118.7 0.5 collective-permute-start.11
  119.1 2.3 %collective-permute-done.11 = bf16[2048,256]{1,0:T(8,128)(2,1)S(1)} collective-permute-done((bf16[2048,256]{1,0:T(8,128)(2,1)S(1)}, bf16[2048,256]{1,0:T(8,128)(2,1)S(1)}, u32[]{:S(2)}, u32[]{:S(2)}) %collective-permute-start.11) | collective-permute-done | bytes 1048608 | tf_op jit(solution)/shard_map/ppermute | solution.py:50
  121.4 1.0 bitcast_dynamic-update-slice_fusion
  122.5 0.0 copy-done.1
  (3 shorter events, 0.0 us)
Async XLA Ops:
  0.0 82.7 %copy-start = (f32[2,2048]{1,0:T(2,128)S(1)}, f32[2,2048]{1,0:T(2,128)}, u32[]{:S(2)}) copy-start(f32[2,2048]{1,0:T(2,128)} %param.12) | copy-start | bytes 49156
  0.0 23.0 %copy-start.2 = (bf16[2,2048,256]{2,1,0:T(8,128)(2,1)S(1)}, bf16[2,2048,256]{2,1,0:T(8,128)(2,1)}, u32[]{:S(2)}) copy-start(bf16[2,2048,256]{2,1,0:T(8,128)(2,1)} %own.1) | copy-start | bytes 6291460
  2.4 20.6 %collective-permute-start = (bf16[2048,256]{1,0:T(8,128)(2,1)}, bf16[2048,256]{1,0:T(8,128)(2,1)S(1)}, u32[]{:S(2)}, u32[]{:S(2)}) collective-permute-start(bf16[2048,256]{1,0:T(8,128)(2,1)} %dynamic-slice_bitcast_fusion.1), channel_id=1, source_target_pairs={{0,1},{1,0},{2,3},{3,2},{4,5},{5,4},{6,7},{7,6},{8,9},{9,8},{10,11... | collective-permute-start | bytes 3145736 | tf_op jit(solution)/shard_map/ppermute | solution.py:50
  4.9 1.6 %collective-permute-start.1 = (bf16[256,512]{1,0:T(8,128)(2,1)S(1)}, bf16[256,512]{1,0:T(8,128)(2,1)S(1)}, u32[]{:S(2)}, u32[]{:S(2)}) collective-permute-start(bf16[256,512]{1,0:T(8,128)(2,1)S(1)} %get-tuple-element.10), channel_id=1, source_target_pairs={{0,1},{1,0},{2,3},{3,2},{4,5},{5,4},{6,7},{7,6},{8,9},{9,8},{10,11... | collective-permute-start | bytes 786440 | tf_op jit(solution)/shard_map/ppermute | solution.py:50
  6.5 0.7 copy-start.6
  8.1 9.7 %collective-permute-start.3 = (bf16[512,512]{1,0:T(8,128)(2,1)}, bf16[512,512]{1,0:T(8,128)(2,1)}, u32[]{:S(2)}, u32[]{:S(2)}) collective-permute-start(bf16[512,512]{1,0:T(8,128)(2,1)} %pad_maximum_fusion), channel_id=1, source_target_pairs={{0,8},{2,10},{8,0},{10,2},{32,40},{34,42},{40,32},{42,34},{6,14},{... | collective-permute-start | bytes 1572872 | tf_op jit(solution)/shard_map/ppermute | solution.py:54
  10.9 10.7 %collective-permute-start.5 = (bf16[512,512]{1,0:T(8,128)(2,1)}, bf16[512,512]{1,0:T(8,128)(2,1)}, u32[]{:S(2)}, u32[]{:S(2)}) collective-permute-start(bf16[512,512]{1,0:T(8,128)(2,1)} %pad_maximum_fusion), channel_id=1, source_target_pairs={{0,32},{2,34},{8,40},{10,42},{32,0},{34,2},{40,8},{42,10},{6,38},{... | collective-permute-start | bytes 1572872 | tf_op jit(solution)/shard_map/ppermute | solution.py:54
  14.8 25.6 %collective-permute-start.2 = (bf16[512,512]{1,0:T(8,128)(2,1)}, bf16[512,512]{1,0:T(8,128)(2,1)}, u32[]{:S(2)}, u32[]{:S(2)}) collective-permute-start(bf16[512,512]{1,0:T(8,128)(2,1)} %pad_maximum_fusion), channel_id=1, source_target_pairs={{0,2},{2,0},{8,10},{10,8},{32,34},{34,32},{40,42},{42,40},{6,4},{4... | collective-permute-start | bytes 1572872 | tf_op jit(solution)/shard_map/ppermute | solution.py:54
  17.8 30.3 %collective-permute-start.4 = (bf16[512,512]{1,0:T(8,128)(2,1)}, bf16[512,512]{1,0:T(8,128)(2,1)}, u32[]{:S(2)}, u32[]{:S(2)}) collective-permute-start(bf16[512,512]{1,0:T(8,128)(2,1)} %collective-permute-done.3), channel_id=1, source_target_pairs={{0,2},{2,0},{8,10},{10,8},{32,34},{34,32},{40,42},{42,40},{6,4},{4... | collective-permute-start | bytes 1572872 | tf_op jit(solution)/shard_map/ppermute | solution.py:54
  21.6 26.3 %collective-permute-start.7 = (bf16[512,512]{1,0:T(8,128)(2,1)}, bf16[512,512]{1,0:T(8,128)(2,1)}, u32[]{:S(2)}, u32[]{:S(2)}) collective-permute-start(bf16[512,512]{1,0:T(8,128)(2,1)} %collective-permute-done.5), channel_id=1, source_target_pairs={{0,8},{2,10},{8,0},{10,2},{32,40},{34,42},{40,32},{42,34},{6,14},{... | collective-permute-start | bytes 1572872 | tf_op jit(solution)/shard_map/ppermute | solution.py:54
  32.9 1.3 %copy-start.3 = (bf16[8,256,512]{2,1,0:T(8,128)(2,1)}, bf16[8,256,512]{2,1,0:T(8,128)(2,1)S(1)}, u32[]{:S(2)}) copy-start(bf16[8,256,512]{2,1,0:T(8,128)(2,1)S(1)} %recoupled.1) | copy-start | bytes 6291460
  34.2 29.7 %all-to-all-start = ((bf16[8,256,512]{2,1,0:T(8,128)(2,1)}), bf16[8,256,512]{2,1,0:T(8,128)(2,1)}, u32[]{:S(2)}, u32[]{:S(2)}) async-start(bf16[8,256,512]{2,1,0:T(8,128)(2,1)} %copy-done.3), calls=%async_computation | async-start | bytes 4194304 | tf_op jit(solution)/shard_map/all_to_all | solution.py:264
  40.4 19.4 %collective-permute-start.6 = (bf16[512,512]{1,0:T(8,128)(2,1)}, bf16[512,512]{1,0:T(8,128)(2,1)S(1)}, u32[]{:S(2)}, u32[]{:S(2)}) collective-permute-start(bf16[512,512]{1,0:T(8,128)(2,1)} %collective-permute-done.2), channel_id=1, source_target_pairs={{0,32},{2,34},{8,40},{10,42},{32,0},{34,2},{40,8},{42,10},{6,38},{... | collective-permute-start | bytes 1572872 | tf_op jit(solution)/shard_map/ppermute | solution.py:54
  48.0 15.2 %collective-permute-start.8 = (bf16[512,512]{1,0:T(8,128)(2,1)}, bf16[512,512]{1,0:T(8,128)(2,1)S(1)}, u32[]{:S(2)}, u32[]{:S(2)}) collective-permute-start(bf16[512,512]{1,0:T(8,128)(2,1)} %collective-permute-done.7), channel_id=1, source_target_pairs={{0,2},{2,0},{8,10},{10,8},{32,34},{34,32},{40,42},{42,40},{6,4},{4... | collective-permute-start | bytes 1572872 | tf_op jit(solution)/shard_map/ppermute | solution.py:54
  70.8 1.3 %copy-start.4 = (bf16[8,8,32,512]{3,2,1,0:T(8,128)(2,1)}, bf16[8,8,32,512]{3,2,1,0:T(8,128)(2,1)S(1)}, u32[]{:S(2)}) copy-start(bf16[8,8,32,512]{3,2,1,0:T(8,128)(2,1)S(1)} %cycle.1) | copy-start | bytes 6291460
  72.2 10.4 %copy-start.7 = (f32[2,256]{1,0:T(2,128)S(1)}, f32[2,256]{1,0:T(2,128)}, u32[]{:S(2)}) copy-start(f32[2,256]{1,0:T(2,128)} %param.13) | copy-start | bytes 6148
  72.2 33.8 %all-to-all-start.1 = ((bf16[8,256,512]{2,1,0:T(8,128)(2,1)}), bf16[8,256,512]{2,1,0:T(8,128)(2,1)}, u32[]{:S(2)}, u32[]{:S(2)}) async-start(bf16[8,256,512]{2,1,0:T(8,128)(2,1)} %bitcast.36), calls=%async_computation.1 | async-start | bytes 4194304 | tf_op jit(solution)/shard_map/all_to_all | solution.py:264
  79.0 15.9 %collective-permute-start.9 = (bf16[2048,256]{1,0:T(8,128)(2,1)}, bf16[2048,256]{1,0:T(8,128)(2,1)}, u32[]{:S(2)}, u32[]{:S(2)}) collective-permute-start(bf16[2048,256]{1,0:T(8,128)(2,1)} %dynamic-slice_bitcast_fusion), channel_id=1, source_target_pairs={{0,1},{1,0},{2,3},{3,2},{4,5},{5,4},{6,7},{7,6},{8,9},{9,8},{10,11... | collective-permute-start | bytes 3145736 | tf_op jit(solution)/shard_map/ppermute | solution.py:50
  82.6 12.4 %collective-permute-start.10 = (f32[256]{0:T(256)S(1)}, f32[256]{0:T(256)S(1)}, u32[]{:S(2)}, u32[]{:S(2)}) collective-permute-start(f32[256]{0:T(256)S(1)} %bitcast.39), channel_id=1, source_target_pairs={{0,1},{1,0},{2,3},{3,2},{4,5},{5,4},{6,7},{7,6},{8,9},{9,8},{10,11... | collective-permute-start | bytes 3080 | tf_op jit(solution)/shard_map/ppermute | solution.py:50
  105.9 1.2 %copy-start.5 = (f32[2048,1]{1,0:T(8,128)S(1)}, f32[2048,1]{1,0:T(8,128)}, u32[]{:S(2)}) copy-start(f32[2048,1]{1,0:T(8,128)} %copy.8.part) | copy-start | bytes 24580
  107.2 15.3 %copy-start.1 = (f32[2,2048]{1,0:T(2,128)S(1)}, f32[2,2048]{1,0:T(2,128)}, u32[]{:S(2)}) copy-start(f32[2,2048]{1,0:T(2,128)} %param.12) | copy-start | bytes 49156
  118.7 2.8 %collective-permute-start.11 = (bf16[2048,256]{1,0:T(8,128)(2,1)S(1)}, bf16[2048,256]{1,0:T(8,128)(2,1)S(1)}, u32[]{:S(2)}, u32[]{:S(2)}) collective-permute-start(bf16[2048,256]{1,0:T(8,128)(2,1)S(1)} %get-tuple-element.8), channel_id=1, source_target_pairs={{0,1},{1,0},{2,3},{3,2},{4,5},{5,4},{6,7},{7,6},{8,9},{9,8},{10,11... | collective-permute-start | bytes 3145736 | tf_op jit(solution)/shard_map/ppermute | solution.py:50

commit v2 on v1

v2 whole, which is shorter than its diff:
```python
import itertools

import jax
import jax.numpy as jnp
from jax import lax
from jax.experimental import pallas as pl
from jax.experimental.pallas import tpu as pltpu
from jax.sharding import PartitionSpec as P

RING = ((0, 0), (0, 1), (1, 1), (1, 0))
PLACE = {bits: at for at, bits in enumerate(RING)}
BF, F32 = jnp.bfloat16, jnp.float32
VMEM = pltpu.VMEM


def chip(bits):
    return (PLACE[bits[0]] * 4 + PLACE[bits[1]]) * 4 + PLACE[bits[2]]


def bits_of(core, moved, kept):
    return [(m, k) if core == 0 else (k, m) for m, k in zip(moved, kept)]


THREE = list(itertools.product((0, 1), repeat=3))
GROUPS = [
    [chip(bits_of(core, moved, kept)) * 2 + core for moved in THREE]
    for core in range(2)
    for kept in THREE
]


def flips(axis):
    pairs = []
    for core, moved, kept in itertools.product(range(2), THREE, THREE):
        other = [k ^ (a == axis) for a, k in enumerate(kept)]
        pairs.append(
            (
                chip(bits_of(core, moved, kept)) * 2 + core,
                chip(bits_of(core, moved, other)) * 2 + core,
            )
        )
    return pairs


FLIPS = [flips(axis) for axis in range(3)]
BOTH = ("chan", "dom")


def swap(array):
    return lax.ppermute(array, "dom", [(0, 1), (1, 0)])


def over(array, axis):
    return lax.ppermute(array, BOTH, FLIPS[axis])


def slot(core, chip_at):
    places = [(chip_at >> shift) & 3 for shift in (4, 2, 0)]
    at = []
    for c in range(2):
        moved = [RING[p][c] for p in places]
        kept = [RING[p][1 - c] for p in places]
        at.append(sum(b << (5 - i) for i, b in enumerate(moved + kept)))
    return at[0] + core * (at[1] - at[0])


def dot(a, b):
    return jnp.dot(a, b, preferred_element_type=F32)


def params(mib):
    return pltpu.CompilerParams(vmem_limit_bytes=mib * 1024 * 1024)


def cost(flops, moved):
    return pl.CostEstimate(flops=flops, bytes_accessed=moved, transcendentals=0)


def held(array):
    return pltpu.with_memory_space_constraint(array, VMEM)


def far(array):
    return pltpu.with_memory_space_constraint(array, pltpu.HBM)


WHOLE = pl.BlockSpec(memory_space=VMEM)
AWAY = pl.BlockSpec(memory_space=pltpu.HBM)
TILES = 4


def scatter(core, got, tile, send, columns):
    seg = send.shape[1]
    each = got.shape[0] // seg
    for j in range(each):
        send[slot(core, tile * each + j), :, columns] = got[j * seg : (j + 1) * seg]


def own_kernel(sc, recouple, amplitudes, rows, send, amp, sems):
    core, n, half = sc[0], rows.shape[0], amp.shape[1]
    tile = n // TILES
    copies = [pltpu.make_async_copy(amplitudes.at[core], amp, sems.at[TILES])]
    for i in range(TILES):
        at = pl.ds(i * tile, tile)
        copies.append(pltpu.make_async_copy(recouple.at[core, at], rows.at[at], sems.at[i]))
    for copy in copies:
        copy.start()
    copies[0].wait()
    for i in range(TILES):
        copies[1 + i].wait()
        got = dot(rows[i * tile : (i + 1) * tile], amp[...]).astype(BF)
        scatter(core, got, i, send, slice(0, half))


def own_call(sc, recouple, amplitudes):
    _, n, half = amplitudes.shape
    return pl.pallas_call(
        own_kernel,
        grid_spec=pltpu.PrefetchScalarGridSpec(
            num_scalar_prefetch=1,
            grid=(1,),
            in_specs=[AWAY, AWAY],
            out_specs=[WHOLE, WHOLE],
            scratch_shapes=[VMEM((n, half), BF), pltpu.SemaphoreType.DMA((TILES + 1,))],
        ),
        out_shape=[VMEM((n, n), BF), VMEM((64, n // 64, 2 * half), BF)],
        compiler_params=params(16),
        cost_estimate=cost(2 * n * n * half, 2 * n * n),
        name="recoupled_own",
    )(sc, far(recouple), far(amplitudes))


def other_kernel(sc, rows, amp, given, send):
    tile, half = rows.shape[0] // TILES, amp.shape[2]
    for i in range(TILES):
        got = dot(rows[i * tile : (i + 1) * tile], amp[0]).astype(BF)
        scatter(sc[0], got, i, send, slice(half, 2 * half))


def other_call(sc, rows, amp_other, send):
    _, n, half = amp_other.shape
    return pl.pallas_call(
        other_kernel,
        grid_spec=pltpu.PrefetchScalarGridSpec(
            num_scalar_prefetch=1,
            grid=(1,),
            in_specs=[WHOLE, pl.BlockSpec((1, n, half), lambda i, sc: (sc[0], 0, 0)), WHOLE],
            out_specs=WHOLE,
        ),
        out_shape=VMEM(send.shape, BF),
        input_output_aliases={3: 0},
        compiler_params=params(16),
        cost_estimate=cost(2 * n * n * half, 4 * n * half),
        name="recoupled_other",
    )(sc, held(rows), amp_other, held(send))


def coupling_kernel(sc, own, oth, out):
    half, h = own.shape[1:]
    for core in range(2):

        @pl.when(sc[0] == core)
        def _():
            for part, ref in enumerate((own, oth)):
                for side in range(2):
                    at = (core ^ side) * half
                    out[part * half : (part + 1) * half, side * half : (side + 1) * half] = ref[
                        0, :, at : at + half
                    ]


def coupling_call(sc, own, oth):
    _, half, h = own.shape
    spec = pl.BlockSpec((1, half, h), lambda i, sc: (sc[0], 0, 0))
    return pl.pallas_call(
        coupling_kernel,
        grid_spec=pltpu.PrefetchScalarGridSpec(
            num_scalar_prefetch=1, grid=(1,), in_specs=[spec, spec], out_specs=WHOLE
        ),
        out_shape=VMEM((h, h), BF),
        compiler_params=params(8),
        cost_estimate=cost(0, 4 * h * h),
        name="coupling",
    )(sc, own, oth)


def cycle_kernel(sc, x, *refs):
    out = refs[8]
    lines = (x.shape[0] * x.shape[2], x.shape[3])
    for r in range(8):
        at = r ^ sc[1]
        got = dot(x[:, at].reshape(lines), refs[r][...]).astype(BF)
        out[:, at] = got.reshape(x.shape[0], x.shape[2], x.shape[3])


def cycle_call(sc, blocks, couplings):
    _, _, rows, h = blocks.shape
    return pl.pallas_call(
        cycle_kernel,
        grid_spec=pltpu.PrefetchScalarGridSpec(
            num_scalar_prefetch=1, grid=(1,), in_specs=[WHOLE] * 9, out_specs=WHOLE
        ),
        out_shape=VMEM(blocks.shape, BF),
        compiler_params=params(8),
        cost_estimate=cost(2 * 64 * rows * h * h, 256 * rows * h + 16 * h * h),
        name="cycle",
    )(sc, held(blocks), *[held(c) for c in couplings])


def ladder_kernel(sc, l, own, oth, drive, drive_oth, part, out, out_part):
    half, tile = own.shape[2], l.shape[1]
    at = pl.ds(pl.multiple_of(pl.program_id(0) * tile, tile), tile)
    out[at, :half] = dot(l[0], own[0]) + drive[0].astype(F32)
    out[at, half:] = dot(l[0], oth[0]) + drive_oth[0].astype(F32)
    out_part[at, :] = jnp.broadcast_to(part[pl.ds(sc[0], 1), :], (128, tile)).T


def ladder_call(sc, ladder_int, amplitudes, amp_other, drive, drive_other, eps_part):
    _, n, half = amplitudes.shape
    tile = n // TILES
    whole = pl.BlockSpec((1, n, half), lambda i, sc: (sc[0], 0, 0))
    piece = pl.BlockSpec((1, tile, half), lambda i, sc: (sc[0], i, 0))
    return pl.pallas_call(
        ladder_kernel,
        grid_spec=pltpu.PrefetchScalarGridSpec(
            num_scalar_prefetch=1,
            grid=(TILES,),
            in_specs=[
                pl.BlockSpec((1, tile, n), lambda i, sc: (sc[0], i, 0)),
                whole,
                whole,
                piece,
                piece,
                pl.BlockSpec((2, tile), lambda i, sc: (0, i)),
            ],
            out_specs=[WHOLE, WHOLE],
        ),
        out_shape=[VMEM((n, 2 * half), F32), VMEM((n, 128), F32)],
        compiler_params=params(20),
        cost_estimate=cost(4 * n * n * half, 2 * n * n + 16 * n * half),
        name="ladder",
    )(sc, far(ladder_int), amplitudes, amp_other, drive, drive_other, eps_part)


def final_kernel(sc, rows, x, ladder, part, hole, hole_oth, out, out_oth, lines):
    core, i = sc[0], pl.program_id(0)
    half, tile, seg = out.shape[2], out.shape[1], x.shape[1]

    @pl.when(i == 0)
    def _():
        for at in range(64):
            lines[at * seg : (at + 1) * seg, :] = x[slot(core, at)]

    at = pl.ds(pl.multiple_of(i * tile, tile), tile)
    low = part[at, :1]
    for side, to, eps in ((1, out_oth, hole_oth), (0, out, hole)):
        cols = slice(side * half, (side + 1) * half)
        total = lax.dot_general(
            rows[:, at], lines[:, cols], (((0,), (0,)), ((), ())), preferred_element_type=F32
        )
        total = total + ladder[at, cols]
        got = (total / (low - eps[pl.ds(core, 1), :])).astype(BF)
        to[...] = got.reshape(to.shape)


def final_call(sc, rows, returned, ladder, part, hole, hole_other):
    n, h = ladder.shape
    tile, half = n // TILES, h // 2
    return pl.pallas_call(
        final_kernel,
        grid_spec=pltpu.PrefetchScalarGridSpec(
            num_scalar_prefetch=1,
            grid=(TILES,),
            in_specs=[WHOLE] * 6,
            out_specs=[
                pl.BlockSpec((1, tile, half), lambda i, sc: (sc[0], i, 0)),
                pl.BlockSpec((tile, half), lambda i, sc: (i, 0)),
            ],
            scratch_shapes=[VMEM((n, h), BF)],
        ),
        out_shape=[
            jax.ShapeDtypeStruct((2, n, half), BF),
            jax.ShapeDtypeStruct((n, half), BF),
        ],
        compiler_params=params(16),
        cost_estimate=cost(2 * n * n * h, 6 * n * h),
        name="final",
    )(sc, held(rows), held(returned), held(ladder), held(part), held(hole), held(hole_other))


def local(amplitudes, recouple, ladder_int, cycle_coupling, drive, eps_part, eps_hole):
    _, n, half = amplitudes.shape
    core, here = lax.axis_index("dom"), lax.axis_index("chan")
    kept = 0
    for weight in (16, 4, 1):
        place = (here // weight) % 4
        high, low = place // 2, ((place + 1) // 2) % 2
        kept = 2 * kept + jnp.where(core == 0, low, high)
    sc = jnp.stack([core, kept]).astype(jnp.int32)

    amp_other = swap(amplitudes)
    rows, send = own_call(sc, recouple, amplitudes)
    c0 = coupling_call(sc, cycle_coupling, swap(cycle_coupling))
    send = other_call(sc, rows, amp_other, send)

    c4, c2, c1 = over(c0, 0), over(c0, 1), over(c0, 2)
    c6, c3, c5 = over(c4, 1), over(c2, 2), over(c1, 0)
    c7 = over(c6, 2)

    def exchange(array):
        return lax.all_to_all(array, BOTH, 0, 0, axis_index_groups=GROUPS, tiled=True)

    blocks = exchange(send)
    ladder, part = ladder_call(
        sc, ladder_int, amplitudes, amp_other, drive, swap(drive), eps_part
    )
    cycle_term = cycle_call(
        sc, blocks.reshape((8, 8) + blocks.shape[1:]), [c0, c1, c2, c3, c4, c5, c6, c7]
    )
    returned = exchange(cycle_term.reshape(blocks.shape))
    out, out_other = final_call(sc, rows, returned, ladder, part, eps_hole, swap(eps_hole))
    return lax.dynamic_update_slice(out, swap(out_other)[None], (1 - core, 0, 0))


def solution(mesh):
    placed = (
        P("chan", None, "dom"),
        P("chan", None, None),
        P("chan", None, None),
        P("chan", "dom", None),
        P("chan", None, "dom"),
        P("chan", None),
        P("chan", "dom"),
    )
    return jax.shard_map(
        local, mesh=mesh, in_specs=placed, out_specs=P("chan", None, "dom"), check_vma=False
    )
```

time: 124 us -> 122 us (0.984)
  Pallas kernels: 50.2 us -> 30.4 us
  local copies, waits for them, and re-layouts: 23.9 us -> 32.9 us
  starting transfers between devices: 31.3 us -> 38.5 us
  waiting for transfers between devices: 14.2 us -> 19.4 us
  other arithmetic: 2.76 us -> 0.07 us
    unnamed x22 -> x54, local copies, waits for them, and re-layouts: 14.8 us -> 31.8 us
    pallas_call x2 -> x3, Pallas kernels: 20.8 us -> 10.9 us  [the longest x1 7.43 us: own_call(): pl.pallas_call(own_kernel, grid_spec=pltpu.PrefetchScalarGridSpec(num_sca...]
    squeeze x3 -> x0, local copies, waits for them, and re-layouts: 5.85 us -> none  [the longest x2 4.78 us: others(): return swap(lax.dynamic_index_in_dim(array, 1 - core, 0, keepdims=False))]
    ppermute x7, waiting for transfers between devices: 10.4 us -> 15.8 us  [over(): return lax.ppermute(array, BOTH, FLIPS[axis])]
    ppermute x7, starting transfers between devices: 16.9 us -> 21.3 us  [over(): return lax.ppermute(array, BOTH, FLIPS[axis])]
    pallas_call x1, Pallas kernels: 6.89 us -> 3.38 us  [cycle_call(): pl.pallas_call(cycle_kernel, grid_spec=pltpu.PrefetchScalarGridSpec(num_s...]
    pallas_call x1, Pallas kernels: 11 us -> 7.65 us  [ladder_call(): pl.pallas_call(ladder_kernel, grid_spec=pltpu.PrefetchScalarGridSpec(num_...]
    pallas_call x1, Pallas kernels: 11.5 us -> 8.45 us  [final_call(): pl.pallas_call(final_kernel, grid_spec=pltpu.PrefetchScalarGridSpec(num_s...]
  transfers between devices with their start and end apart: 14 -> 14, of which waited for: 6 -> 6; matrix products, arithmetic and copies ran while one was open for 15% -> 0% of each run, Pallas kernels for 26% -> 18%
where the time goes in v2:
time: 122 us; the launch traced here: 121 us
  starting transfers between devices  38.5 us (32%)
  local copies, waits for them, and re-layouts  32.9 us (27%)
  Pallas kernels  30.4 us (25%)
  waiting for transfers between devices  19.4 us (16%)
    unnamed x54, local copies, waits for them, and re-layouts  31.8 us
    ppermute x7, starting transfers between devices, over(): return lax.ppermute(array, BOTH, FLIPS[axis])  21.3 us
    ppermute x7, waiting for transfers between devices, over(): return lax.ppermute(array, BOTH, FLIPS[axis])  15.8 us
    all_to_all x2, starting transfers between devices, exchange(): lax.all_to_all(array, BOTH, 0, 0, axis_index_groups=GROUPS, tiled=True)  9.55 us
    pallas_call x1, Pallas kernels, final_call(): pl.pallas_call(final_kernel, grid_spec=pltpu.PrefetchScalarGridSpec(num_s...  8.45 us
    pallas_call x1, Pallas kernels, ladder_call(): pl.pallas_call(ladder_kernel, grid_spec=pltpu.PrefetchScalarGridSpec(num_...  7.65 us
    ppermute x5, starting transfers between devices, swap(): return lax.ppermute(array, 'dom', [(0, 1), (1, 0)])  7.65 us
    pallas_call x1, Pallas kernels, own_call(): pl.pallas_call(own_kernel, grid_spec=pltpu.PrefetchScalarGridSpec(num_sca...  7.43 us
  transfers between devices with their start and end apart: 14, of which 6 were waited for; matrix products, arithmetic and copies ran while one was open for 0% of the time, Pallas kernels for 18%

profile of v2, /device:TPU:1, one launch (start us, length us, event | category | flops | bytes accessed | tf_op | source)
XLA Modules:
  0.0 121.4 jit_solution(14701071946626410362)
XLA Ops:
  0.0 1.4 %collective-permute-start = (bf16[2,2048,256]{2,1,0:T(8,128)(2,1)}, bf16[2,2048,256]{2,1,0:T(8,128)(2,1)S(1)}, u32[]{:S(2)}, u32[]{:S(2)}) collective-permute-start(bf16[2,2048,256]{2,1,0:T(8,128)(2,1)} %own.3), channel_id=1, source_target_pairs={{0,1},{1,0},{2,3},{3,2},{4,5},{5,4},{6,7},{7,6},{8,9},{9,8},{10,11... | collective-permute-start | bytes 6291464 | tf_op jit(solution)/shard_map/ppermute | solution.py:50
  1.4 0.0 collective-permute-start.1
  1.4 0.1 pad_add_fusion.sc
  1.5 7.4 %recoupled_own.1 = (bf16[2048,2048]{1,0:T(8,128)(2,1)S(1)}, bf16[64,32,512]{2,1,0:T(8,128)(2,1)S(1)}) custom-call(s32[2]{0:T(128)S(1)} %pad_add_fusion.sc, bf16[2,2048,2048]{2,1,0:T(8,128)(2,1)} %recouple.1, bf16[2,2048,256]{2,1,0:T(8,128)(2,1)} %own.3), custom_call_target="tpu_custom_call" | custom-call | flops 2147483648 | bytes 8388608 | tf_op jit(solution)/shard_map/recoupled_own/pallas_call | solution.py:117
  8.9 0.0 collective-permute-done.amp.oth
  8.9 2.9 %recoupled_other.1 = bf16[64,32,512]{2,1,0:T(8,128)(2,1)S(1)} custom-call(s32[2]{0:T(128)S(1)} %pad_add_fusion.sc, bf16[2048,2048]{1,0:T(8,128)(2,1)S(1)} %get-tuple-element.11.rows, bf16[2,2048,256]{2,1,0:T(8,128)(2,1)S(1)} %collective-permute-done.amp.oth, bf16[64,32,512]{2,1,0:T(8,128)(2,1)S(1)} %get-tuple-element.12.given), custom_call_target="tpu_custom_call", output_to_operand_aliasing={{}: (3, {})} | custom-call | flops 2147483648 | bytes 2097152 | tf_op jit(solution)/shard_map/recoupled_other/pallas_call | solution.py:142
  11.9 0.0 copy-start
  11.9 3.3 %copy-done = bf16[2048,2048]{1,0:T(8,128)(2,1)} copy-done((bf16[2048,2048]{1,0:T(8,128)(2,1)}, bf16[2048,2048]{1,0:T(8,128)(2,1)S(1)}, u32[]{:S(2)}) %copy-start) | copy-done | bytes 8388632
  15.1 1.3 %copy-done.3 = bf16[64,32,512]{2,1,0:T(8,128)(2,1)} copy-done((bf16[64,32,512]{2,1,0:T(8,128)(2,1)}, bf16[64,32,512]{2,1,0:T(8,128)(2,1)S(1)}, u32[]{:S(2)}) %copy-start.3) | copy-done | bytes 2097176
  16.5 5.1 %all-to-all-start = ((bf16[64,32,512]{2,1,0:T(8,128)(2,1)}), bf16[64,32,512]{2,1,0:T(8,128)(2,1)}, u32[]{:S(2)}, u32[]{:S(2)}) async-start(bf16[64,32,512]{2,1,0:T(8,128)(2,1)} %copy-done.3), calls=%async_computation | async-start | bytes 4194304 | tf_op jit(solution)/shard_map/all_to_all | solution.py:311
  21.5 0.0 collective-permute-done.1.oth
  21.5 0.0 copy-start.19
  21.5 0.8 copy-done.19
  22.3 1.0 copy-done.20
  23.4 0.6 coupling.1.refs_0_
  24.0 3.4 %collective-permute-start.5 = (bf16[512,512]{1,0:T(8,128)(2,1)S(1)}, bf16[512,512]{1,0:T(8,128)(2,1)S(1)}, u32[]{:S(2)}, u32[]{:S(2)}) collective-permute-start(bf16[512,512]{1,0:T(8,128)(2,1)S(1)} %coupling.1.refs_0_), channel_id=1, source_target_pairs={{0,32},{2,34},{8,40},{10,42},{32,0},{34,2},{40,8},{42,10},{6,38},{... | collective-permute-start | bytes 1572872 | tf_op jit(solution)/shard_map/ppermute | solution.py:54
  27.3 2.7 %collective-permute-start.3 = (bf16[512,512]{1,0:T(8,128)(2,1)S(1)}, bf16[512,512]{1,0:T(8,128)(2,1)S(1)}, u32[]{:S(2)}, u32[]{:S(2)}) collective-permute-start(bf16[512,512]{1,0:T(8,128)(2,1)S(1)} %coupling.1.refs_0_), channel_id=1, source_target_pairs={{0,8},{2,10},{8,0},{10,2},{32,40},{34,42},{40,32},{42,34},{6,14},{... | collective-permute-start | bytes 1572872 | tf_op jit(solution)/shard_map/ppermute | solution.py:54
  30.1 2.5 %collective-permute-start.2 = (bf16[512,512]{1,0:T(8,128)(2,1)S(1)}, bf16[512,512]{1,0:T(8,128)(2,1)S(1)}, u32[]{:S(2)}, u32[]{:S(2)}) collective-permute-start(bf16[512,512]{1,0:T(8,128)(2,1)S(1)} %coupling.1.refs_0_), channel_id=1, source_target_pairs={{0,2},{2,0},{8,10},{10,8},{32,34},{34,32},{40,42},{42,40},{6,4},{4... | collective-permute-start | bytes 1572872 | tf_op jit(solution)/shard_map/ppermute | solution.py:54
  32.5 9.3 %collective-permute-done.5.refs_4_ = bf16[512,512]{1,0:T(8,128)(2,1)S(1)} collective-permute-done((bf16[512,512]{1,0:T(8,128)(2,1)S(1)}, bf16[512,512]{1,0:T(8,128)(2,1)S(1)}, u32[]{:S(2)}, u32[]{:S(2)}) %collective-permute-start.5) | collective-permute-done | bytes 524320 | tf_op jit(solution)/shard_map/ppermute | solution.py:54
  41.9 4.9 %collective-permute-start.7 = (bf16[512,512]{1,0:T(8,128)(2,1)S(1)}, bf16[512,512]{1,0:T(8,128)(2,1)S(1)}, u32[]{:S(2)}, u32[]{:S(2)}) collective-permute-start(bf16[512,512]{1,0:T(8,128)(2,1)S(1)} %collective-permute-done.5.refs_4_), channel_id=1, source_target_pairs={{0,8},{2,10},{8,0},{10,2},{32,40},{34,42},{40,32},{42,34},{6,14},{... | collective-permute-start | bytes 1572872 | tf_op jit(solution)/shard_map/ppermute | solution.py:54
  46.8 0.0 collective-permute-start.9
  46.8 0.0 collective-permute-done.3.refs_2_
  46.8 4.0 %collective-permute-start.4 = (bf16[512,512]{1,0:T(8,128)(2,1)S(1)}, bf16[512,512]{1,0:T(8,128)(2,1)S(1)}, u32[]{:S(2)}, u32[]{:S(2)}) collective-permute-start(bf16[512,512]{1,0:T(8,128)(2,1)S(1)} %collective-permute-done.3.refs_2_), channel_id=1, source_target_pairs={{0,2},{2,0},{8,10},{10,8},{32,34},{34,32},{40,42},{42,40},{6,4},{4... | collective-permute-start | bytes 1572872 | tf_op jit(solution)/shard_map/ppermute | solution.py:54
  50.8 0.8 copy-done.6
  51.6 0.0 collective-permute-done.2.refs_1_
  51.6 2.4 %collective-permute-start.6 = (bf16[512,512]{1,0:T(8,128)(2,1)S(1)}, bf16[512,512]{1,0:T(8,128)(2,1)S(1)}, u32[]{:S(2)}, u32[]{:S(2)}) collective-permute-start(bf16[512,512]{1,0:T(8,128)(2,1)S(1)} %collective-permute-done.2.refs_1_), channel_id=1, source_target_pairs={{0,32},{2,34},{8,40},{10,42},{32,0},{34,2},{40,8},{42,10},{6,38},{... | collective-permute-start | bytes 1572872 | tf_op jit(solution)/shard_map/ppermute | solution.py:54
  54.0 0.8 copy-done.8
  54.8 1.0 collective-permute-done.7.refs_6_
  55.9 1.4 %collective-permute-start.8 = (bf16[512,512]{1,0:T(8,128)(2,1)S(1)}, bf16[512,512]{1,0:T(8,128)(2,1)S(1)}, u32[]{:S(2)}, u32[]{:S(2)}) collective-permute-start(bf16[512,512]{1,0:T(8,128)(2,1)S(1)} %collective-permute-done.7.refs_6_), channel_id=1, source_target_pairs={{0,2},{2,0},{8,10},{10,8},{32,34},{34,32},{40,42},{42,40},{6,4},{4... | collective-permute-start | bytes 1572872 | tf_op jit(solution)/shard_map/ppermute | solution.py:54
  57.3 0.8 copy-done.10
  58.1 0.0 collective-permute-done.4.refs_3_
  58.1 0.8 copy-done.12
  58.9 1.9 %collective-permute-done.6.refs_5_ = bf16[512,512]{1,0:T(8,128)(2,1)S(1)} collective-permute-done((bf16[512,512]{1,0:T(8,128)(2,1)S(1)}, bf16[512,512]{1,0:T(8,128)(2,1)S(1)}, u32[]{:S(2)}, u32[]{:S(2)}) %collective-permute-start.6) | collective-permute-done | bytes 524320 | tf_op jit(solution)/shard_map/ppermute | solution.py:54
  60.8 0.8 copy-done.14
  61.6 3.5 %collective-permute-done.8.refs_7_ = bf16[512,512]{1,0:T(8,128)(2,1)S(1)} collective-permute-done((bf16[512,512]{1,0:T(8,128)(2,1)S(1)}, bf16[512,512]{1,0:T(8,128)(2,1)S(1)}, u32[]{:S(2)}, u32[]{:S(2)}) %collective-permute-start.8) | collective-permute-done | bytes 524320 | tf_op jit(solution)/shard_map/ppermute | solution.py:54
  65.1 0.8 copy-done.16
  66.0 0.0 all-to-all-done
  66.0 1.0 copy-done.7
  67.0 1.0 copy-done.9
  68.0 1.0 copy-done.11
  69.1 1.0 copy-done.13
  70.1 1.0 copy-done.15
  71.2 1.0 copy-done.17
  72.2 3.4 %cycle.1 = bf16[8,8,32,512]{3,2,1,0:T(8,128)(2,1)S(1)} custom-call(s32[2]{0:T(128)S(1)} %pad_add_fusion.sc, bf16[8,8,32,512]{3,2,1,0:T(8,128)(2,1)} %bitcast.2.x, bf16[512,512]{1,0:T(8,128)(2,1)S(1)} %coupling.1.refs_0_, bf16[512,512]{1,0:T(8,128)(2,1)S(1)} %copy-done.9, bf16[512,512]{1,0:T(8,128)(2,1)S(1)} %copy-done.7, bf16[512,512]{1,0:T(8,128)(2,1)S(1)} %copy-done.13, ...), custom_call_target="tpu_custom_call" | custom-call | flops 1073741824 | bytes 8388608 | tf_op jit(solution)/shard_map/cycle/pallas_call | solution.py:198
  75.6 0.0 copy-start.2
  75.6 1.3 %copy-done.2 = bf16[8,8,32,512]{3,2,1,0:T(8,128)(2,1)} copy-done((bf16[8,8,32,512]{3,2,1,0:T(8,128)(2,1)}, bf16[8,8,32,512]{3,2,1,0:T(8,128)(2,1)S(1)}, u32[]{:S(2)}) %copy-start.2) | copy-done | bytes 2097176
  76.9 4.5 %all-to-all-start.1 = ((bf16[64,32,512]{2,1,0:T(8,128)(2,1)}), bf16[64,32,512]{2,1,0:T(8,128)(2,1)}, u32[]{:S(2)}, u32[]{:S(2)}) async-start(bf16[64,32,512]{2,1,0:T(8,128)(2,1)} %bitcast.6), calls=%async_computation.1 | async-start | bytes 4194304 | tf_op jit(solution)/shard_map/all_to_all | solution.py:311
  81.4 0.0 copy-done.26
  81.4 0.9 collective-permute-start.10
  82.4 0.0 collective-permute-done.9.drive_oth
  82.4 1.6 %copy-done.4 = bf16[2,2048,256]{2,1,0:T(8,128)(2,1)S(1)} copy-done((bf16[2,2048,256]{2,1,0:T(8,128)(2,1)S(1)}, bf16[2,2048,256]{2,1,0:T(8,128)(2,1)}, u32[]{:S(2)}) %copy-start.4) | copy-done | bytes 2097176
  84.0 1.6 %copy-done.5 = bf16[2,2048,256]{2,1,0:T(8,128)(2,1)S(1)} copy-done((bf16[2,2048,256]{2,1,0:T(8,128)(2,1)S(1)}, bf16[2,2048,256]{2,1,0:T(8,128)(2,1)}, u32[]{:S(2)}) %copy-start.5) | copy-done | bytes 2097176
  85.5 7.7 %ladder.1 = (f32[2048,512]{1,0:T(8,128)S(1)}, f32[2048,128]{1,0:T(8,128)S(1)}) custom-call(s32[2]{0:T(128)S(1)} %pad_add_fusion.sc, bf16[2,2048,2048]{2,1,0:T(8,128)(2,1)} %l.1, bf16[2,2048,256]{2,1,0:T(8,128)(2,1)S(1)} %copy-done.4, bf16[2,2048,256]{2,1,0:T(8,128)(2,1)S(1)} %collective-permute-done.amp.oth, bf16[2,2048,256]{2,1,0:T(8,128)(2,1)S(1)} %copy-done.5, ...), custom_call_target="tpu_custom_call" | custom-call | flops 4294967296 | bytes 16777216 | tf_op jit(solution)/shard_map/ladder/pallas_call | solution.py:223
  93.2 2.0 %copy-done.22 = f32[2048,512]{1,0:T(8,128)} copy-done((f32[2048,512]{1,0:T(8,128)}, f32[2048,512]{1,0:T(8,128)S(1)}, u32[]{:S(2)}) %copy-start.22) | copy-done | bytes 4194328
  95.2 1.0 copy-done.24
  96.3 0.0 collective-permute-done.10.hole_oth
  96.3 1.3 %all-to-all-done.1.x = bf16[64,32,512]{2,1,0:T(8,128)(2,1)} async-done(((bf16[64,32,512]{2,1,0:T(8,128)(2,1)}), bf16[64,32,512]{2,1,0:T(8,128)(2,1)}, u32[]{:S(2)}, u32[]{:S(2)}) %all-to-all-start.1) | async-done | bytes 2097184 | tf_op jit(solution)/shard_map/all_to_all | solution.py:311
  97.6 3.4 %copy-done.1 = bf16[2048,2048]{1,0:T(8,128)(2,1)S(1)} copy-done((bf16[2048,2048]{1,0:T(8,128)(2,1)S(1)}, bf16[2048,2048]{1,0:T(8,128)(2,1)}, u32[]{:S(2)}) %copy-start.1) | copy-done | bytes 8388632
  100.9 2.2 %copy-done.23 = f32[2048,512]{1,0:T(8,128)S(1)} copy-done((f32[2048,512]{1,0:T(8,128)S(1)}, f32[2048,512]{1,0:T(8,128)}, u32[]{:S(2)}) %copy-start.23) | copy-done | bytes 4194328
  103.1 1.2 %copy-done.25 = f32[2048,128]{1,0:T(8,128)S(1)} copy-done((f32[2048,128]{1,0:T(8,128)S(1)}, f32[2048,128]{1,0:T(8,128)}, u32[]{:S(2)}) %copy-start.25) | copy-done | bytes 1048600
  104.3 8.4 %final.1 = (bf16[2,2048,256]{2,1,0:T(8,128)(2,1)}, bf16[2048,256]{1,0:T(8,128)(2,1)S(1)}) custom-call(s32[2]{0:T(128)S(1)} %pad_add_fusion.sc, bf16[2048,2048]{1,0:T(8,128)(2,1)S(1)} %copy-done.1, bf16[64,32,512]{2,1,0:T(8,128)(2,1)} %all-to-all-done.1.x, f32[2048,512]{1,0:T(8,128)S(1)} %copy-done.23, f32[2048,128]{1,0:T(8,128)S(1)} %copy-done.25, ...), custom_call_target="tpu_custom_call" | custom-call | flops 4294967296 | bytes 6291456 | tf_op jit(solution)/shard_map/final/pallas_call | solution.py:269
  112.8 5.3 %collective-permute-start.11 = (bf16[2048,256]{1,0:T(8,128)(2,1)S(1)}, bf16[2048,256]{1,0:T(8,128)(2,1)S(1)}, u32[]{:S(2)}, u32[]{:S(2)}) collective-permute-start(bf16[2048,256]{1,0:T(8,128)(2,1)S(1)} %get-tuple-element.16), channel_id=1, source_target_pairs={{0,1},{1,0},{2,3},{3,2},{4,5},{5,4},{6,7},{7,6},{8,9},{9,8},{10,11... | collective-permute-start | bytes 3145736 | tf_op jit(solution)/shard_map/ppermute | solution.py:50
  118.1 2.3 %collective-permute-done.11 = bf16[2048,256]{1,0:T(8,128)(2,1)S(1)} collective-permute-done((bf16[2048,256]{1,0:T(8,128)(2,1)S(1)}, bf16[2048,256]{1,0:T(8,128)(2,1)S(1)}, u32[]{:S(2)}, u32[]{:S(2)}) %collective-permute-start.11) | collective-permute-done | bytes 1048608 | tf_op jit(solution)/shard_map/ppermute | solution.py:50
  120.4 1.0 bitcast_dynamic-update-slice_fusion
  (26 shorter events, 0.0 us)
Async XLA Ops:
  0.0 8.9 %collective-permute-start = (bf16[2,2048,256]{2,1,0:T(8,128)(2,1)}, bf16[2,2048,256]{2,1,0:T(8,128)(2,1)S(1)}, u32[]{:S(2)}, u32[]{:S(2)}) collective-permute-start(bf16[2,2048,256]{2,1,0:T(8,128)(2,1)} %own.3), channel_id=1, source_target_pairs={{0,1},{1,0},{2,3},{3,2},{4,5},{5,4},{6,7},{7,6},{8,9},{9,8},{10,11... | collective-permute-start | bytes 6291464 | tf_op jit(solution)/shard_map/ppermute | solution.py:50
  1.4 20.1 %collective-permute-start.1 = (bf16[2,256,512]{2,1,0:T(8,128)(2,1)}, bf16[2,256,512]{2,1,0:T(8,128)(2,1)S(1)}, u32[]{:S(2)}, u32[]{:S(2)}) collective-permute-start(bf16[2,256,512]{2,1,0:T(8,128)(2,1)} %own.2), channel_id=1, source_target_pairs={{0,1},{1,0},{2,3},{3,2},{4,5},{5,4},{6,7},{7,6},{8,9},{9,8},{10,11... | collective-permute-start | bytes 1572872 | tf_op jit(solution)/shard_map/ppermute | solution.py:50
  11.9 3.3 %copy-start = (bf16[2048,2048]{1,0:T(8,128)(2,1)}, bf16[2048,2048]{1,0:T(8,128)(2,1)S(1)}, u32[]{:S(2)}) copy-start(bf16[2048,2048]{1,0:T(8,128)(2,1)S(1)} %get-tuple-element.11.rows) | copy-start | bytes 25165828
  15.1 1.3 %copy-start.3 = (bf16[64,32,512]{2,1,0:T(8,128)(2,1)}, bf16[64,32,512]{2,1,0:T(8,128)(2,1)S(1)}, u32[]{:S(2)}) copy-start(bf16[64,32,512]{2,1,0:T(8,128)(2,1)S(1)} %recoupled_other.1) | copy-start | bytes 6291460
  16.5 5.9 %copy-start.18 = (bf16[2,256,512]{2,1,0:T(8,128)(2,1)S(1)}, bf16[2,256,512]{2,1,0:T(8,128)(2,1)}, u32[]{:S(2)}) copy-start(bf16[2,256,512]{2,1,0:T(8,128)(2,1)} %own.2) | copy-start | bytes 1572868
  16.5 49.5 %all-to-all-start = ((bf16[64,32,512]{2,1,0:T(8,128)(2,1)}), bf16[64,32,512]{2,1,0:T(8,128)(2,1)}, u32[]{:S(2)}, u32[]{:S(2)}) async-start(bf16[64,32,512]{2,1,0:T(8,128)(2,1)} %copy-done.3), calls=%async_computation | async-start | bytes 4194304 | tf_op jit(solution)/shard_map/all_to_all | solution.py:311
  21.5 0.8 copy-start.19
  22.3 1.0 copy-start.20
  24.0 17.9 %collective-permute-start.5 = (bf16[512,512]{1,0:T(8,128)(2,1)S(1)}, bf16[512,512]{1,0:T(8,128)(2,1)S(1)}, u32[]{:S(2)}, u32[]{:S(2)}) collective-permute-start(bf16[512,512]{1,0:T(8,128)(2,1)S(1)} %coupling.1.refs_0_), channel_id=1, source_target_pairs={{0,32},{2,34},{8,40},{10,42},{32,0},{34,2},{40,8},{42,10},{6,38},{... | collective-permute-start | bytes 1572872 | tf_op jit(solution)/shard_map/ppermute | solution.py:54
  27.3 19.5 %collective-permute-start.3 = (bf16[512,512]{1,0:T(8,128)(2,1)S(1)}, bf16[512,512]{1,0:T(8,128)(2,1)S(1)}, u32[]{:S(2)}, u32[]{:S(2)}) collective-permute-start(bf16[512,512]{1,0:T(8,128)(2,1)S(1)} %coupling.1.refs_0_), channel_id=1, source_target_pairs={{0,8},{2,10},{8,0},{10,2},{32,40},{34,42},{40,32},{42,34},{6,14},{... | collective-permute-start | bytes 1572872 | tf_op jit(solution)/shard_map/ppermute | solution.py:54
  30.1 21.5 %collective-permute-start.2 = (bf16[512,512]{1,0:T(8,128)(2,1)S(1)}, bf16[512,512]{1,0:T(8,128)(2,1)S(1)}, u32[]{:S(2)}, u32[]{:S(2)}) collective-permute-start(bf16[512,512]{1,0:T(8,128)(2,1)S(1)} %coupling.1.refs_0_), channel_id=1, source_target_pairs={{0,2},{2,0},{8,10},{10,8},{32,34},{34,32},{40,42},{42,40},{6,4},{4... | collective-permute-start | bytes 1572872 | tf_op jit(solution)/shard_map/ppermute | solution.py:54
  41.9 14.0 %collective-permute-start.7 = (bf16[512,512]{1,0:T(8,128)(2,1)S(1)}, bf16[512,512]{1,0:T(8,128)(2,1)S(1)}, u32[]{:S(2)}, u32[]{:S(2)}) collective-permute-start(bf16[512,512]{1,0:T(8,128)(2,1)S(1)} %collective-permute-done.5.refs_4_), channel_id=1, source_target_pairs={{0,8},{2,10},{8,0},{10,2},{32,40},{34,42},{40,32},{42,34},{6,14},{... | collective-permute-start | bytes 1572872 | tf_op jit(solution)/shard_map/ppermute | solution.py:54
  46.8 35.6 %collective-permute-start.9 = (bf16[2,2048,256]{2,1,0:T(8,128)(2,1)}, bf16[2,2048,256]{2,1,0:T(8,128)(2,1)}, u32[]{:S(2)}, u32[]{:S(2)}) collective-permute-start(bf16[2,2048,256]{2,1,0:T(8,128)(2,1)} %drive.1), channel_id=1, source_target_pairs={{0,1},{1,0},{2,3},{3,2},{4,5},{5,4},{6,7},{7,6},{8,9},{9,8},{10,11... | collective-permute-start | bytes 6291464 | tf_op jit(solution)/shard_map/ppermute | solution.py:50
  46.8 11.3 %collective-permute-start.4 = (bf16[512,512]{1,0:T(8,128)(2,1)S(1)}, bf16[512,512]{1,0:T(8,128)(2,1)S(1)}, u32[]{:S(2)}, u32[]{:S(2)}) collective-permute-start(bf16[512,512]{1,0:T(8,128)(2,1)S(1)} %collective-permute-done.3.refs_2_), channel_id=1, source_target_pairs={{0,2},{2,0},{8,10},{10,8},{32,34},{34,32},{40,42},{42,40},{6,4},{4... | collective-permute-start | bytes 1572872 | tf_op jit(solution)/shard_map/ppermute | solution.py:54
  50.8 0.8 copy-start.6
  51.6 9.2 %collective-permute-start.6 = (bf16[512,512]{1,0:T(8,128)(2,1)S(1)}, bf16[512,512]{1,0:T(8,128)(2,1)S(1)}, u32[]{:S(2)}, u32[]{:S(2)}) collective-permute-start(bf16[512,512]{1,0:T(8,128)(2,1)S(1)} %collective-permute-done.2.refs_1_), channel_id=1, source_target_pairs={{0,32},{2,34},{8,40},{10,42},{32,0},{34,2},{40,8},{42,10},{6,38},{... | collective-permute-start | bytes 1572872 | tf_op jit(solution)/shard_map/ppermute | solution.py:54
  54.0 0.8 copy-start.8
  55.9 9.2 %collective-permute-start.8 = (bf16[512,512]{1,0:T(8,128)(2,1)S(1)}, bf16[512,512]{1,0:T(8,128)(2,1)S(1)}, u32[]{:S(2)}, u32[]{:S(2)}) collective-permute-start(bf16[512,512]{1,0:T(8,128)(2,1)S(1)} %collective-permute-done.7.refs_6_), channel_id=1, source_target_pairs={{0,2},{2,0},{8,10},{10,8},{32,34},{34,32},{40,42},{42,40},{6,4},{4... | collective-permute-start | bytes 1572872 | tf_op jit(solution)/shard_map/ppermute | solution.py:54
  57.3 0.8 copy-start.10
  58.1 0.8 copy-start.12
  60.8 0.8 copy-start.14
  65.1 0.8 copy-start.16
  66.0 1.0 copy-start.7
  67.0 1.0 copy-start.9
  68.0 1.0 copy-start.11
  69.1 1.0 copy-start.13
  70.1 1.0 copy-start.15
  71.2 1.0 copy-start.17
  75.6 1.3 %copy-start.2 = (bf16[8,8,32,512]{3,2,1,0:T(8,128)(2,1)}, bf16[8,8,32,512]{3,2,1,0:T(8,128)(2,1)S(1)}, u32[]{:S(2)}) copy-start(bf16[8,8,32,512]{3,2,1,0:T(8,128)(2,1)S(1)} %cycle.1) | copy-start | bytes 6291460
  76.9 4.5 %copy-start.26 = (f32[2,256]{1,0:T(2,128)S(1)}, f32[2,256]{1,0:T(2,128)}, u32[]{:S(2)}) copy-start(f32[2,256]{1,0:T(2,128)} %hole.1) | copy-start | bytes 6148
  76.9 5.4 %copy-start.21 = (f32[2,2048]{1,0:T(2,128)S(1)}, f32[2,2048]{1,0:T(2,128)}, u32[]{:S(2)}) copy-start(f32[2,2048]{1,0:T(2,128)} %part.1) | copy-start | bytes 49156
  76.9 20.6 %all-to-all-start.1 = ((bf16[64,32,512]{2,1,0:T(8,128)(2,1)}), bf16[64,32,512]{2,1,0:T(8,128)(2,1)}, u32[]{:S(2)}, u32[]{:S(2)}) async-start(bf16[64,32,512]{2,1,0:T(8,128)(2,1)} %bitcast.6), calls=%async_computation.1 | async-start | bytes 4194304 | tf_op jit(solution)/shard_map/all_to_all | solution.py:311
  81.4 14.8 %collective-permute-start.10 = (f32[2,256]{1,0:T(2,128)S(1)}, f32[2,256]{1,0:T(2,128)S(1)}, u32[]{:S(2)}, u32[]{:S(2)}) collective-permute-start(f32[2,256]{1,0:T(2,128)S(1)} %copy-done.26), channel_id=1, source_target_pairs={{0,1},{1,0},{2,3},{3,2},{4,5},{5,4},{6,7},{7,6},{8,9},{9,8},{10,11... | collective-permute-start | bytes 6152 | tf_op jit(solution)/shard_map/ppermute | solution.py:50
  82.4 1.6 %copy-start.4 = (bf16[2,2048,256]{2,1,0:T(8,128)(2,1)S(1)}, bf16[2,2048,256]{2,1,0:T(8,128)(2,1)}, u32[]{:S(2)}) copy-start(bf16[2,2048,256]{2,1,0:T(8,128)(2,1)} %own.3) | copy-start | bytes 6291460
  84.0 1.6 %copy-start.5 = (bf16[2,2048,256]{2,1,0:T(8,128)(2,1)S(1)}, bf16[2,2048,256]{2,1,0:T(8,128)(2,1)}, u32[]{:S(2)}) copy-start(bf16[2,2048,256]{2,1,0:T(8,128)(2,1)} %drive.1) | copy-start | bytes 6291460
  93.2 2.0 %copy-start.22 = (f32[2048,512]{1,0:T(8,128)}, f32[2048,512]{1,0:T(8,128)S(1)}, u32[]{:S(2)}) copy-start(f32[2048,512]{1,0:T(8,128)S(1)} %get-tuple-element.13.ladder) | copy-start | bytes 12582916
  95.2 1.0 copy-start.24
  97.6 3.4 %copy-start.1 = (bf16[2048,2048]{1,0:T(8,128)(2,1)S(1)}, bf16[2048,2048]{1,0:T(8,128)(2,1)}, u32[]{:S(2)}) copy-start(bf16[2048,2048]{1,0:T(8,128)(2,1)} %copy-done) | copy-start | bytes 25165828
  100.9 2.2 %copy-start.23 = (f32[2048,512]{1,0:T(8,128)S(1)}, f32[2048,512]{1,0:T(8,128)}, u32[]{:S(2)}) copy-start(f32[2048,512]{1,0:T(8,128)} %copy-done.22) | copy-start | bytes 12582916
  103.1 1.2 %copy-start.25 = (f32[2048,128]{1,0:T(8,128)S(1)}, f32[2048,128]{1,0:T(8,128)}, u32[]{:S(2)}) copy-start(f32[2048,128]{1,0:T(8,128)} %copy-done.24) | copy-start | bytes 3145732
  112.8 7.6 %collective-permute-start.11 = (bf16[2048,256]{1,0:T(8,128)(2,1)S(1)}, bf16[2048,256]{1,0:T(8,128)(2,1)S(1)}, u32[]{:S(2)}, u32[]{:S(2)}) collective-permute-start(bf16[2048,256]{1,0:T(8,128)(2,1)S(1)} %get-tuple-element.16), channel_id=1, source_target_pairs={{0,1},{1,0},{2,3},{3,2},{4,5},{5,4},{6,7},{7,6},{8,9},{9,8},{10,11... | collective-permute-start | bytes 3145736 | tf_op jit(solution)/shard_map/ppermute | solution.py:50

commit v3 on v0

v3 whole, which is shorter than its diff:
```python
import functools
import itertools

import jax
import jax.numpy as jnp
from jax import lax
from jax.experimental import pallas as pl
from jax.experimental.pallas import tpu as pltpu
from jax.sharding import PartitionSpec as P

RING = ((0, 0), (0, 1), (1, 1), (1, 0))
PLACE = {bits: at for at, bits in enumerate(RING)}
BF, F32 = jnp.bfloat16, jnp.float32
VMEM = pltpu.VMEM


def chip(bits):
    return (PLACE[bits[0]] * 4 + PLACE[bits[1]]) * 4 + PLACE[bits[2]]


def bits_of(core, moved, kept):
    return [(m, k) if core == 0 else (k, m) for m, k in zip(moved, kept)]


THREE = list(itertools.product((0, 1), repeat=3))
def flips(of_moved, of_kept):
    pairs = []
    for core, moved, kept in itertools.product(range(2), THREE, THREE):
        to = [m ^ f for m, f in zip(moved, THREE[of_moved])]
        at = [k ^ f for k, f in zip(kept, THREE[of_kept])]
        pairs.append(
            (
                chip(bits_of(core, moved, kept)) * 2 + core,
                chip(bits_of(core, to, at)) * 2 + core,
            )
        )
    return pairs


BOTH = ("chan", "dom")


def swap(array):
    return lax.ppermute(array, "dom", [(0, 1), (1, 0)])


def over(array, moved=0, kept=0):
    return lax.ppermute(array, BOTH, flips(moved, kept))


def segment(core, moved, kept):
    at = 0
    for shift in (2, 1, 0):
        m, k = (moved >> shift) & 1, (kept >> shift) & 1
        at = at * 4 + 2 * jnp.where(core == 0, m, k) + (m ^ k)
    return at


def dot(a, b):
    return jnp.dot(a, b, preferred_element_type=F32)


def dot_rows(a, b):
    return lax.dot_general(a, b, (((0,), (0,)), ((), ())), preferred_element_type=F32)


def params(mib):
    return pltpu.CompilerParams(vmem_limit_bytes=mib * 1024 * 1024)


def cost(flops, moved):
    return pl.CostEstimate(flops=flops, bytes_accessed=moved, transcendentals=0)


def held(array):
    return pltpu.with_memory_space_constraint(array, VMEM)


def far(array):
    return pltpu.with_memory_space_constraint(array, pltpu.HBM)


WHOLE = pl.BlockSpec(memory_space=VMEM)
AWAY = pl.BlockSpec(memory_space=pltpu.HBM)
WAIT = pl.BlockSpec(memory_space=pl.ANY)
TILES = 4
FIRST, THEN = (7, 1), (3, 5, 6, 2, 4)
BACK = (0, 7, 3, 5, 1), (6, 2, 4)
EARLY, LATE = (0, 7, 3, 5), (1, 6, 2, 4)


def tie_kernel(*refs):
    pass


def tie(arrays, *waits):
    count = len(arrays)
    return pl.pallas_call(
        tie_kernel,
        in_specs=[WAIT] * (count + len(waits)),
        out_specs=[WAIT] * count,
        out_shape=[jax.ShapeDtypeStruct(a.shape, a.dtype) for a in arrays],
        input_output_aliases={i: i for i in range(count)},
        compiler_params=params(1),
        cost_estimate=cost(0, 0),
        name="tie",
    )(*arrays, *waits)


def load_kernel(sc, recouple, amplitudes, drive, rows, amp, amp_send, drive_send, sems):
    core, seg = sc[0], rows.shape[0] // 64
    copies = [
        pltpu.make_async_copy(source, to, sems.at[64 + i])
        for i, (source, to) in enumerate(
            (
                (amplitudes.at[1 - core], amp_send),
                (drive.at[1 - core], drive_send),
                (amplitudes.at[core], amp),
            )
        )
    ]
    for at in range(64):
        chip_at = segment(core, sc[2] ^ (at // 8), sc[1] ^ (at % 8))
        source = recouple.at[core, pl.ds(pl.multiple_of(chip_at * seg, seg), seg)]
        copies.append(
            pltpu.make_async_copy(source, rows.at[at * seg : (at + 1) * seg], sems.at[at])
        )
    for copy in copies:
        copy.start()
    for copy in copies:
        copy.wait()


def load_call(sc, recouple, amplitudes, drive):
    _, n, half = amplitudes.shape
    return pl.pallas_call(
        load_kernel,
        grid_spec=pltpu.PrefetchScalarGridSpec(
            num_scalar_prefetch=1,
            grid=(1,),
            in_specs=[AWAY] * 3,
            out_specs=[WHOLE] * 4,
            scratch_shapes=[pltpu.SemaphoreType.DMA((67,))],
        ),
        out_shape=[VMEM((n, n), BF)] + [VMEM((n, half), BF)] * 3,
        compiler_params=params(1),
        cost_estimate=cost(0, 2 * n * n),
        name="load",
    )(sc, far(recouple), far(amplitudes), far(drive))


def spread(got, i, outs, columns):
    each = 8 // TILES
    seg = outs[0].shape[1]
    for j in range(each):
        piece = got[j * 8 * seg : (j + 1) * 8 * seg]
        outs[i * each + j][:, :, columns] = piece.reshape(8, seg, piece.shape[1])


def own_kernel(rows, amp, *refs):
    outs = refs[-8:]
    tile = rows.shape[0] // TILES
    for i in range(TILES):
        got = dot(rows[i * tile : (i + 1) * tile], amp[...]).astype(BF)
        spread(got, i, outs, slice(0, amp.shape[1]))


def own_call(rows, amp, *waits):
    n, half = amp.shape
    return pl.pallas_call(
        own_kernel,
        in_specs=[WHOLE, WHOLE] + [WAIT] * len(waits),
        out_specs=[WHOLE] * 8,
        out_shape=[VMEM((8, n // 64, 2 * half), BF)] * 8,
        compiler_params=params(4),
        cost_estimate=cost(2 * n * n * half, 2 * n * n),
        name="recoupled_own",
    )(held(rows), held(amp), *waits)


def other_kernel(rows, amp, *refs):
    outs = refs[-8:]
    n, half = amp.shape
    tile = n // TILES
    for i in range(TILES):
        got = dot(rows[i * tile : (i + 1) * tile], amp[...]).astype(BF)
        spread(got, i, outs, slice(half, 2 * half))


def other_call(rows, amp_other, begun, *waits):
    n, half = amp_other.shape
    return pl.pallas_call(
        other_kernel,
        in_specs=[WHOLE] * 10 + [WAIT] * len(waits),
        out_specs=[WHOLE] * 8,
        out_shape=[VMEM(begun[0].shape, BF)] * 8,
        input_output_aliases={2 + r: r for r in range(8)},
        compiler_params=params(4),
        cost_estimate=cost(2 * n * n * half, 4 * n * half),
        name="recoupled_other",
    )(held(rows), held(amp_other), *[held(block) for block in begun], *waits)


def coupling_kernel(sc, own, oth, *refs):
    out, sems = refs[-2:]
    half = own.shape[1]
    copies = []
    for part, ref in enumerate((own, oth)):
        for side in range(2):
            at = pl.ds(pl.multiple_of((sc[0] ^ side) * half, half), half)
            to = out.at[part * half : (part + 1) * half, side * half : (side + 1) * half]
            copies.append(pltpu.make_async_copy(ref.at[sc[0], :, at], to, sems.at[len(copies)]))
    for copy in copies:
        copy.start()
    for copy in copies:
        copy.wait()


def coupling_call(sc, own, oth, *waits):
    _, half, h = own.shape
    return pl.pallas_call(
        coupling_kernel,
        grid_spec=pltpu.PrefetchScalarGridSpec(
            num_scalar_prefetch=1,
            grid=(1,),
            in_specs=[AWAY, WAIT] + [WAIT] * len(waits),
            out_specs=WHOLE,
            scratch_shapes=[pltpu.SemaphoreType.DMA((4,))],
        ),
        out_shape=VMEM((h, h), BF),
        compiler_params=params(1),
        cost_estimate=cost(0, 4 * h * h),
        name="coupling",
    )(sc, far(own), oth, *waits)


def cycle_kernel(count, *refs):
    blocks, couplings, outs = refs[:count], refs[count : count + 8], refs[-count:]
    seg = blocks[0].shape[1]
    for k in range(8):
        lines = jnp.concatenate([block[k] for block in blocks], axis=0)
        got = dot(lines, couplings[k][...]).astype(BF)
        for r, out in enumerate(outs):
            out[k] = got[r * seg : (r + 1) * seg]


def cycle_call(blocks, couplings, *waits):
    count = len(blocks)
    _, rows, h = blocks[0].shape
    return pl.pallas_call(
        functools.partial(cycle_kernel, count),
        in_specs=[WHOLE] * (count + 8) + [WAIT] * len(waits),
        out_specs=[WHOLE] * count,
        out_shape=[VMEM(blocks[0].shape, BF)] * count,
        compiler_params=params(4),
        cost_estimate=cost(16 * count * rows * h * h, 32 * count * rows * h + 16 * h * h),
        name="cycle",
    )(*[held(b) for b in blocks], *[held(c) for c in couplings], *waits)


def ladder_kernel(tiles, sc, ladder_int, amp, amp_other, drive, drive_other, part, *refs):
    out, out_part = refs[-2:]
    core, half, tile = sc[0], amp.shape[1], amp.shape[0] // TILES
    for i in tiles:
        at = slice(i * tile, (i + 1) * tile)
        left = ladder_int[core, at]
        out[at, :half] = dot(left, amp[...]) + drive[core, at].astype(F32)
        out[at, half:] = dot(left, amp_other[...]) + drive_other[at].astype(F32)
        out_part[at, :] = jnp.broadcast_to(part[pl.ds(core, 1), at], (128, tile)).T


def ladder_call(tiles, begun, operands, *waits):
    n, half = operands[2].shape
    operands = operands[:1] + [held(a) for a in operands[1:]]
    return pl.pallas_call(
        functools.partial(ladder_kernel, tiles),
        grid_spec=pltpu.PrefetchScalarGridSpec(
            num_scalar_prefetch=1,
            grid=(1,),
            in_specs=[WHOLE] * (6 + len(begun)) + [WAIT] * len(waits),
            out_specs=[WHOLE, WHOLE],
        ),
        out_shape=[VMEM((n, 2 * half), F32), VMEM((n, 128), F32)],
        input_output_aliases={7 + i: i for i in range(len(begun))},
        compiler_params=params(4),
        cost_estimate=cost(n * n * half * len(tiles), 8 * n * half),
        name="ladder",
    )(*operands, *[held(array) for array in begun], *waits)


def gathered(blocks, lines, columns):
    rows = blocks[0].shape[0] * blocks[0].shape[1]
    for j, block in enumerate(blocks):
        got = block[:, :, columns]
        lines[j * rows : (j + 1) * rows, :] = got.reshape(rows, got.shape[2])


def folded_kernel(chosen, rows, ladder, *refs):
    blocks, (out, lines) = refs[: len(chosen)], refs[-2:]
    tile = rows.shape[1] // TILES
    gathered(blocks, lines, slice(0, lines.shape[1]))
    for i in range(TILES):
        at = slice(i * tile, (i + 1) * tile)
        out[at] = ladder[at] + folded(chosen, rows, at, lines)


def folded(chosen, rows, at, lines):
    each = rows.shape[0] // 8
    total = 0
    for j, r in enumerate(chosen):
        total += dot_rows(
            rows[r * each : (r + 1) * each, at], lines[j * each : (j + 1) * each, :]
        )
    return total


def folded_call(chosen, rows, returned, ladder, *waits):
    n, h = ladder.shape
    part = n * len(chosen) // 8
    return pl.pallas_call(
        functools.partial(folded_kernel, chosen),
        in_specs=[WHOLE] * (2 + len(chosen)) + [WAIT] * len(waits),
        out_specs=WHOLE,
        out_shape=VMEM(ladder.shape, F32),
        input_output_aliases={1: 0},
        scratch_shapes=[VMEM((part, h), BF)],
        compiler_params=params(8),
        cost_estimate=cost(2 * n * part * h, 6 * n * h),
        name="folded",
    )(held(rows), held(ladder), *[held(returned[r]) for r in chosen], *waits)


def final_kernel(chosen, side, sc, rows, ladder, part, hole, *refs):
    blocks, (out, lines) = refs[: len(chosen)], refs[-2:]
    core, i = sc[0], pl.program_id(0)
    tile, half = out.shape[-2:]
    cols = slice(side * half, (side + 1) * half)

    @pl.when(i == 0)
    def _():
        gathered(blocks, lines, cols)

    at = pl.ds(pl.multiple_of(i * tile, tile), tile)
    total = ladder[at, cols] + folded(chosen, rows, at, lines)
    got = (total / (part[at, :1] - hole[pl.ds(core, 1), :])).astype(BF)
    out[...] = got.reshape(out.shape)


def final_call(chosen, side, sc, rows, returned, ladder, part, hole, *waits):
    n, h = ladder.shape
    tile, half = n // TILES, h // 2
    if side == 0:
        out_spec = pl.BlockSpec((1, tile, half), lambda i, sc: (sc[0], i, 0))
    else:
        out_spec = pl.BlockSpec((tile, half), lambda i, sc: (i, 0))
    return pl.pallas_call(
        functools.partial(final_kernel, chosen, side),
        grid_spec=pltpu.PrefetchScalarGridSpec(
            num_scalar_prefetch=1,
            grid=(TILES,),
            in_specs=[WHOLE] * (4 + len(chosen)) + [WAIT] * len(waits),
            out_specs=out_spec,
            scratch_shapes=[VMEM((n * len(chosen) // 8, half), BF)],
        ),
        out_shape=pltpu.HBM((2, n, half), BF) if side == 0 else VMEM((n, half), BF),
        compiler_params=params(6),
        cost_estimate=cost(2 * n * n * half, 6 * n * half),
        name=("final_own", "final_other")[side],
    )(
        sc,
        held(rows),
        held(ladder),
        held(part),
        held(hole),
        *[held(returned[r]) for r in chosen],
        *waits,
    )


def place_kernel(sc, given, arrived, out, sem):
    copy = pltpu.make_async_copy(arrived, out.at[1 - sc[0]], sem)
    copy.start()
    copy.wait()


def place_call(sc, out, arrived):
    return pl.pallas_call(
        place_kernel,
        grid_spec=pltpu.PrefetchScalarGridSpec(
            num_scalar_prefetch=1,
            grid=(1,),
            in_specs=[AWAY, WAIT],
            out_specs=AWAY,
            scratch_shapes=[pltpu.SemaphoreType.DMA],
        ),
        out_shape=pltpu.HBM(out.shape, BF),
        input_output_aliases={1: 0},
        compiler_params=params(1),
        cost_estimate=cost(0, 2 * out.shape[1] * out.shape[2]),
        name="place",
    )(sc, far(out), arrived)


def local(amplitudes, recouple, ladder_int, cycle_coupling, drive, eps_part, eps_hole):
    core, here = lax.axis_index("dom"), lax.axis_index("chan")
    moved = kept = 0
    for weight in (16, 4, 1):
        place = (here // weight) % 4
        high, low = place // 2, ((place + 1) // 2) % 2
        moved = 2 * moved + jnp.where(core == 0, high, low)
        kept = 2 * kept + jnp.where(core == 0, low, high)
    sc = jnp.stack([core, kept, moved]).astype(jnp.int32)

    coupling_other = swap(cycle_coupling)
    hole_other = swap(eps_hole)
    rows, amp, amp_send, drive_send = load_call(sc, recouple, amplitudes, drive)
    c0 = coupling_call(sc, cycle_coupling, coupling_other, amp_send)
    amp_send, drive_send = tie([amp_send, drive_send], c0)
    amp_other, drive_other = swap(amp_send), swap(drive_send)

    c4, c2, c1 = over(c0, kept=4), over(c0, kept=2), over(c0, kept=1)
    begun = own_call(rows, amp, c0, hole_other)
    send = other_call(rows, amp_other, begun, drive_other)

    c4, c2, c1 = tie([c4, c2, c1], send[0])
    c6, c3, c5 = over(c4, kept=2), over(c2, kept=1), over(c1, kept=4)
    blocks = [send[0]] + [None] * 7
    for r in FIRST:
        blocks[r] = over(send[r], moved=r)
    operands = [sc, ladder_int, amp, amp_other, drive, drive_other, eps_part]
    begun = ladder_call((0, 1), (), operands, send[0])
    ladder, part = ladder_call((2, 3), begun, operands, *[blocks[r] for r in FIRST])

    c6, c3, c5, *rest = tie([c6, c3, c5] + [send[r] for r in THEN], ladder)
    c7 = over(c6, kept=1)
    for r, block in zip(THEN, rest):
        blocks[r] = over(block, moved=r)

    couplings = [c0, c1, c2, c3, c4, c5, c6, c7]
    returned = [None] * 8
    for group in BACK:
        for r, block in zip(group, cycle_call([blocks[r] for r in group], couplings)):
            returned[r] = over(block, moved=r) if r else block
    ladder = folded_call(EARLY, rows, returned, ladder)
    out_other = final_call(LATE, 1, sc, rows, returned, ladder, part, hole_other)
    out = final_call(LATE, 0, sc, rows, returned, ladder, part, eps_hole, out_other)
    return place_call(sc, out, swap(out_other))


def solution(mesh):
    placed = (
        P("chan", None, "dom"),
        P("chan", None, None),
        P("chan", None, None),
        P("chan", "dom", None),
        P("chan", None, "dom"),
        P("chan", None),
        P("chan", "dom"),
    )
    return jax.shard_map(
        local, mesh=mesh, in_specs=placed, out_specs=P("chan", None, "dom"), check_vma=False
    )
```

time: 148 us -> 95.9 us (0.65)
  blocking collectives: 40.3 us -> 0 us
  matrix products: 35.9 us -> 0 us
  starting transfers between devices: 10.6 us -> 44.3 us
  Pallas kernels: 0 us -> 29.6 us
  waiting for transfers between devices: 37.4 us -> 21.3 us
  between operations: 13.4 us -> 0.44 us
  local copies, waits for them, and re-layouts: 6.7 us -> 0.04 us
  other arithmetic: 2.39 us -> 0.08 us
    ppermute x0 -> x26, starting transfers between devices: none -> 44.3 us  [the longest x21 31.9 us: over(): return lax.ppermute(array, BOTH, flips(moved, kept))]
    all_to_all x1 -> x0, blocking collectives: 40.3 us -> none  [local(): lax.all_to_all(recoupled.reshape(chan_count, peer_count, seg_rows, col_co...]
    dot_general x4 -> x0, matrix products: 35.9 us -> none  [the longest x1 13 us: local(): jnp.einsum('cqp,cqh->cph', recouple, returned, preferred_element_type=jnp...]
    pallas_call x0 -> x15, Pallas kernels: none -> 29.6 us  [the longest x2 6.2 us: final_call(): pl.pallas_call(functools.partial(final_kernel, chosen, side), grid_spec=p...]
    ppermute x0 -> x26, waiting for transfers between devices: none -> 21.3 us  [the longest x21 21.3 us: over(): return lax.ppermute(array, BOTH, flips(moved, kept))]
    reduce_scatter x1 -> x0, waiting for transfers between devices: 18.7 us -> none  [local(): lax.psum_scatter(pieces_sum, 'dom', scatter_dimension=2, tiled=True)]
    all_to_all x1 -> x0, waiting for transfers between devices: 18.7 us -> none  [local(): lax.all_to_all(cycle_term.reshape(chan_count, peer_count, seg_rows, col_c...]
    all_to_all x1 -> x0, starting transfers between devices: 10.6 us -> none  [local(): lax.all_to_all(cycle_term.reshape(chan_count, peer_count, seg_rows, col_c...]
  transfers between devices with their start and end apart: 2 -> 26, of which waited for: 2 -> 8; matrix products, arithmetic and copies ran while one was open for 7% -> 0% of each run, Pallas kernels for 0% -> 25%
where the time goes in v3:
time: 95.9 us; the launch traced here: 95.8 us
  starting transfers between devices  44.3 us (46%)
  Pallas kernels  29.6 us (31%)
  waiting for transfers between devices  21.3 us (22%)
    ppermute x21, starting transfers between devices, over(): return lax.ppermute(array, BOTH, flips(moved, kept))  31.9 us
    ppermute x21, waiting for transfers between devices, over(): return lax.ppermute(array, BOTH, flips(moved, kept))  21.3 us
    ppermute x5, starting transfers between devices, swap(): return lax.ppermute(array, 'dom', [(0, 1), (1, 0)])  12.3 us
    pallas_call x2, Pallas kernels, final_call(): pl.pallas_call(functools.partial(final_kernel, chosen, side), grid_spec=p...  6.2 us
    pallas_call x2, Pallas kernels, ladder_call(): pl.pallas_call(functools.partial(ladder_kernel, tiles), grid_spec=pltpu.P...  5.74 us
    pallas_call x1, Pallas kernels, load_call(): pl.pallas_call(load_kernel, grid_spec=pltpu.PrefetchScalarGridSpec(num_sc...  5.69 us
    pallas_call x1, Pallas kernels, folded_call(): pl.pallas_call(functools.partial(folded_kernel, chosen), in_specs=[WHOLE]...  2.57 us
    pallas_call x1, Pallas kernels, other_call(): pl.pallas_call(other_kernel, in_specs=[WHOLE] * 10 + [WAIT] * len(waits),...  2.33 us
  transfers between devices with their start and end apart: 26, of which 8 were waited for; matrix products, arithmetic and copies ran while one was open for 0% of the time, Pallas kernels for 25%

profile of v3, /device:TPU:1, one launch (start us, length us, event | category | flops | bytes accessed | tf_op | source)
XLA Modules:
  0.0 95.8 jit_solution(5196216378280115805)
XLA Ops:
  0.0 1.4 %collective-permute-start = (bf16[2,256,512]{2,1,0:T(8,128)(2,1)}, bf16[2,256,512]{2,1,0:T(8,128)(2,1)S(1)}, u32[]{:S(2)}, u32[]{:S(2)}) collective-permute-start(bf16[2,256,512]{2,1,0:T(8,128)(2,1)} %own.1), channel_id=1, source_target_pairs={{0,1},{1,0},{2,3},{3,2},{4,5},{5,4},{6,7},{7,6},{8,9},{9,8},{10,11... | collective-permute-start | bytes 1572872 | tf_op jit(solution)/shard_map/ppermute | solution.py:44
  1.4 0.1 pad_add_fusion.sc
  1.5 5.7 %load.1 = (bf16[2048,2048]{1,0:T(8,128)(2,1)S(1)}, bf16[2048,256]{1,0:T(8,128)(2,1)S(1)}, bf16[2048,256]{1,0:T(8,128)(2,1)S(1)}, bf16[2048,256]{1,0:T(8,128)(2,1)S(1)}) custom-call(s32[3]{0:T(128)S(1)} %pad_add_fusion.sc, bf16[2,2048,2048]{2,1,0:T(8,128)(2,1)} %recouple.1, bf16[2,2048,256]{2,1,0:T(8,128)(2,1)} %amplitudes.1, bf16[2,2048,256]{2,1,0:T(8,128)(2,1)} %drive.5), custom_call_target="tpu_custom_call" | custom-call | bytes 8388608 | tf_op jit(solution)/shard_map/load/pallas_call | solution.py:136
  7.2 0.0 copy-start.2
  7.2 0.0 collective-permute-done.oth
  7.2 1.6 %coupling.1.refs_2_.refs_0_.refs_5_.refs_3_ = bf16[512,512]{1,0:T(8,128)(2,1)S(1)} custom-call(s32[3]{0:T(128)S(1)} %pad_add_fusion.sc, bf16[2,256,512]{2,1,0:T(8,128)(2,1)} %own.1, bf16[2,256,512]{2,1,0:T(8,128)(2,1)S(1)} %collective-permute-done.oth, bf16[2048,256]{1,0:T(8,128)(2,1)S(1)} %get-tuple-element.52.refs_0_), custom_call_target="tpu_custom_call" | custom-call | bytes 1048576 | tf_op jit(solution)/shard_map/coupling/pallas_call | solution.py:221
  8.8 0.0 slice-start.2
  8.8 0.1 collective-permute-start.1
  8.9 0.5 collective-permute-start.2
  9.4 0.1 collective-permute-start.3
  9.5 3.8 %collective-permute-start.6 = (bf16[512,512]{1,0:T(8,128)(2,1)S(1)}, bf16[512,512]{1,0:T(8,128)(2,1)S(1)}, u32[]{:S(2)}, u32[]{:S(2)}) collective-permute-start(bf16[512,512]{1,0:T(8,128)(2,1)S(1)} %coupling.1.refs_2_.refs_0_.refs_5_.refs_3_), channel_id=1, source_target_pairs={{0,32},{2,34},{8,40},{10,42},{32,0},{34,2},{40,8},{42,10},{6,38},{... | collective-permute-start | bytes 1572872 | tf_op jit(solution)/shard_map/ppermute | solution.py:48
  13.3 2.7 %collective-permute-start.7 = (bf16[512,512]{1,0:T(8,128)(2,1)S(1)}, bf16[512,512]{1,0:T(8,128)(2,1)S(1)}, u32[]{:S(2)}, u32[]{:S(2)}) collective-permute-start(bf16[512,512]{1,0:T(8,128)(2,1)S(1)} %coupling.1.refs_2_.refs_0_.refs_5_.refs_3_), channel_id=1, source_target_pairs={{0,8},{2,10},{8,0},{10,2},{32,40},{34,42},{40,32},{42,34},{6,14},{... | collective-permute-start | bytes 1572872 | tf_op jit(solution)/shard_map/ppermute | solution.py:48
  16.1 0.0 collective-permute-done.3.refs_1_.hole
  16.1 2.5 %collective-permute-start.8 = (bf16[512,512]{1,0:T(8,128)(2,1)S(1)}, bf16[512,512]{1,0:T(8,128)(2,1)S(1)}, u32[]{:S(2)}, u32[]{:S(2)}) collective-permute-start(bf16[512,512]{1,0:T(8,128)(2,1)S(1)} %coupling.1.refs_2_.refs_0_.refs_5_.refs_3_), channel_id=1, source_target_pairs={{0,2},{2,0},{8,10},{10,8},{32,34},{34,32},{40,42},{42,40},{6,4},{4... | collective-permute-start | bytes 1572872 | tf_op jit(solution)/shard_map/ppermute | solution.py:48
  18.6 2.3 %recoupled_own.1 = (bf16[8,32,512]{2,1,0:T(8,128)(2,1)S(1)}, bf16[8,32,512]{2,1,0:T(8,128)(2,1)S(1)}, bf16[8,32,512]{2,1,0:T(8,128)(2,1)S(1)}, bf16[8,32,512]{2,...) custom-call(bf16[2048,2048]{1,0:T(8,128)(2,1)S(1)} %get-tuple-elemen, ...), custom_call_target="tpu_custom_call" | custom-call | flops 2147483648 | bytes 8388608 | tf_op jit(solution)/shard_map/recoupled_own/pallas_call | solution.py:170
  20.9 0.0 collective-permute-done.1.amp.amp_other
  20.9 0.0 collective-permute-done.2.refs_8_.drive_other
  20.9 0.0 slice-start.3
  20.9 0.0 copy-start
  20.9 0.0 copy-start.1
  20.9 2.3 %recoupled_other.1 = (bf16[8,32,512]{2,1,0:T(8,128)(2,1)S(1)}, bf16[8,32,512]{2,1,0:T(8,128)(2,1)S(1)}, bf16[8,32,512]{2,1,0:T(8,128)(2,1)S(1)}, bf16[8,32,512]{...) custom-call(bf16[2048,2048]{1,0:T(8,128)(2,1)S(1)} %get-tuple-elemen, ...), custom_call_target="tpu_custom_call", output_to_operand_aliasing={{0}: (2, {}), {1}: (3, {}), {2}: (4, {}), {3}: (5, {}), {4}... | custom-call | flops 2147483648 | bytes 2097152 | tf_op jit(solution)/shard_map/recoupled_other/pallas_call | solution.py:192
  23.3 0.0 collective-permute-done.6.refs_0_
  23.3 2.0 %collective-permute-done.8.refs_2_ = bf16[512,512]{1,0:T(8,128)(2,1)S(1)} collective-permute-done((bf16[512,512]{1,0:T(8,128)(2,1)S(1)}, bf16[512,512]{1,0:T(8,128)(2,1)S(1)}, u32[]{:S(2)}, u32[]{:S(2)}) %collective-permute-start.8) | collective-permute-done | bytes 524320 | tf_op jit(solution)/shard_map/ppermute | solution.py:48
  25.3 0.0 collective-permute-start.9
  25.3 2.5 %collective-permute-start.10 = (bf16[512,512]{1,0:T(8,128)(2,1)S(1)}, bf16[512,512]{1,0:T(8,128)(2,1)S(1)}, u32[]{:S(2)}, u32[]{:S(2)}) collective-permute-start(bf16[512,512]{1,0:T(8,128)(2,1)S(1)} %get-tuple-element.71.refs_7_.refs_5_), channel_id=1, source_target_pairs={{0,2},{2,0},{8,10},{10,8},{32,34},{34,32},{40,42},{42,40},{6,4},{4... | collective-permute-start | bytes 1572872 | tf_op jit(solution)/shard_map/ppermute | solution.py:48
  27.8 3.5 %collective-permute-start.11 = (bf16[512,512]{1,0:T(8,128)(2,1)S(1)}, bf16[512,512]{1,0:T(8,128)(2,1)S(1)}, u32[]{:S(2)}, u32[]{:S(2)}) collective-permute-start(bf16[512,512]{1,0:T(8,128)(2,1)S(1)} %get-tuple-element.72.refs_6_.refs_4_), channel_id=1, source_target_pairs={{0,32},{2,34},{8,40},{10,42},{32,0},{34,2},{40,8},{42,10},{6,38},{... | collective-permute-start | bytes 1572872 | tf_op jit(solution)/shard_map/ppermute | solution.py:48
  31.4 0.3 collective-permute-start.5
  31.7 2.9 %ladder.2 = (f32[2048,512]{1,0:T(8,128)S(1)}, f32[2048,128]{1,0:T(8,128)S(1)}) custom-call(s32[3]{0:T(128)S(1)} %pad_add_fusion.sc, bf16[2,2048,2048]{2,1,0:T(8,128)(2,1)S(1)} %bitcast.4, bf16[2048,256]{1,0:T(8,128)(2,1)S(1)} %get-tuple-element.51.amp, bf16[2048,256]{1,0:T(8,128)(2,1)S(1)} %collective-permute-done.1.amp.amp_other, ...), custom_call_target="tpu_custom_call" | custom-call | flops 2147483648 | bytes 4194304 | tf_op jit(solution)/shard_map/ladder/pallas_call | solution.py:275
  34.5 4.1 %collective-permute-done.4.refs_2_.refs_1_ = bf16[8,32,512]{2,1,0:T(8,128)(2,1)S(1)} collective-permute-done((bf16[8,32,512]{2,1,0:T(8,128)(2,1)S(1)}, bf16[8,32,512]{2,1,0:T(8,128)(2,1)S(1)}, u32[]{:S(2)}, u32[]{:S(2)}) %collective-permute-start.4) | collective-permute-done | bytes 262176 | tf_op jit(solution)/shard_map/ppermute | solution.py:48
  38.7 0.0 collective-permute-done.5.refs_3_.refs_4_
  38.7 2.9 %ladder.3 = (f32[2048,512]{1,0:T(8,128)S(1)}, f32[2048,128]{1,0:T(8,128)S(1)}) custom-call(s32[3]{0:T(128)S(1)} %pad_add_fusion.sc, bf16[2,2048,2048]{2,1,0:T(8,128)(2,1)S(1)} %bitcast.4, bf16[2048,256]{1,0:T(8,128)(2,1)S(1)} %get-tuple-element.51.amp, ...), custom_call_target="tpu_custom_call", output_to_operand_aliasing={{0}: (7, {}), {1}: (8, {})} | custom-call | flops 2147483648 | bytes 4194304 | tf_op jit(solution)/shard_map/ladder/pallas_call | solution.py:275
  41.5 0.0 collective-permute-done.9.refs_0_
  41.6 0.0 collective-permute-done.10.refs_1_
  41.6 2.3 %collective-permute-start.14 = (bf16[512,512]{1,0:T(8,128)(2,1)S(1)}, bf16[512,512]{1,0:T(8,128)(2,1)S(1)}, u32[]{:S(2)}, u32[]{:S(2)}) collective-permute-start(bf16[512,512]{1,0:T(8,128)(2,1)S(1)} %get-tuple-element.82.refs_11_.refs_9_), channel_id=1, source_target_pairs={{0,2},{2,0},{8,10},{10,8},{32,34},{34,32},{40,42},{42,40},{6,4},{4... | collective-permute-start | bytes 1572872 | tf_op jit(solution)/shard_map/ppermute | solution.py:48
  43.9 0.1 collective-permute-start.12
  44.0 2.7 %collective-permute-start.13 = (bf16[8,32,512]{2,1,0:T(8,128)(2,1)S(1)}, bf16[8,32,512]{2,1,0:T(8,128)(2,1)S(1)}, u32[]{:S(2)}, u32[]{:S(2)}) collective-permute-start(bf16[8,32,512]{2,1,0:T(8,128)(2,1)S(1)} %get-tuple-element.79), channel_id=1, source_target_pairs={{0,102},{2,100},{8,110},{10,108},{32,70},{34,68},{40,78},{42,76},{... | collective-permute-start | bytes 786440 | tf_op jit(solution)/shard_map/ppermute | solution.py:48
  46.6 0.8 collective-permute-start.19
  47.5 0.5 collective-permute-start.20
  47.9 5.0 %collective-permute-done.12.refs_2_ = bf16[8,32,512]{2,1,0:T(8,128)(2,1)S(1)} collective-permute-done((bf16[8,32,512]{2,1,0:T(8,128)(2,1)S(1)}, bf16[8,32,512]{2,1,0:T(8,128)(2,1)S(1)}, u32[]{:S(2)}, u32[]{:S(2)}) %collective-permute-start.12) | collective-permute-done | bytes 262176 | tf_op jit(solution)/shard_map/ppermute | solution.py:48
  53.0 1.8 %collective-permute-start.21 = (bf16[8,32,512]{2,1,0:T(8,128)(2,1)S(1)}, bf16[8,32,512]{2,1,0:T(8,128)(2,1)S(1)}, u32[]{:S(2)}, u32[]{:S(2)}) collective-permute-start(bf16[8,32,512]{2,1,0:T(8,128)(2,1)S(1)} %get-tuple-element.91), channel_id=1, source_target_pairs={{0,96},{2,98},{8,104},{10,106},{32,64},{34,66},{40,72},{42,74},{6,... | collective-permute-start | bytes 786440 | tf_op jit(solution)/shard_map/ppermute | solution.py:48
  54.7 4.0 %collective-permute-done.13.refs_3_ = bf16[8,32,512]{2,1,0:T(8,128)(2,1)S(1)} collective-permute-done((bf16[8,32,512]{2,1,0:T(8,128)(2,1)S(1)}, bf16[8,32,512]{2,1,0:T(8,128)(2,1)S(1)}, u32[]{:S(2)}, u32[]{:S(2)}) %collective-permute-start.13) | collective-permute-done | bytes 262176 | tf_op jit(solution)/shard_map/ppermute | solution.py:48
  58.8 0.0 collective-permute-done.14.refs_12_.refs_10_
  58.8 0.9 cycle.2
  59.6 0.9 collective-permute-start.15
  60.5 0.8 collective-permute-start.16
  61.4 0.0 collective-permute-done.19.refs_0_
  61.4 2.0 %collective-permute-start.17 = (bf16[8,32,512]{2,1,0:T(8,128)(2,1)S(1)}, bf16[8,32,512]{2,1,0:T(8,128)(2,1)S(1)}, u32[]{:S(2)}, u32[]{:S(2)}) collective-permute-start(bf16[8,32,512]{2,1,0:T(8,128)(2,1)S(1)} %get-tuple-element.86), channel_id=1, source_target_pairs={{0,102},{2,100},{8,110},{10,108},{32,70},{34,68},{40,78},{42,76},{... | collective-permute-start | bytes 786440 | tf_op jit(solution)/shard_map/ppermute | solution.py:48
  63.4 1.1 %collective-permute-start.18 = (bf16[8,32,512]{2,1,0:T(8,128)(2,1)S(1)}, bf16[8,32,512]{2,1,0:T(8,128)(2,1)S(1)}, u32[]{:S(2)}, u32[]{:S(2)}) collective-permute-start(bf16[8,32,512]{2,1,0:T(8,128)(2,1)S(1)} %get-tuple-element.88), channel_id=1, source_target_pairs={{0,6},{2,4},{8,14},{10,12},{32,38},{34,36},{40,46},{42,44},{6,0},{... | collective-permute-start | bytes 786440 | tf_op jit(solution)/shard_map/ppermute | solution.py:48
  64.5 0.0 collective-permute-done.21.refs_2_
  64.5 0.8 cycle.3
  65.3 0.8 collective-permute-start.22
  66.1 0.6 collective-permute-done.15.refs_1_
  66.7 0.9 collective-permute-start.23
  67.6 0.4 collective-permute-done.16.refs_2_
  68.0 1.9 %collective-permute-start.24 = (bf16[8,32,512]{2,1,0:T(8,128)(2,1)S(1)}, bf16[8,32,512]{2,1,0:T(8,128)(2,1)S(1)}, u32[]{:S(2)}, u32[]{:S(2)}) collective-permute-start(bf16[8,32,512]{2,1,0:T(8,128)(2,1)S(1)} %get-tuple-element.94), channel_id=1, source_target_pairs={{0,96},{2,98},{8,104},{10,106},{32,64},{34,66},{40,72},{42,74},{6,... | collective-permute-start | bytes 786440 | tf_op jit(solution)/shard_map/ppermute | solution.py:48
  69.9 4.7 %collective-permute-done.17.refs_3_ = bf16[8,32,512]{2,1,0:T(8,128)(2,1)S(1)} collective-permute-done((bf16[8,32,512]{2,1,0:T(8,128)(2,1)S(1)}, bf16[8,32,512]{2,1,0:T(8,128)(2,1)S(1)}, u32[]{:S(2)}, u32[]{:S(2)}) %collective-permute-start.17) | collective-permute-done | bytes 262176 | tf_op jit(solution)/shard_map/ppermute | solution.py:48
  74.6 2.6 %folded.1.ladder = f32[2048,512]{1,0:T(8,128)S(1)} custom-call(bf16[2048,2048]{1,0:T(8,128)(2,1)S(1)} %get-tuple-element.50.rows, f32[2048,512]{1,0:T(8,128)S(1)} %get-tuple-element.69.refs_8_.ladder, bf16[8,32,512]{2,1,0:T(8,128)(2,1)S(1)} %get-tuple-element.83.refs_0_, ...), custom_call_target="tpu_custom_call", output_to_operand_aliasing={{}: (1, {})} | custom-call | flops 2147483648 | bytes 6291456 | tf_op jit(solution)/shard_map/folded/pallas_call | solution.py:320
  77.2 0.0 collective-permute-done.23.refs_2_
  77.2 0.4 collective-permute-done.24.refs_3_
  77.6 2.6 %final_other.1.refs_4_ = bf16[2048,256]{1,0:T(8,128)(2,1)S(1)} custom-call(s32[3]{0:T(128)S(1)} %pad_add_fusion.sc, bf16[2048,2048]{1,0:T(8,128)(2,1)S(1)} %get-tuple-element.50.rows, f32[2048,512]{1,0:T(8,128)S(1)} %folded.1.ladder, f32[2048,128]{1,0:T(8,128)S(1)} %get-tuple-element.87.part, f32[2,256]{1,0:T(2,128)S(1)} %collective-permute-done.3.refs_1_.hole, ...), custom_call_target="tpu_custom_call" | custom-call | flops 2147483648 | bytes 3145728 | tf_op jit(solution)/shard_map/final_other/pallas_call | solution.py:356
  80.3 10.2 %collective-permute-start.25 = (bf16[2048,256]{1,0:T(8,128)(2,1)S(1)}, bf16[2048,256]{1,0:T(8,128)(2,1)S(1)}, u32[]{:S(2)}, u32[]{:S(2)}) collective-permute-start(bf16[2048,256]{1,0:T(8,128)(2,1)S(1)} %final_other.1.refs_4_), channel_id=1, source_target_pairs={{0,1},{1,0},{2,3},{3,2},{4,5},{5,4},{6,7},{7,6},{8,9},{9,8},{10,11... | collective-permute-start | bytes 3145736 | tf_op jit(solution)/shard_map/ppermute | solution.py:44
  90.5 3.6 %final_own.1.given = bf16[2,2048,256]{2,1,0:T(8,128)(2,1)} custom-call(s32[3]{0:T(128)S(1)} %pad_add_fusion.sc, bf16[2048,2048]{1,0:T(8,128)(2,1)S(1)} %get-tuple-element.50.rows, f32[2048,512]{1,0:T(8,128)S(1)} %folded.1.ladder, f32[2048,128]{1,0:T(8,128)S(1)} %get-tuple-element.87.part, f32[2,256]{1,0:T(2,128)S(1)} %copy-done.2, ...), custom_call_target="tpu_custom_call" | custom-call | flops 2147483648 | bytes 3145728 | tf_op jit(solution)/shard_map/final_own/pallas_call | solution.py:356
  94.1 0.0 collective-permute-done.25.arrived
  94.1 1.5 %place.1 = bf16[2,2048,256]{2,1,0:T(8,128)(2,1)} custom-call(s32[3]{0:T(128)S(1)} %pad_add_fusion.sc, bf16[2,2048,256]{2,1,0:T(8,128)(2,1)} %final_own.1.given, bf16[2048,256]{1,0:T(8,128)(2,1)S(1)} %collective-permute-done.25.arrived), custom_call_target="tpu_custom_call", output_to_operand_aliasing={{}: (1, {})} | custom-call | bytes 1048576 | tf_op jit(solution)/shard_map/place/pallas_call | solution.py:387
  (19 shorter events, 0.0 us)
Async XLA Ops:
  0.0 7.2 %collective-permute-start = (bf16[2,256,512]{2,1,0:T(8,128)(2,1)}, bf16[2,256,512]{2,1,0:T(8,128)(2,1)S(1)}, u32[]{:S(2)}, u32[]{:S(2)}) collective-permute-start(bf16[2,256,512]{2,1,0:T(8,128)(2,1)} %own.1), channel_id=1, source_target_pairs={{0,1},{1,0},{2,3},{3,2},{4,5},{5,4},{6,7},{7,6},{8,9},{9,8},{10,11... | collective-permute-start | bytes 1572872 | tf_op jit(solution)/shard_map/ppermute | solution.py:44
  1.5 30.1 %slice-start = ((s8[16777216]{0:T(1024)(128)(4,1)}), s8[4194304]{0:T(1024)(128)(4,1)S(1)}, s32[]{:S(2)}) async-start(s8[16777216]{0:T(1024)(128)(4,1)} %bitcast.3), calls=%async_computation | async-start | bytes 8388608
  1.5 30.1 %slice-start.1 = ((s8[16777216]{0:T(1024)(128)(4,1)}), s8[4194304]{0:T(1024)(128)(4,1)S(1)}, s32[]{:S(2)}) async-start(s8[16777216]{0:T(1024)(128)(4,1)} %bitcast.3), calls=%async_computation.1 | async-start | bytes 8388608
  7.2 2.2 %copy-start.2 = (f32[2,256]{1,0:T(2,128)S(1)}, f32[2,256]{1,0:T(2,128)}, u32[]{:S(2)}) copy-start(f32[2,256]{1,0:T(2,128)} %hole.1) | copy-start | bytes 6148
  8.8 22.8 %slice-start.2 = ((s8[16777216]{0:T(1024)(128)(4,1)}), s8[4194304]{0:T(1024)(128)(4,1)S(1)}, s32[]{:S(2)}) async-start(s8[16777216]{0:T(1024)(128)(4,1)} %bitcast.3), calls=%async_computation.2 | async-start | bytes 8388608
  8.8 12.1 %collective-permute-start.1 = (bf16[2048,256]{1,0:T(8,128)(2,1)S(1)}, bf16[2048,256]{1,0:T(8,128)(2,1)S(1)}, u32[]{:S(2)}, u32[]{:S(2)}) collective-permute-start(bf16[2048,256]{1,0:T(8,128)(2,1)S(1)} %get-tuple-element.54), channel_id=1, source_target_pairs={{0,1},{1,0},{2,3},{3,2},{4,5},{5,4},{6,7},{7,6},{8,9},{9,8},{10,11... | collective-permute-start | bytes 3145736 | tf_op jit(solution)/shard_map/ppermute | solution.py:44
  8.9 12.0 %collective-permute-start.2 = (bf16[2048,256]{1,0:T(8,128)(2,1)S(1)}, bf16[2048,256]{1,0:T(8,128)(2,1)S(1)}, u32[]{:S(2)}, u32[]{:S(2)}) collective-permute-start(bf16[2048,256]{1,0:T(8,128)(2,1)S(1)} %get-tuple-element.55), channel_id=1, source_target_pairs={{0,1},{1,0},{2,3},{3,2},{4,5},{5,4},{6,7},{7,6},{8,9},{9,8},{10,11... | collective-permute-start | bytes 3145736 | tf_op jit(solution)/shard_map/ppermute | solution.py:44
  9.4 6.7 %collective-permute-start.3 = (f32[2,256]{1,0:T(2,128)S(1)}, f32[2,256]{1,0:T(2,128)S(1)}, u32[]{:S(2)}, u32[]{:S(2)}) collective-permute-start(f32[2,256]{1,0:T(2,128)S(1)} %copy-done.2), channel_id=1, source_target_pairs={{0,1},{1,0},{2,3},{3,2},{4,5},{5,4},{6,7},{7,6},{8,9},{9,8},{10,11... | collective-permute-start | bytes 6152 | tf_op jit(solution)/shard_map/ppermute | solution.py:44
  9.5 13.8 %collective-permute-start.6 = (bf16[512,512]{1,0:T(8,128)(2,1)S(1)}, bf16[512,512]{1,0:T(8,128)(2,1)S(1)}, u32[]{:S(2)}, u32[]{:S(2)}) collective-permute-start(bf16[512,512]{1,0:T(8,128)(2,1)S(1)} %coupling.1.refs_2_.refs_0_.refs_5_.refs_3_), channel_id=1, source_target_pairs={{0,32},{2,34},{8,40},{10,42},{32,0},{34,2},{40,8},{42,10},{6,38},{... | collective-permute-start | bytes 1572872 | tf_op jit(solution)/shard_map/ppermute | solution.py:48
  13.3 10.0 %collective-permute-start.7 = (bf16[512,512]{1,0:T(8,128)(2,1)S(1)}, bf16[512,512]{1,0:T(8,128)(2,1)S(1)}, u32[]{:S(2)}, u32[]{:S(2)}) collective-permute-start(bf16[512,512]{1,0:T(8,128)(2,1)S(1)} %coupling.1.refs_2_.refs_0_.refs_5_.refs_3_), channel_id=1, source_target_pairs={{0,8},{2,10},{8,0},{10,2},{32,40},{34,42},{40,32},{42,34},{6,14},{... | collective-permute-start | bytes 1572872 | tf_op jit(solution)/shard_map/ppermute | solution.py:48
  16.1 9.2 %collective-permute-start.8 = (bf16[512,512]{1,0:T(8,128)(2,1)S(1)}, bf16[512,512]{1,0:T(8,128)(2,1)S(1)}, u32[]{:S(2)}, u32[]{:S(2)}) collective-permute-start(bf16[512,512]{1,0:T(8,128)(2,1)S(1)} %coupling.1.refs_2_.refs_0_.refs_5_.refs_3_), channel_id=1, source_target_pairs={{0,2},{2,0},{8,10},{10,8},{32,34},{34,32},{40,42},{42,40},{6,4},{4... | collective-permute-start | bytes 1572872 | tf_op jit(solution)/shard_map/ppermute | solution.py:48
  20.9 10.7 %slice-start.3 = ((s8[16777216]{0:T(1024)(128)(4,1)}), s8[4194304]{0:T(1024)(128)(4,1)S(1)}, s32[]{:S(2)}) async-start(s8[16777216]{0:T(1024)(128)(4,1)} %bitcast.3), calls=%async_computation.3 | async-start | bytes 8388608
  20.9 10.7 %copy-start = (bf16[2,2048,256]{2,1,0:T(8,128)(2,1)S(1)}, bf16[2,2048,256]{2,1,0:T(8,128)(2,1)}, u32[]{:S(2)}) copy-start(bf16[2,2048,256]{2,1,0:T(8,128)(2,1)} %drive.5) | copy-start | bytes 6291460
  20.9 10.7 %copy-start.1 = (f32[2,2048]{1,0:T(2,128)S(1)}, f32[2,2048]{1,0:T(2,128)}, u32[]{:S(2)}) copy-start(f32[2,2048]{1,0:T(2,128)} %part.3) | copy-start | bytes 49156
  25.3 16.2 %collective-permute-start.9 = (bf16[512,512]{1,0:T(8,128)(2,1)S(1)}, bf16[512,512]{1,0:T(8,128)(2,1)S(1)}, u32[]{:S(2)}, u32[]{:S(2)}) collective-permute-start(bf16[512,512]{1,0:T(8,128)(2,1)S(1)} %get-tuple-element.70.refs_9_.refs_7_), channel_id=1, source_target_pairs={{0,8},{2,10},{8,0},{10,2},{32,40},{34,42},{40,32},{42,34},{6,14},{... | collective-permute-start | bytes 1572872 | tf_op jit(solution)/shard_map/ppermute | solution.py:48
  25.3 16.2 %collective-permute-start.10 = (bf16[512,512]{1,0:T(8,128)(2,1)S(1)}, bf16[512,512]{1,0:T(8,128)(2,1)S(1)}, u32[]{:S(2)}, u32[]{:S(2)}) collective-permute-start(bf16[512,512]{1,0:T(8,128)(2,1)S(1)} %get-tuple-element.71.refs_7_.refs_5_), channel_id=1, source_target_pairs={{0,2},{2,0},{8,10},{10,8},{32,34},{34,32},{40,42},{42,40},{6,4},{4... | collective-permute-start | bytes 1572872 | tf_op jit(solution)/shard_map/ppermute | solution.py:48
  27.8 13.8 %collective-permute-start.11 = (bf16[512,512]{1,0:T(8,128)(2,1)S(1)}, bf16[512,512]{1,0:T(8,128)(2,1)S(1)}, u32[]{:S(2)}, u32[]{:S(2)}) collective-permute-start(bf16[512,512]{1,0:T(8,128)(2,1)S(1)} %get-tuple-element.72.refs_6_.refs_4_), channel_id=1, source_target_pairs={{0,32},{2,34},{8,40},{10,42},{32,0},{34,2},{40,8},{42,10},{6,38},{... | collective-permute-start | bytes 1572872 | tf_op jit(solution)/shard_map/ppermute | solution.py:48
  31.4 7.3 %collective-permute-start.4 = (bf16[8,32,512]{2,1,0:T(8,128)(2,1)S(1)}, bf16[8,32,512]{2,1,0:T(8,128)(2,1)S(1)}, u32[]{:S(2)}, u32[]{:S(2)}) collective-permute-start(bf16[8,32,512]{2,1,0:T(8,128)(2,1)S(1)} %get-tuple-element.67), channel_id=1, source_target_pairs={{0,126},{2,124},{8,118},{10,116},{32,94},{34,92},{40,86},{42,84},{... | collective-permute-start | bytes 786440 | tf_op jit(solution)/shard_map/ppermute | solution.py:48
  31.4 7.3 %collective-permute-start.5 = (bf16[8,32,512]{2,1,0:T(8,128)(2,1)S(1)}, bf16[8,32,512]{2,1,0:T(8,128)(2,1)S(1)}, u32[]{:S(2)}, u32[]{:S(2)}) collective-permute-start(bf16[8,32,512]{2,1,0:T(8,128)(2,1)S(1)} %get-tuple-element.68), channel_id=1, source_target_pairs={{0,6},{2,4},{8,14},{10,12},{32,38},{34,36},{40,46},{42,44},{6,0},{... | collective-permute-start | bytes 786440 | tf_op jit(solution)/shard_map/ppermute | solution.py:48
  41.6 17.2 %collective-permute-start.14 = (bf16[512,512]{1,0:T(8,128)(2,1)S(1)}, bf16[512,512]{1,0:T(8,128)(2,1)S(1)}, u32[]{:S(2)}, u32[]{:S(2)}) collective-permute-start(bf16[512,512]{1,0:T(8,128)(2,1)S(1)} %get-tuple-element.82.refs_11_.refs_9_), channel_id=1, source_target_pairs={{0,2},{2,0},{8,10},{10,8},{32,34},{34,32},{40,42},{42,40},{6,4},{4... | collective-permute-start | bytes 1572872 | tf_op jit(solution)/shard_map/ppermute | solution.py:48
  43.9 9.1 %collective-permute-start.12 = (bf16[8,32,512]{2,1,0:T(8,128)(2,1)S(1)}, bf16[8,32,512]{2,1,0:T(8,128)(2,1)S(1)}, u32[]{:S(2)}, u32[]{:S(2)}) collective-permute-start(bf16[8,32,512]{2,1,0:T(8,128)(2,1)S(1)} %get-tuple-element.78), channel_id=1, source_target_pairs={{0,30},{2,28},{8,22},{10,20},{32,62},{34,60},{40,54},{42,52},{6,24... | collective-permute-start | bytes 786440 | tf_op jit(solution)/shard_map/ppermute | solution.py:48
  44.0 14.8 %collective-permute-start.13 = (bf16[8,32,512]{2,1,0:T(8,128)(2,1)S(1)}, bf16[8,32,512]{2,1,0:T(8,128)(2,1)S(1)}, u32[]{:S(2)}, u32[]{:S(2)}) collective-permute-start(bf16[8,32,512]{2,1,0:T(8,128)(2,1)S(1)} %get-tuple-element.79), channel_id=1, source_target_pairs={{0,102},{2,100},{8,110},{10,108},{32,70},{34,68},{40,78},{42,76},{... | collective-permute-start | bytes 786440 | tf_op jit(solution)/shard_map/ppermute | solution.py:48
  46.6 14.7 %collective-permute-start.19 = (bf16[8,32,512]{2,1,0:T(8,128)(2,1)S(1)}, bf16[8,32,512]{2,1,0:T(8,128)(2,1)S(1)}, u32[]{:S(2)}, u32[]{:S(2)}) collective-permute-start(bf16[8,32,512]{2,1,0:T(8,128)(2,1)S(1)} %get-tuple-element.89), channel_id=1, source_target_pairs={{0,120},{2,122},{8,112},{10,114},{32,88},{34,90},{40,80},{42,82},{... | collective-permute-start | bytes 786440 | tf_op jit(solution)/shard_map/ppermute | solution.py:48
  47.5 15.9 %collective-permute-start.20 = (bf16[8,32,512]{2,1,0:T(8,128)(2,1)S(1)}, bf16[8,32,512]{2,1,0:T(8,128)(2,1)S(1)}, u32[]{:S(2)}, u32[]{:S(2)}) collective-permute-start(bf16[8,32,512]{2,1,0:T(8,128)(2,1)S(1)} %get-tuple-element.90), channel_id=1, source_target_pairs={{0,24},{2,26},{8,16},{10,18},{32,56},{34,58},{40,48},{42,50},{6,30... | collective-permute-start | bytes 786440 | tf_op jit(solution)/shard_map/ppermute | solution.py:48
  53.0 11.5 %collective-permute-start.21 = (bf16[8,32,512]{2,1,0:T(8,128)(2,1)S(1)}, bf16[8,32,512]{2,1,0:T(8,128)(2,1)S(1)}, u32[]{:S(2)}, u32[]{:S(2)}) collective-permute-start(bf16[8,32,512]{2,1,0:T(8,128)(2,1)S(1)} %get-tuple-element.91), channel_id=1, source_target_pairs={{0,96},{2,98},{8,104},{10,106},{32,64},{34,66},{40,72},{42,74},{6,... | collective-permute-start | bytes 786440 | tf_op jit(solution)/shard_map/ppermute | solution.py:48
  59.6 7.1 %collective-permute-start.15 = (bf16[8,32,512]{2,1,0:T(8,128)(2,1)S(1)}, bf16[8,32,512]{2,1,0:T(8,128)(2,1)S(1)}, u32[]{:S(2)}, u32[]{:S(2)}) collective-permute-start(bf16[8,32,512]{2,1,0:T(8,128)(2,1)S(1)} %get-tuple-element.84), channel_id=1, source_target_pairs={{0,126},{2,124},{8,118},{10,116},{32,94},{34,92},{40,86},{42,84},{... | collective-permute-start | bytes 786440 | tf_op jit(solution)/shard_map/ppermute | solution.py:48
  60.5 7.5 %collective-permute-start.16 = (bf16[8,32,512]{2,1,0:T(8,128)(2,1)S(1)}, bf16[8,32,512]{2,1,0:T(8,128)(2,1)S(1)}, u32[]{:S(2)}, u32[]{:S(2)}) collective-permute-start(bf16[8,32,512]{2,1,0:T(8,128)(2,1)S(1)} %get-tuple-element.85), channel_id=1, source_target_pairs={{0,30},{2,28},{8,22},{10,20},{32,62},{34,60},{40,54},{42,52},{6,24... | collective-permute-start | bytes 786440 | tf_op jit(solution)/shard_map/ppermute | solution.py:48
  61.4 13.3 %collective-permute-start.17 = (bf16[8,32,512]{2,1,0:T(8,128)(2,1)S(1)}, bf16[8,32,512]{2,1,0:T(8,128)(2,1)S(1)}, u32[]{:S(2)}, u32[]{:S(2)}) collective-permute-start(bf16[8,32,512]{2,1,0:T(8,128)(2,1)S(1)} %get-tuple-element.86), channel_id=1, source_target_pairs={{0,102},{2,100},{8,110},{10,108},{32,70},{34,68},{40,78},{42,76},{... | collective-permute-start | bytes 786440 | tf_op jit(solution)/shard_map/ppermute | solution.py:48
  63.4 13.8 %collective-permute-start.18 = (bf16[8,32,512]{2,1,0:T(8,128)(2,1)S(1)}, bf16[8,32,512]{2,1,0:T(8,128)(2,1)S(1)}, u32[]{:S(2)}, u32[]{:S(2)}) collective-permute-start(bf16[8,32,512]{2,1,0:T(8,128)(2,1)S(1)} %get-tuple-element.88), channel_id=1, source_target_pairs={{0,6},{2,4},{8,14},{10,12},{32,38},{34,36},{40,46},{42,44},{6,0},{... | collective-permute-start | bytes 786440 | tf_op jit(solution)/shard_map/ppermute | solution.py:48
  65.3 11.9 %collective-permute-start.22 = (bf16[8,32,512]{2,1,0:T(8,128)(2,1)S(1)}, bf16[8,32,512]{2,1,0:T(8,128)(2,1)S(1)}, u32[]{:S(2)}, u32[]{:S(2)}) collective-permute-start(bf16[8,32,512]{2,1,0:T(8,128)(2,1)S(1)} %get-tuple-element.92), channel_id=1, source_target_pairs={{0,120},{2,122},{8,112},{10,114},{32,88},{34,90},{40,80},{42,82},{... | collective-permute-start | bytes 786440 | tf_op jit(solution)/shard_map/ppermute | solution.py:48
  66.7 10.5 %collective-permute-start.23 = (bf16[8,32,512]{2,1,0:T(8,128)(2,1)S(1)}, bf16[8,32,512]{2,1,0:T(8,128)(2,1)S(1)}, u32[]{:S(2)}, u32[]{:S(2)}) collective-permute-start(bf16[8,32,512]{2,1,0:T(8,128)(2,1)S(1)} %get-tuple-element.93), channel_id=1, source_target_pairs={{0,24},{2,26},{8,16},{10,18},{32,56},{34,58},{40,48},{42,50},{6,30... | collective-permute-start | bytes 786440 | tf_op jit(solution)/shard_map/ppermute | solution.py:48
  68.0 9.6 %collective-permute-start.24 = (bf16[8,32,512]{2,1,0:T(8,128)(2,1)S(1)}, bf16[8,32,512]{2,1,0:T(8,128)(2,1)S(1)}, u32[]{:S(2)}, u32[]{:S(2)}) collective-permute-start(bf16[8,32,512]{2,1,0:T(8,128)(2,1)S(1)} %get-tuple-element.94), channel_id=1, source_target_pairs={{0,96},{2,98},{8,104},{10,106},{32,64},{34,66},{40,72},{42,74},{6,... | collective-permute-start | bytes 786440 | tf_op jit(solution)/shard_map/ppermute | solution.py:48
  80.3 13.8 %collective-permute-start.25 = (bf16[2048,256]{1,0:T(8,128)(2,1)S(1)}, bf16[2048,256]{1,0:T(8,128)(2,1)S(1)}, u32[]{:S(2)}, u32[]{:S(2)}) collective-permute-start(bf16[2048,256]{1,0:T(8,128)(2,1)S(1)} %final_other.1.refs_4_), channel_id=1, source_target_pairs={{0,1},{1,0},{2,3},{3,2},{4,5},{5,4},{6,7},{7,6},{8,9},{9,8},{10,11... | collective-permute-start | bytes 3145736 | tf_op jit(solution)/shard_map/ppermute | solution.py:44

commit v4 on v3

--- a/solution.py
+++ b/solution.py
@@ -18,8 +18,11 @@
     return (PLACE[bits[0]] * 4 + PLACE[bits[1]]) * 4 + PLACE[bits[2]]
 
 
+HIGH = (1, 0, 1)
+
+
 def bits_of(core, moved, kept):
-    return [(m, k) if core == 0 else (k, m) for m, k in zip(moved, kept)]
+    return [(m, k) if first ^ core else (k, m) for first, m, k in zip(HIGH, moved, kept)]
 
 
 THREE = list(itertools.product((0, 1), repeat=3))
@@ -50,9 +53,9 @@
 
 def segment(core, moved, kept):
     at = 0
-    for shift in (2, 1, 0):
+    for first, shift in zip(HIGH, (2, 1, 0)):
         m, k = (moved >> shift) & 1, (kept >> shift) & 1
-        at = at * 4 + 2 * jnp.where(core == 0, m, k) + (m ^ k)
+        at = at * 4 + 2 * jnp.where(core == 1 - first, m, k) + (m ^ k)
     return at
 
 
@@ -84,9 +87,10 @@
 AWAY = pl.BlockSpec(memory_space=pltpu.HBM)
 WAIT = pl.BlockSpec(memory_space=pl.ANY)
 TILES = 4
-FIRST, THEN = (7, 1), (3, 5, 6, 2, 4)
-BACK = (0, 7, 3, 5, 1), (6, 2, 4)
-EARLY, LATE = (0, 7, 3, 5), (1, 6, 2, 4)
+FIRST, THEN = (1, 3), (7, 5, 6, 2, 4)
+BACK = (0, 7, 5, 3, 1), (6, 2, 4)
+ORDER = BACK[0] + BACK[1]
+EARLY, LATE = (range(5), range(5, 7)), range(7, 8)
 
 
 def tie_kernel(*refs):
@@ -107,20 +111,40 @@
     )(*arrays, *waits)
 
 
-def load_kernel(sc, recouple, amplitudes, drive, rows, amp, amp_send, drive_send, sems):
+def cut_kernel(sc, amplitudes, drive, pair, sems):
+    copies = [
+        pltpu.make_async_copy(whole.at[1 - sc[0]], pair.at[i], sems.at[i])
+        for i, whole in enumerate((amplitudes, drive))
+    ]
+    for copy in copies:
+        copy.start()
+    for copy in copies:
+        copy.wait()
+
+
+def cut_call(sc, amplitudes, drive):
+    return pl.pallas_call(
+        cut_kernel,
+        grid_spec=pltpu.PrefetchScalarGridSpec(
+            num_scalar_prefetch=1,
+            grid=(1,),
+            in_specs=[AWAY, AWAY],
+            out_specs=WHOLE,
+            scratch_shapes=[pltpu.SemaphoreType.DMA((2,))],
+        ),
+        out_shape=VMEM(amplitudes.shape, BF),
+        compiler_params=params(1),
+        cost_estimate=cost(0, 8 * amplitudes.shape[1] * amplitudes.shape[2]),
+        name="cut",
+    )(sc, far(amplitudes), far(drive))
+
+
+def load_kernel(sc, recouple, amplitudes, *refs):
+    rows, amp, sems = refs[-3:]
     core, seg = sc[0], rows.shape[0] // 64
-    copies = [
-        pltpu.make_async_copy(source, to, sems.at[64 + i])
-        for i, (source, to) in enumerate(
-            (
-                (amplitudes.at[1 - core], amp_send),
-                (drive.at[1 - core], drive_send),
-                (amplitudes.at[core], amp),
-            )
-        )
-    ]
+    copies = [pltpu.make_async_copy(amplitudes.at[core], amp, sems.at[64])]
     for at in range(64):
-        chip_at = segment(core, sc[2] ^ (at // 8), sc[1] ^ (at % 8))
+        chip_at = segment(core, sc[2] ^ ORDER[at // 8], sc[1] ^ (at % 8))
         source = recouple.at[core, pl.ds(pl.multiple_of(chip_at * seg, seg), seg)]
         copies.append(
             pltpu.make_async_copy(source, rows.at[at * seg : (at + 1) * seg], sems.at[at])
@@ -131,22 +155,22 @@
         copy.wait()
 
 
-def load_call(sc, recouple, amplitudes, drive):
+def load_call(sc, recouple, amplitudes, *waits):
     _, n, half = amplitudes.shape
     return pl.pallas_call(
         load_kernel,
         grid_spec=pltpu.PrefetchScalarGridSpec(
             num_scalar_prefetch=1,
             grid=(1,),
-            in_specs=[AWAY] * 3,
-            out_specs=[WHOLE] * 4,
-            scratch_shapes=[pltpu.SemaphoreType.DMA((67,))],
+            in_specs=[AWAY, AWAY] + [WAIT] * len(waits),
+            out_specs=[WHOLE] * 2,
+            scratch_shapes=[pltpu.SemaphoreType.DMA((65,))],
         ),
-        out_shape=[VMEM((n, n), BF)] + [VMEM((n, half), BF)] * 3,
+        out_shape=[VMEM((n, n), BF), VMEM((n, half), BF)],
         compiler_params=params(1),
-        cost_estimate=cost(0, 2 * n * n),
+        cost_estimate=cost(0, 4 * n * n),
         name="load",
-    )(sc, far(recouple), far(amplitudes), far(drive))
+    )(sc, far(recouple), far(amplitudes), *waits)
 
 
 def spread(got, i, outs, columns):
@@ -178,17 +202,17 @@
     )(held(rows), held(amp), *waits)
 
 
-def other_kernel(rows, amp, *refs):
+def other_kernel(rows, pair, *refs):
     outs = refs[-8:]
-    n, half = amp.shape
+    _, n, half = pair.shape
     tile = n // TILES
     for i in range(TILES):
-        got = dot(rows[i * tile : (i + 1) * tile], amp[...]).astype(BF)
+        got = dot(rows[i * tile : (i + 1) * tile], pair[0]).astype(BF)
         spread(got, i, outs, slice(half, 2 * half))
 
 
-def other_call(rows, amp_other, begun, *waits):
-    n, half = amp_other.shape
+def other_call(rows, pair, begun, *waits):
+    _, n, half = pair.shape
     return pl.pallas_call(
         other_kernel,
         in_specs=[WHOLE] * 10 + [WAIT] * len(waits),
@@ -198,7 +222,7 @@
         compiler_params=params(4),
         cost_estimate=cost(2 * n * n * half, 4 * n * half),
         name="recoupled_other",
-    )(held(rows), held(amp_other), *[held(block) for block in begun], *waits)
+    )(held(rows), held(pair), *[held(block) for block in begun], *waits)
 
 
 def coupling_kernel(sc, own, oth, *refs):
@@ -258,14 +282,14 @@
     )(*[held(b) for b in blocks], *[held(c) for c in couplings], *waits)
 
 
-def ladder_kernel(tiles, sc, ladder_int, amp, amp_other, drive, drive_other, part, *refs):
+def ladder_kernel(tiles, sc, ladder_int, amp, drive, pair, part, *refs):
     out, out_part = refs[-2:]
     core, half, tile = sc[0], amp.shape[1], amp.shape[0] // TILES
     for i in tiles:
         at = slice(i * tile, (i + 1) * tile)
         left = ladder_int[core, at]
         out[at, :half] = dot(left, amp[...]) + drive[core, at].astype(F32)
-        out[at, half:] = dot(left, amp_other[...]) + drive_other[at].astype(F32)
+        out[at, half:] = dot(left, pair[0]) + pair[1, at].astype(F32)
         out_part[at, :] = jnp.broadcast_to(part[pl.ds(core, 1), at], (128, tile)).T
 
 
@@ -277,11 +301,11 @@
         grid_spec=pltpu.PrefetchScalarGridSpec(
             num_scalar_prefetch=1,
             grid=(1,),
-            in_specs=[WHOLE] * (6 + len(begun)) + [WAIT] * len(waits),
+            in_specs=[WHOLE] * (5 + len(begun)) + [WAIT] * len(waits),
             out_specs=[WHOLE, WHOLE],
         ),
         out_shape=[VMEM((n, 2 * half), F32), VMEM((n, 128), F32)],
-        input_output_aliases={7 + i: i for i in range(len(begun))},
+        input_output_aliases={6 + i: i for i in range(len(begun))},
         compiler_params=params(4),
         cost_estimate=cost(n * n * half * len(tiles), 8 * n * half),
         name="ladder",
@@ -306,12 +330,7 @@
 
 def folded(chosen, rows, at, lines):
     each = rows.shape[0] // 8
-    total = 0
-    for j, r in enumerate(chosen):
-        total += dot_rows(
-            rows[r * each : (r + 1) * each, at], lines[j * each : (j + 1) * each, :]
-        )
-    return total
+    return dot_rows(rows[chosen[0] * each : (chosen[-1] + 1) * each, at], lines[...])
 
 
 def folded_call(chosen, rows, returned, ladder, *waits):
@@ -331,38 +350,45 @@
 
 
 def final_kernel(chosen, side, sc, rows, ladder, part, hole, *refs):
-    blocks, (out, lines) = refs[: len(chosen)], refs[-2:]
-    core, i = sc[0], pl.program_id(0)
-    tile, half = out.shape[-2:]
+    blocks, (out, lines, made, sems) = refs[: len(chosen)], refs[-4:]
+    n, half = lines.shape[0] * 8 // len(chosen), lines.shape[1]
+    tile = n // TILES
     cols = slice(side * half, (side + 1) * half)
-
-    @pl.when(i == 0)
-    def _():
-        gathered(blocks, lines, cols)
-
-    at = pl.ds(pl.multiple_of(i * tile, tile), tile)
-    total = ladder[at, cols] + folded(chosen, rows, at, lines)
-    got = (total / (part[at, :1] - hole[pl.ds(core, 1), :])).astype(BF)
-    out[...] = got.reshape(out.shape)
+    gathered(blocks, lines, cols)
+    copies = []
+    for i in range(TILES):
+        at = slice(i * tile, (i + 1) * tile)
+        total = ladder[at, cols] + folded(chosen, rows, at, lines)
+        got = (total / (part[at, :1] - hole[pl.ds(sc[0], 1), :])).astype(BF)
+        if side == 1:
+            out[at] = got
+        else:
+            made[at] = got
+            copies.append(
+                pltpu.make_async_copy(made.at[at], out.at[sc[0], at], sems.at[i])
+            )
+            copies[-1].start()
+    for copy in copies:
+        copy.wait()
 
 
 def final_call(chosen, side, sc, rows, returned, ladder, part, hole, *waits):
     n, h = ladder.shape
-    tile, half = n // TILES, h // 2
-    if side == 0:
-        out_spec = pl.BlockSpec((1, tile, half), lambda i, sc: (sc[0], i, 0))
-    else:
-        out_spec = pl.BlockSpec((tile, half), lambda i, sc: (i, 0))
+    half = h // 2
     return pl.pallas_call(
         functools.partial(final_kernel, chosen, side),
         grid_spec=pltpu.PrefetchScalarGridSpec(
             num_scalar_prefetch=1,
-            grid=(TILES,),
+            grid=(1,),
             in_specs=[WHOLE] * (4 + len(chosen)) + [WAIT] * len(waits),
-            out_specs=out_spec,
-            scratch_shapes=[VMEM((n * len(chosen) // 8, half), BF)],
+            out_specs=WHOLE if side else AWAY,
+            scratch_shapes=[
+                VMEM((n * len(chosen) // 8, half), BF),
+                VMEM((n, half), BF),
+                pltpu.SemaphoreType.DMA((TILES,)),
+            ],
         ),
-        out_shape=pltpu.HBM((2, n, half), BF) if side == 0 else VMEM((n, half), BF),
+        out_shape=VMEM((n, half), BF) if side else pltpu.HBM((2, n, half), BF),
         compiler_params=params(6),
         cost_estimate=cost(2 * n * n * half, 6 * n * half),
         name=("final_own", "final_other")[side],
@@ -377,74 +403,88 @@
     )
 
 
-def place_kernel(sc, given, arrived, out, sem):
-    copy = pltpu.make_async_copy(arrived, out.at[1 - sc[0]], sem)
-    copy.start()
-    copy.wait()
-
-
-def place_call(sc, out, arrived):
+def place_kernel(sc, arrived, given, out, sems):
+    each = arrived.shape[0] // TILES
+    copies = []
+    for i in range(TILES):
+        at = slice(i * each, (i + 1) * each)
+        copies.append(
+            pltpu.make_async_copy(arrived.at[at], out.at[1 - sc[0], at], sems.at[i])
+        )
+    for copy in copies:
+        copy.start()
+    for copy in copies:
+        copy.wait()
+
+
+def place_call(sc, arrived, out):
+    n, half = arrived.shape
     return pl.pallas_call(
         place_kernel,
         grid_spec=pltpu.PrefetchScalarGridSpec(
             num_scalar_prefetch=1,
             grid=(1,),
-            in_specs=[AWAY, WAIT],
+            in_specs=[WHOLE, AWAY],
             out_specs=AWAY,
-            scratch_shapes=[pltpu.SemaphoreType.DMA],
+            scratch_shapes=[pltpu.SemaphoreType.DMA((TILES,))],
         ),
-        out_shape=pltpu.HBM(out.shape, BF),
-        input_output_aliases={1: 0},
+        out_shape=pltpu.HBM((2, n, half), BF),
+        input_output_aliases={2: 0},
         compiler_params=params(1),
-        cost_estimate=cost(0, 2 * out.shape[1] * out.shape[2]),
+        cost_estimate=cost(0, 4 * n * half),
         name="place",
-    )(sc, far(out), arrived)
+    )(sc, held(arrived), far(out))
 
 
 def local(amplitudes, recouple, ladder_int, cycle_coupling, drive, eps_part, eps_hole):
     core, here = lax.axis_index("dom"), lax.axis_index("chan")
     moved = kept = 0
-    for weight in (16, 4, 1):
+    for first, weight in zip(HIGH, (16, 4, 1)):
         place = (here // weight) % 4
         high, low = place // 2, ((place + 1) // 2) % 2
-        moved = 2 * moved + jnp.where(core == 0, high, low)
-        kept = 2 * kept + jnp.where(core == 0, low, high)
+        moved = 2 * moved + jnp.where(core == 1 - first, high, low)
+        kept = 2 * kept + jnp.where(core == 1 - first, low, high)
     sc = jnp.stack([core, kept, moved]).astype(jnp.int32)
 
     coupling_other = swap(cycle_coupling)
     hole_other = swap(eps_hole)
-    rows, amp, amp_send, drive_send = load_call(sc, recouple, amplitudes, drive)
-    c0 = coupling_call(sc, cycle_coupling, coupling_other, amp_send)
-    amp_send, drive_send = tie([amp_send, drive_send], c0)
-    amp_other, drive_other = swap(amp_send), swap(drive_send)
+    pair = cut_call(sc, amplitudes, drive)
+    c0 = coupling_call(sc, cycle_coupling, coupling_other, pair, hole_other)
+    (pair,) = tie([pair], c0)
+    pair = swap(pair)
 
     c4, c2, c1 = over(c0, kept=4), over(c0, kept=2), over(c0, kept=1)
-    begun = own_call(rows, amp, c0, hole_other)
-    send = other_call(rows, amp_other, begun, drive_other)
-
-    c4, c2, c1 = tie([c4, c2, c1], send[0])
+    rows, amp = load_call(sc, recouple, amplitudes, c0)
+
+    begun = own_call(rows, amp)
+    c4, c2, c1 = tie([c4, c2, c1], begun[0])
     c6, c3, c5 = over(c4, kept=2), over(c2, kept=1), over(c1, kept=4)
-    blocks = [send[0]] + [None] * 7
+    send = dict(zip(ORDER, other_call(rows, pair, begun)))
+
+    blocks = {0: send[0]}
     for r in FIRST:
         blocks[r] = over(send[r], moved=r)
-    operands = [sc, ladder_int, amp, amp_other, drive, drive_other, eps_part]
-    begun = ladder_call((0, 1), (), operands, send[0])
-    ladder, part = ladder_call((2, 3), begun, operands, *[blocks[r] for r in FIRST])
-
-    c6, c3, c5, *rest = tie([c6, c3, c5] + [send[r] for r in THEN], ladder)
+    operands = [sc, ladder_int, amp, drive, pair, eps_part]
+    ladder = ladder_call((0,), (), operands)
+
+    c6, c3, c5, *rest = tie(
+        [c6, c3, c5] + [send[r] for r in THEN], ladder[0], blocks[FIRST[0]]
+    )
     c7 = over(c6, kept=1)
     for r, block in zip(THEN, rest):
         blocks[r] = over(block, moved=r)
+    ladder, part = ladder_call((1, 2, 3), ladder, operands)
 
     couplings = [c0, c1, c2, c3, c4, c5, c6, c7]
-    returned = [None] * 8
+    returned = []
     for group in BACK:
-        for r, block in zip(group, cycle_call([blocks[r] for r in group], couplings)):
-            returned[r] = over(block, moved=r) if r else block
-    ladder = folded_call(EARLY, rows, returned, ladder)
+        cycled = cycle_call([blocks[r] for r in group], couplings, ladder)
+        returned += [over(block, moved=r) if r else block for r, block in zip(group, cycled)]
+    for group in EARLY:
+        ladder = folded_call(group, rows, returned, ladder)
     out_other = final_call(LATE, 1, sc, rows, returned, ladder, part, hole_other)
     out = final_call(LATE, 0, sc, rows, returned, ladder, part, eps_hole, out_other)
-    return place_call(sc, out, swap(out_other))
+    return place_call(sc, swap(out_other), out)
 
 
 def solution(mesh):

time: 95.9 us -> 82.7 us (0.86)
  waiting for transfers between devices: 21.3 us -> 10.5 us
  starting transfers between devices: 44.3 us -> 40.9 us
    ppermute x21, waiting for transfers between devices: 21.3 us -> 10.3 us  [over(): return lax.ppermute(array, BOTH, flips(moved, kept))]
    ppermute x5 -> x4, starting transfers between devices: 12.3 us -> 6.77 us  [swap(): return lax.ppermute(array, 'dom', [(0, 1), (1, 0)])]
    pallas_call x2, Pallas kernels: 6.2 us -> 3.53 us  [final_call(): pl.pallas_call(functools.partial(final_kernel, chosen, side), grid_spec=p...]
    ppermute x21, starting transfers between devices: 31.9 us -> 34.2 us  [over(): return lax.ppermute(array, BOTH, flips(moved, kept))]
    pallas_call x1 -> x2, Pallas kernels: 2.57 us -> 4.68 us  [folded_call(): pl.pallas_call(functools.partial(folded_kernel, chosen), in_specs=[WHOLE]...]
    pallas_call x0 -> x1, Pallas kernels: none -> 2.1 us  [cut_call(): pl.pallas_call(cut_kernel, grid_spec=pltpu.PrefetchScalarGridSpec(num_sca...]
  transfers between devices with their start and end apart: 26 -> 25, of which waited for: 8 -> 7; matrix products, arithmetic and copies ran while one was open for 0% -> 0% of each run, Pallas kernels for 25% -> 32%
where the time goes in v4:
time: 82.7 us; the launch traced here: 82.5 us
  starting transfers between devices  40.9 us (49%)
  Pallas kernels  30.5 us (37%)
  waiting for transfers between devices  10.5 us (13%)
    ppermute x21, starting transfers between devices, over(): return lax.ppermute(array, BOTH, flips(moved, kept))  34.2 us
    ppermute x21, waiting for transfers between devices, over(): return lax.ppermute(array, BOTH, flips(moved, kept))  10.3 us
    ppermute x4, starting transfers between devices, swap(): return lax.ppermute(array, 'dom', [(0, 1), (1, 0)])  6.77 us
    pallas_call x2, Pallas kernels, ladder_call(): pl.pallas_call(functools.partial(ladder_kernel, tiles), grid_spec=pltpu.P...  5.73 us
    pallas_call x1, Pallas kernels, load_call(): pl.pallas_call(load_kernel, grid_spec=pltpu.PrefetchScalarGridSpec(num_sc...  5.08 us
    pallas_call x2, Pallas kernels, folded_call(): pl.pallas_call(functools.partial(folded_kernel, chosen), in_specs=[WHOLE]...  4.68 us
    pallas_call x2, Pallas kernels, final_call(): pl.pallas_call(functools.partial(final_kernel, chosen, side), grid_spec=p...  3.53 us
    pallas_call x1, Pallas kernels, other_call(): pl.pallas_call(other_kernel, in_specs=[WHOLE] * 10 + [WAIT] * len(waits),...  2.33 us
  transfers between devices with their start and end apart: 25, of which 7 were waited for; matrix products, arithmetic and copies ran while one was open for 0% of the time, Pallas kernels for 32%

profile of v4, /device:TPU:1, one launch (start us, length us, event | category | flops | bytes accessed | tf_op | source)
XLA Modules:
  0.0 82.5 jit_solution(3885453356757106330)
XLA Ops:
  0.0 1.4 %collective-permute-start = (bf16[2,256,512]{2,1,0:T(8,128)(2,1)}, bf16[2,256,512]{2,1,0:T(8,128)(2,1)S(1)}, u32[]{:S(2)}, u32[]{:S(2)}) collective-permute-start(bf16[2,256,512]{2,1,0:T(8,128)(2,1)} %own.1), channel_id=1, source_target_pairs={{0,1},{1,0},{2,3},{3,2},{4,5},{5,4},{6,7},{7,6},{8,9},{9,8},{10,11... | collective-permute-start | bytes 1572872 | tf_op jit(solution)/shard_map/ppermute | solution.py:47
  1.4 0.0 collective-permute-start.1
  1.4 0.1 pad_add_fusion.sc
  1.5 2.1 %cut.1.refs_0_ = bf16[2,2048,256]{2,1,0:T(8,128)(2,1)S(1)} custom-call(s32[3]{0:T(128)S(1)} %pad_add_fusion.sc, bf16[2,2048,256]{2,1,0:T(8,128)(2,1)} %amplitudes.3, bf16[2,2048,256]{2,1,0:T(8,128)(2,1)} %drive.5), custom_call_target="tpu_custom_call" | custom-call | bytes 4194304 | tf_op jit(solution)/shard_map/cut/pallas_call | solution.py:126
  3.6 0.0 collective-permute-done.1.refs_1_.hole
  3.6 0.0 collective-permute-done.oth
  3.6 1.6 %coupling.1.refs_0_.refs_1_.refs_5_.refs_3_ = bf16[512,512]{1,0:T(8,128)(2,1)S(1)} custom-call(s32[3]{0:T(128)S(1)} %pad_add_fusion.sc, bf16[2,256,512]{2,1,0:T(8,128)(2,1)} %own.1, bf16[2,256,512]{2,1,0:T(8,128)(2,1)S(1)} %collective-permute-done.oth, bf16[2,2048,256]{2,1,0:T(8,128)(2,1)S(1)} %cut.1.refs_0_, f32[2,256]{1,0:T(2,128)S(1)} %collective-permute-done.1.refs_1_.hole), custom_call_target="tpu_custom_call" | custom-call | bytes 1048576 | tf_op jit(solution)/shard_map/coupling/pallas_call | solution.py:245
  5.2 0.6 collective-permute-start.2
  5.8 2.6 %collective-permute-start.5 = (bf16[512,512]{1,0:T(8,128)(2,1)S(1)}, bf16[512,512]{1,0:T(8,128)(2,1)S(1)}, u32[]{:S(2)}, u32[]{:S(2)}) collective-permute-start(bf16[512,512]{1,0:T(8,128)(2,1)S(1)} %coupling.1.refs_0_.refs_1_.refs_5_.refs_3_), channel_id=1, source_target_pairs={{0,2},{2,0},{24,26},{26,24},{32,34},{34,32},{56,58},{58,56},{6,4},... | collective-permute-start | bytes 1572872 | tf_op jit(solution)/shard_map/ppermute | solution.py:51
  8.4 1.3 %collective-permute-start.4 = (bf16[512,512]{1,0:T(8,128)(2,1)S(1)}, bf16[512,512]{1,0:T(8,128)(2,1)S(1)}, u32[]{:S(2)}, u32[]{:S(2)}) collective-permute-start(bf16[512,512]{1,0:T(8,128)(2,1)S(1)} %coupling.1.refs_0_.refs_1_.refs_5_.refs_3_), channel_id=1, source_target_pairs={{0,24},{2,26},{24,0},{26,2},{32,56},{34,58},{56,32},{58,34},{6,30}... | collective-permute-start | bytes 1572872 | tf_op jit(solution)/shard_map/ppermute | solution.py:51
  9.6 3.8 %collective-permute-start.3 = (bf16[512,512]{1,0:T(8,128)(2,1)S(1)}, bf16[512,512]{1,0:T(8,128)(2,1)S(1)}, u32[]{:S(2)}, u32[]{:S(2)}) collective-permute-start(bf16[512,512]{1,0:T(8,128)(2,1)S(1)} %coupling.1.refs_0_.refs_1_.refs_5_.refs_3_), channel_id=1, source_target_pairs={{0,32},{2,34},{24,56},{26,58},{32,0},{34,2},{56,24},{58,26},{6,38}... | collective-permute-start | bytes 1572872 | tf_op jit(solution)/shard_map/ppermute | solution.py:51
  13.4 5.1 %load.1 = (bf16[2048,2048]{1,0:T(8,128)(2,1)S(1)}, bf16[2048,256]{1,0:T(8,128)(2,1)S(1)}) custom-call(s32[3]{0:T(128)S(1)} %pad_add_fusion.sc, bf16[2,2048,2048]{2,1,0:T(8,128)(2,1)} %recouple.1, bf16[2,2048,256]{2,1,0:T(8,128)(2,1)} %amplitudes.3, bf16[512,512]{1,0:T(8,128)(2,1)S(1)} %coupling.1.refs_0_.refs_1_.refs_5_.refs_3_), custom_call_target="tpu_custom_call" | custom-call | bytes 16777216 | tf_op jit(solution)/shard_map/load/pallas_call | solution.py:160
  18.5 0.0 slice-start.2
  18.5 2.3 %recoupled_own.1 = (bf16[8,32,512]{2,1,0:T(8,128)(2,1)S(1)}, bf16[8,32,512]{2,1,0:T(8,128)(2,1)S(1)}, bf16[8,32,512]{2,1,0:T(8,128)(2,1)S(1)}, bf16[8,32,512]{2,...) custom-call(bf16[2048,2048]{1,0:T(8,128)(2,1)S(1)} %get-tuple-elemen, ...), custom_call_target="tpu_custom_call" | custom-call | flops 2147483648 | bytes 8388608 | tf_op jit(solution)/shard_map/recoupled_own/pallas_call | solution.py:194
  20.8 0.0 collective-permute-done.5.refs_2_
  20.9 0.0 collective-permute-done.4.refs_1_
  20.9 0.0 collective-permute-done.3.refs_0_
  20.9 0.2 collective-permute-start.6
  21.1 0.2 collective-permute-start.7
  21.3 1.7 %collective-permute-start.8 = (bf16[512,512]{1,0:T(8,128)(2,1)S(1)}, bf16[512,512]{1,0:T(8,128)(2,1)S(1)}, u32[]{:S(2)}, u32[]{:S(2)}) collective-permute-start(bf16[512,512]{1,0:T(8,128)(2,1)S(1)} %get-tuple-element.62.refs_6_.refs_4_), channel_id=1, source_target_pairs={{0,32},{2,34},{24,56},{26,58},{32,0},{34,2},{56,24},{58,26},{6,38}... | collective-permute-start | bytes 1572872 | tf_op jit(solution)/shard_map/ppermute | solution.py:51
  23.0 0.0 collective-permute-done.2.pair
  23.0 2.3 %recoupled_other.1 = (bf16[8,32,512]{2,1,0:T(8,128)(2,1)S(1)}, bf16[8,32,512]{2,1,0:T(8,128)(2,1)S(1)}, bf16[8,32,512]{2,1,0:T(8,128)(2,1)S(1)}, bf16[8,32,512]{...) custom-call(bf16[2048,2048]{1,0:T(8,128)(2,1)S(1)} %get-tuple-elemen, ...), custom_call_target="tpu_custom_call", output_to_operand_aliasing={{0}: (2, {}), {1}: (3, {}), {2}: (4, {}), {3}: (5, {}), {4}... | custom-call | flops 2147483648 | bytes 2097152 | tf_op jit(solution)/shard_map/recoupled_other/pallas_call | solution.py:216
  25.4 0.2 collective-permute-start.9
  25.6 3.8 %collective-permute-start.12 = (bf16[8,32,512]{2,1,0:T(8,128)(2,1)S(1)}, bf16[8,32,512]{2,1,0:T(8,128)(2,1)S(1)}, u32[]{:S(2)}, u32[]{:S(2)}) collective-permute-start(bf16[8,32,512]{2,1,0:T(8,128)(2,1)S(1)} %get-tuple-element.71), channel_id=1, source_target_pairs={{0,14},{2,12},{24,22},{26,20},{32,46},{34,44},{56,54},{58,52},{6,8... | collective-permute-start | bytes 786440 | tf_op jit(solution)/shard_map/ppermute | solution.py:51
  29.4 1.8 %ladder.2 = (f32[2048,512]{1,0:T(8,128)S(1)}, f32[2048,128]{1,0:T(8,128)S(1)}) custom-call(s32[3]{0:T(128)S(1)} %pad_add_fusion.sc, bf16[2,2048,2048]{2,1,0:T(8,128)(2,1)S(1)} %bitcast.4, bf16[2048,256]{1,0:T(8,128)(2,1)S(1)} %get-tuple-element.47.amp, bf16[2,2048,256]{2,1,0:T(8,128)(2,1)S(1)} %copy-done, ...), custom_call_target="tpu_custom_call" | custom-call | flops 1073741824 | bytes 4194304 | tf_op jit(solution)/shard_map/ladder/pallas_call | solution.py:299
  31.2 0.0 collective-permute-done.6.refs_0_
  31.2 0.0 collective-permute-done.7.refs_1_
  31.2 0.0 collective-permute-done.8.refs_2_
  31.2 1.2 %collective-permute-done.9.refs_9_.refs_4_ = bf16[8,32,512]{2,1,0:T(8,128)(2,1)S(1)} collective-permute-done((bf16[8,32,512]{2,1,0:T(8,128)(2,1)S(1)}, bf16[8,32,512]{2,1,0:T(8,128)(2,1)S(1)}, u32[]{:S(2)}, u32[]{:S(2)}) %collective-permute-start.9) | collective-permute-done | bytes 262176 | tf_op jit(solution)/shard_map/ppermute | solution.py:51
  32.5 1.8 %collective-permute-start.13 = (bf16[512,512]{1,0:T(8,128)(2,1)S(1)}, bf16[512,512]{1,0:T(8,128)(2,1)S(1)}, u32[]{:S(2)}, u32[]{:S(2)}) collective-permute-start(bf16[512,512]{1,0:T(8,128)(2,1)S(1)} %get-tuple-element.74.refs_11_.refs_9_), channel_id=1, source_target_pairs={{0,2},{2,0},{24,26},{26,24},{32,34},{34,32},{56,58},{58,56},{6,4},... | collective-permute-start | bytes 1572872 | tf_op jit(solution)/shard_map/ppermute | solution.py:51
  34.3 1.9 %collective-permute-start.10 = (bf16[8,32,512]{2,1,0:T(8,128)(2,1)S(1)}, bf16[8,32,512]{2,1,0:T(8,128)(2,1)S(1)}, u32[]{:S(2)}, u32[]{:S(2)}) collective-permute-start(bf16[8,32,512]{2,1,0:T(8,128)(2,1)S(1)} %get-tuple-element.69), channel_id=1, source_target_pairs={{0,110},{2,108},{24,118},{26,116},{32,78},{34,76},{56,86},{58,84},... | collective-permute-start | bytes 786440 | tf_op jit(solution)/shard_map/ppermute | solution.py:51
  36.2 2.2 %collective-permute-start.11 = (bf16[8,32,512]{2,1,0:T(8,128)(2,1)S(1)}, bf16[8,32,512]{2,1,0:T(8,128)(2,1)S(1)}, u32[]{:S(2)}, u32[]{:S(2)}) collective-permute-start(bf16[8,32,512]{2,1,0:T(8,128)(2,1)S(1)} %get-tuple-element.70), channel_id=1, source_target_pairs={{0,102},{2,100},{24,126},{26,124},{32,70},{34,68},{56,94},{58,92},... | collective-permute-start | bytes 786440 | tf_op jit(solution)/shard_map/ppermute | solution.py:51
  38.4 1.0 %collective-permute-start.18 = (bf16[8,32,512]{2,1,0:T(8,128)(2,1)S(1)}, bf16[8,32,512]{2,1,0:T(8,128)(2,1)S(1)}, u32[]{:S(2)}, u32[]{:S(2)}) collective-permute-start(bf16[8,32,512]{2,1,0:T(8,128)(2,1)S(1)} %get-tuple-element.80), channel_id=1, source_target_pairs={{0,104},{2,106},{24,112},{26,114},{32,72},{34,74},{56,80},{58,82},... | collective-permute-start | bytes 786440 | tf_op jit(solution)/shard_map/ppermute | solution.py:51
  39.4 0.0 collective-permute-done.12.refs_3_
  39.4 2.4 %collective-permute-start.19 = (bf16[8,32,512]{2,1,0:T(8,128)(2,1)S(1)}, bf16[8,32,512]{2,1,0:T(8,128)(2,1)S(1)}, u32[]{:S(2)}, u32[]{:S(2)}) collective-permute-start(bf16[8,32,512]{2,1,0:T(8,128)(2,1)S(1)} %get-tuple-element.81), channel_id=1, source_target_pairs={{0,8},{2,10},{24,16},{26,18},{32,40},{34,42},{56,48},{58,50},{6,14... | collective-permute-start | bytes 786440 | tf_op jit(solution)/shard_map/ppermute | solution.py:51
  41.8 3.9 %ladder.3 = (f32[2048,512]{1,0:T(8,128)S(1)}, f32[2048,128]{1,0:T(8,128)S(1)}) custom-call(s32[3]{0:T(128)S(1)} %pad_add_fusion.sc, bf16[2,2048,2048]{2,1,0:T(8,128)(2,1)S(1)} %bitcast.4, bf16[2048,256]{1,0:T(8,128)(2,1)S(1)} %get-tuple-element.47.amp, bf16[2,2048,256]{2,1,0:T(8,128)(2,1)S(1)} %copy-done, ...), custom_call_target="tpu_custom_call", output_to_operand_aliasing={{0}: (6, {}), {1}: (7, {})} | custom-call | flops 3221225472 | bytes 4194304 | tf_op jit(solution)/shard_map/ladder/pallas_call | solution.py:299
  45.8 0.0 collective-permute-done.10.refs_1_
  45.8 0.5 collective-permute-start.20
  46.3 3.7 %collective-permute-done.11.refs_2_ = bf16[8,32,512]{2,1,0:T(8,128)(2,1)S(1)} collective-permute-done((bf16[8,32,512]{2,1,0:T(8,128)(2,1)S(1)}, bf16[8,32,512]{2,1,0:T(8,128)(2,1)S(1)}, u32[]{:S(2)}, u32[]{:S(2)}) %collective-permute-start.11) | collective-permute-done | bytes 262176 | tf_op jit(solution)/shard_map/ppermute | solution.py:51
  50.0 0.0 collective-permute-done.13.refs_12_.refs_10_
  50.0 0.9 %cycle.2 = (bf16[8,32,512]{2,1,0:T(8,128)(2,1)S(1)}, bf16[8,32,512]{2,1,0:T(8,128)(2,1)S(1)}, bf16[8,32,512]{2,1,0:T(8,128)(2,1)S(1)}, bf16[8,32,512]{2,1,0:T(8,128)(2,1)S(1)}, bf16[8,32,512]{2,1,0:T(8,128)(2,1)S(1)}) custom-call(bf16[8,32,512]{2,1,0:T(8,128)(2,1)S(1)} %get-tuple-element.59.refs_0_, bf16[8,32,512]{2,1,0:T(8,128)(2,1)S(1)} %collective-permute-done.10.refs_1_, ...), custom_call_target="tpu_custom_call" | custom-call | flops 671088640 | bytes 6815744 | tf_op jit(solution)/shard_map/cycle/pallas_call | solution.py:274
  50.9 1.0 %collective-permute-start.14 = (bf16[8,32,512]{2,1,0:T(8,128)(2,1)S(1)}, bf16[8,32,512]{2,1,0:T(8,128)(2,1)S(1)}, u32[]{:S(2)}, u32[]{:S(2)}) collective-permute-start(bf16[8,32,512]{2,1,0:T(8,128)(2,1)S(1)} %get-tuple-element.76), channel_id=1, source_target_pairs={{0,110},{2,108},{24,118},{26,116},{32,78},{34,76},{56,86},{58,84},... | collective-permute-start | bytes 786440 | tf_op jit(solution)/shard_map/ppermute | solution.py:51
  51.9 2.5 %collective-permute-start.15 = (bf16[8,32,512]{2,1,0:T(8,128)(2,1)S(1)}, bf16[8,32,512]{2,1,0:T(8,128)(2,1)S(1)}, u32[]{:S(2)}, u32[]{:S(2)}) collective-permute-start(bf16[8,32,512]{2,1,0:T(8,128)(2,1)S(1)} %get-tuple-element.77), channel_id=1, source_target_pairs={{0,102},{2,100},{24,126},{26,124},{32,70},{34,68},{56,94},{58,92},... | collective-permute-start | bytes 786440 | tf_op jit(solution)/shard_map/ppermute | solution.py:51
  54.4 0.0 collective-permute-done.18.refs_0_
  54.4 1.4 %collective-permute-start.16 = (bf16[8,32,512]{2,1,0:T(8,128)(2,1)S(1)}, bf16[8,32,512]{2,1,0:T(8,128)(2,1)S(1)}, u32[]{:S(2)}, u32[]{:S(2)}) collective-permute-start(bf16[8,32,512]{2,1,0:T(8,128)(2,1)S(1)} %get-tuple-element.78), channel_id=1, source_target_pairs={{0,14},{2,12},{24,22},{26,20},{32,46},{34,44},{56,54},{58,52},{6,8... | collective-permute-start | bytes 786440 | tf_op jit(solution)/shard_map/ppermute | solution.py:51
  55.8 0.0 collective-permute-done.19.refs_1_
  55.8 1.1 %collective-permute-start.17 = (bf16[8,32,512]{2,1,0:T(8,128)(2,1)S(1)}, bf16[8,32,512]{2,1,0:T(8,128)(2,1)S(1)}, u32[]{:S(2)}, u32[]{:S(2)}) collective-permute-start(bf16[8,32,512]{2,1,0:T(8,128)(2,1)S(1)} %get-tuple-element.79), channel_id=1, source_target_pairs={{0,6},{2,4},{24,30},{26,28},{32,38},{34,36},{56,62},{58,60},{6,0},... | collective-permute-start | bytes 786440 | tf_op jit(solution)/shard_map/ppermute | solution.py:51
  56.9 0.8 cycle.3
  57.7 2.2 %collective-permute-start.21 = (bf16[8,32,512]{2,1,0:T(8,128)(2,1)S(1)}, bf16[8,32,512]{2,1,0:T(8,128)(2,1)S(1)}, u32[]{:S(2)}, u32[]{:S(2)}) collective-permute-start(bf16[8,32,512]{2,1,0:T(8,128)(2,1)S(1)} %get-tuple-element.83), channel_id=1, source_target_pairs={{0,104},{2,106},{24,112},{26,114},{32,72},{34,74},{56,80},{58,82},... | collective-permute-start | bytes 786440 | tf_op jit(solution)/shard_map/ppermute | solution.py:51
  59.9 0.3 collective-permute-done.14.refs_1_
  60.2 1.4 %collective-permute-start.22 = (bf16[8,32,512]{2,1,0:T(8,128)(2,1)S(1)}, bf16[8,32,512]{2,1,0:T(8,128)(2,1)S(1)}, u32[]{:S(2)}, u32[]{:S(2)}) collective-permute-start(bf16[8,32,512]{2,1,0:T(8,128)(2,1)S(1)} %get-tuple-element.84), channel_id=1, source_target_pairs={{0,8},{2,10},{24,16},{26,18},{32,40},{34,42},{56,48},{58,50},{6,14... | collective-permute-start | bytes 786440 | tf_op jit(solution)/shard_map/ppermute | solution.py:51
  61.6 0.6 collective-permute-done.15.refs_2_
  62.2 0.9 %collective-permute-start.23 = (bf16[8,32,512]{2,1,0:T(8,128)(2,1)S(1)}, bf16[8,32,512]{2,1,0:T(8,128)(2,1)S(1)}, u32[]{:S(2)}, u32[]{:S(2)}) collective-permute-start(bf16[8,32,512]{2,1,0:T(8,128)(2,1)S(1)} %get-tuple-element.86), channel_id=1, source_target_pairs={{0,96},{2,98},{24,120},{26,122},{32,64},{34,66},{56,88},{58,90},{6... | collective-permute-start | bytes 786440 | tf_op jit(solution)/shard_map/ppermute | solution.py:51
  63.1 2.9 %collective-permute-done.16.refs_3_ = bf16[8,32,512]{2,1,0:T(8,128)(2,1)S(1)} collective-permute-done((bf16[8,32,512]{2,1,0:T(8,128)(2,1)S(1)}, bf16[8,32,512]{2,1,0:T(8,128)(2,1)S(1)}, u32[]{:S(2)}, u32[]{:S(2)}) %collective-permute-start.16) | collective-permute-done | bytes 262176 | tf_op jit(solution)/shard_map/ppermute | solution.py:51
  66.0 1.6 %collective-permute-done.17.refs_4_ = bf16[8,32,512]{2,1,0:T(8,128)(2,1)S(1)} collective-permute-done((bf16[8,32,512]{2,1,0:T(8,128)(2,1)S(1)}, bf16[8,32,512]{2,1,0:T(8,128)(2,1)S(1)}, u32[]{:S(2)}, u32[]{:S(2)}) %collective-permute-start.17) | collective-permute-done | bytes 262176 | tf_op jit(solution)/shard_map/ppermute | solution.py:51
  67.6 3.2 %folded.2.ladder = f32[2048,512]{1,0:T(8,128)S(1)} custom-call(bf16[2048,2048]{1,0:T(8,128)(2,1)S(1)} %get-tuple-element.46.rows, f32[2048,512]{1,0:T(8,128)S(1)} %get-tuple-element.50.refs_13_.ladder.refs_11_, bf16[8,32,512]{2,1,0:T(8,128)(2,1)S(1)} %get-tuple-element.75.refs_0_, ...), custom_call_target="tpu_custom_call", output_to_operand_aliasing={{}: (1, {})} | custom-call | flops 2684354560 | bytes 6291456 | tf_op jit(solution)/shard_map/folded/pallas_call | solution.py:339
  70.8 0.0 collective-permute-done.22.refs_1_
  70.8 1.5 %folded.3.ladder = f32[2048,512]{1,0:T(8,128)S(1)} custom-call(bf16[2048,2048]{1,0:T(8,128)(2,1)S(1)} %get-tuple-element.46.rows, f32[2048,512]{1,0:T(8,128)S(1)} %folded.2.ladder, bf16[8,32,512]{2,1,0:T(8,128)(2,1)S(1)} %collective-permute-done.21.refs_0_, bf16[8,32,512]{2,1,0:T(8,128)(2,1)S(1)} %collective-permute-done.22.refs_1_), custom_call_target="tpu_custom_call", output_to_operand_aliasing={{}: (1, {})} | custom-call | flops 1073741824 | bytes 6291456 | tf_op jit(solution)/shard_map/folded/pallas_call | solution.py:339
  72.3 0.0 copy-start.2
  72.3 1.4 %final_other.1.refs_1_ = bf16[2048,256]{1,0:T(8,128)(2,1)S(1)} custom-call(s32[3]{0:T(128)S(1)} %pad_add_fusion.sc, bf16[2048,2048]{1,0:T(8,128)(2,1)S(1)} %get-tuple-element.46.rows, f32[2048,512]{1,0:T(8,128)S(1)} %folded.3.ladder, f32[2048,128]{1,0:T(8,128)S(1)} %get-tuple-element.85.part, f32[2,256]{1,0:T(2,128)S(1)} %collective-permute-done.1.refs_1_.hole, ...), custom_call_target="tpu_custom_call" | custom-call | flops 2147483648 | bytes 3145728 | tf_op jit(solution)/shard_map/final_other/pallas_call | solution.py:378
  73.8 4.8 %collective-permute-start.24 = (bf16[2048,256]{1,0:T(8,128)(2,1)S(1)}, bf16[2048,256]{1,0:T(8,128)(2,1)S(1)}, u32[]{:S(2)}, u32[]{:S(2)}) collective-permute-start(bf16[2048,256]{1,0:T(8,128)(2,1)S(1)} %final_other.1.refs_1_), channel_id=1, source_target_pairs={{0,1},{1,0},{2,3},{3,2},{4,5},{5,4},{6,7},{7,6},{8,9},{9,8},{10,11... | collective-permute-start | bytes 3145736 | tf_op jit(solution)/shard_map/ppermute | solution.py:47
  78.5 2.1 %final_own.1.given = bf16[2,2048,256]{2,1,0:T(8,128)(2,1)} custom-call(s32[3]{0:T(128)S(1)} %pad_add_fusion.sc, bf16[2048,2048]{1,0:T(8,128)(2,1)S(1)} %get-tuple-element.46.rows, f32[2048,512]{1,0:T(8,128)S(1)} %folded.3.ladder, f32[2048,128]{1,0:T(8,128)S(1)} %get-tuple-element.85.part, f32[2,256]{1,0:T(2,128)S(1)} %copy-done.2, ...), custom_call_target="tpu_custom_call" | custom-call | flops 2147483648 | bytes 3145728 | tf_op jit(solution)/shard_map/final_own/pallas_call | solution.py:378
  80.7 0.2 collective-permute-done.24.arrived
  80.8 1.5 %place.1 = bf16[2,2048,256]{2,1,0:T(8,128)(2,1)} custom-call(s32[3]{0:T(128)S(1)} %pad_add_fusion.sc, bf16[2048,256]{1,0:T(8,128)(2,1)S(1)} %collective-permute-done.24.arrived, bf16[2,2048,256]{2,1,0:T(8,128)(2,1)} %final_own.1.given), custom_call_target="tpu_custom_call", output_to_operand_aliasing={{}: (2, {})} | custom-call | bytes 2097152 | tf_op jit(solution)/shard_map/place/pallas_call | solution.py:422
  (19 shorter events, 0.0 us)
Async XLA Ops:
  0.0 3.6 %collective-permute-start = (bf16[2,256,512]{2,1,0:T(8,128)(2,1)}, bf16[2,256,512]{2,1,0:T(8,128)(2,1)S(1)}, u32[]{:S(2)}, u32[]{:S(2)}) collective-permute-start(bf16[2,256,512]{2,1,0:T(8,128)(2,1)} %own.1), channel_id=1, source_target_pairs={{0,1},{1,0},{2,3},{3,2},{4,5},{5,4},{6,7},{7,6},{8,9},{9,8},{10,11... | collective-permute-start | bytes 1572872 | tf_op jit(solution)/shard_map/ppermute | solution.py:47
  1.4 2.2 %collective-permute-start.1 = (f32[2,256]{1,0:T(2,128)}, f32[2,256]{1,0:T(2,128)S(1)}, u32[]{:S(2)}, u32[]{:S(2)}) collective-permute-start(f32[2,256]{1,0:T(2,128)} %hole.1), channel_id=1, source_target_pairs={{0,1},{1,0},{2,3},{3,2},{4,5},{5,4},{6,7},{7,6},{8,9},{9,8},{10,11... | collective-permute-start | bytes 6152 | tf_op jit(solution)/shard_map/ppermute | solution.py:47
  5.2 17.8 %collective-permute-start.2 = (bf16[2,2048,256]{2,1,0:T(8,128)(2,1)S(1)}, bf16[2,2048,256]{2,1,0:T(8,128)(2,1)S(1)}, u32[]{:S(2)}, u32[]{:S(2)}) collective-permute-start(bf16[2,2048,256]{2,1,0:T(8,128)(2,1)S(1)} %tie.3), channel_id=1, source_target_pairs={{0,1},{1,0},{2,3},{3,2},{4,5},{5,4},{6,7},{7,6},{8,9},{9,8},{10,11... | collective-permute-start | bytes 6291464 | tf_op jit(solution)/shard_map/ppermute | solution.py:47
  5.8 15.1 %collective-permute-start.5 = (bf16[512,512]{1,0:T(8,128)(2,1)S(1)}, bf16[512,512]{1,0:T(8,128)(2,1)S(1)}, u32[]{:S(2)}, u32[]{:S(2)}) collective-permute-start(bf16[512,512]{1,0:T(8,128)(2,1)S(1)} %coupling.1.refs_0_.refs_1_.refs_5_.refs_3_), channel_id=1, source_target_pairs={{0,2},{2,0},{24,26},{26,24},{32,34},{34,32},{56,58},{58,56},{6,4},... | collective-permute-start | bytes 1572872 | tf_op jit(solution)/shard_map/ppermute | solution.py:51
  8.4 12.5 %collective-permute-start.4 = (bf16[512,512]{1,0:T(8,128)(2,1)S(1)}, bf16[512,512]{1,0:T(8,128)(2,1)S(1)}, u32[]{:S(2)}, u32[]{:S(2)}) collective-permute-start(bf16[512,512]{1,0:T(8,128)(2,1)S(1)} %coupling.1.refs_0_.refs_1_.refs_5_.refs_3_), channel_id=1, source_target_pairs={{0,24},{2,26},{24,0},{26,2},{32,56},{34,58},{56,32},{58,34},{6,30}... | collective-permute-start | bytes 1572872 | tf_op jit(solution)/shard_map/ppermute | solution.py:51
  9.6 11.2 %collective-permute-start.3 = (bf16[512,512]{1,0:T(8,128)(2,1)S(1)}, bf16[512,512]{1,0:T(8,128)(2,1)S(1)}, u32[]{:S(2)}, u32[]{:S(2)}) collective-permute-start(bf16[512,512]{1,0:T(8,128)(2,1)S(1)} %coupling.1.refs_0_.refs_1_.refs_5_.refs_3_), channel_id=1, source_target_pairs={{0,32},{2,34},{24,56},{26,58},{32,0},{34,2},{56,24},{58,26},{6,38}... | collective-permute-start | bytes 1572872 | tf_op jit(solution)/shard_map/ppermute | solution.py:51
  13.4 16.0 %slice-start = ((s8[16777216]{0:T(1024)(128)(4,1)}), s8[4194304]{0:T(1024)(128)(4,1)S(1)}, s32[]{:S(2)}) async-start(s8[16777216]{0:T(1024)(128)(4,1)} %bitcast.3), calls=%async_computation | async-start | bytes 8388608
  13.4 16.0 %slice-start.1 = ((s8[16777216]{0:T(1024)(128)(4,1)}), s8[4194304]{0:T(1024)(128)(4,1)S(1)}, s32[]{:S(2)}) async-start(s8[16777216]{0:T(1024)(128)(4,1)} %bitcast.3), calls=%async_computation.1 | async-start | bytes 8388608
  18.5 10.9 %slice-start.2 = ((s8[16777216]{0:T(1024)(128)(4,1)}), s8[4194304]{0:T(1024)(128)(4,1)S(1)}, s32[]{:S(2)}) async-start(s8[16777216]{0:T(1024)(128)(4,1)} %bitcast.3), calls=%async_computation.2 | async-start | bytes 8388608
  20.9 10.3 %collective-permute-start.6 = (bf16[512,512]{1,0:T(8,128)(2,1)S(1)}, bf16[512,512]{1,0:T(8,128)(2,1)S(1)}, u32[]{:S(2)}, u32[]{:S(2)}) collective-permute-start(bf16[512,512]{1,0:T(8,128)(2,1)S(1)} %get-tuple-element.60.refs_9_.refs_7_), channel_id=1, source_target_pairs={{0,24},{2,26},{24,0},{26,2},{32,56},{34,58},{56,32},{58,34},{6,30}... | collective-permute-start | bytes 1572872 | tf_op jit(solution)/shard_map/ppermute | solution.py:51
  21.1 10.1 %collective-permute-start.7 = (bf16[512,512]{1,0:T(8,128)(2,1)S(1)}, bf16[512,512]{1,0:T(8,128)(2,1)S(1)}, u32[]{:S(2)}, u32[]{:S(2)}) collective-permute-start(bf16[512,512]{1,0:T(8,128)(2,1)S(1)} %get-tuple-element.61.refs_7_.refs_5_), channel_id=1, source_target_pairs={{0,2},{2,0},{24,26},{26,24},{32,34},{34,32},{56,58},{58,56},{6,4},... | collective-permute-start | bytes 1572872 | tf_op jit(solution)/shard_map/ppermute | solution.py:51
  21.3 9.9 %collective-permute-start.8 = (bf16[512,512]{1,0:T(8,128)(2,1)S(1)}, bf16[512,512]{1,0:T(8,128)(2,1)S(1)}, u32[]{:S(2)}, u32[]{:S(2)}) collective-permute-start(bf16[512,512]{1,0:T(8,128)(2,1)S(1)} %get-tuple-element.62.refs_6_.refs_4_), channel_id=1, source_target_pairs={{0,32},{2,34},{24,56},{26,58},{32,0},{34,2},{56,24},{58,26},{6,38}... | collective-permute-start | bytes 1572872 | tf_op jit(solution)/shard_map/ppermute | solution.py:51
  23.0 6.3 %slice-start.3 = ((s8[16777216]{0:T(1024)(128)(4,1)}), s8[4194304]{0:T(1024)(128)(4,1)S(1)}, s32[]{:S(2)}) async-start(s8[16777216]{0:T(1024)(128)(4,1)} %bitcast.3), calls=%async_computation.3 | async-start | bytes 8388608
  23.0 6.3 %copy-start = (bf16[2,2048,256]{2,1,0:T(8,128)(2,1)S(1)}, bf16[2,2048,256]{2,1,0:T(8,128)(2,1)}, u32[]{:S(2)}) copy-start(bf16[2,2048,256]{2,1,0:T(8,128)(2,1)} %drive.5) | copy-start | bytes 6291460
  23.0 6.4 %copy-start.1 = (f32[2,2048]{1,0:T(2,128)S(1)}, f32[2,2048]{1,0:T(2,128)}, u32[]{:S(2)}) copy-start(f32[2,2048]{1,0:T(2,128)} %part.3) | copy-start | bytes 49156
  25.4 7.1 %collective-permute-start.9 = (bf16[8,32,512]{2,1,0:T(8,128)(2,1)S(1)}, bf16[8,32,512]{2,1,0:T(8,128)(2,1)S(1)}, u32[]{:S(2)}, u32[]{:S(2)}) collective-permute-start(bf16[8,32,512]{2,1,0:T(8,128)(2,1)S(1)} %get-tuple-element.68), channel_id=1, source_target_pairs={{0,6},{2,4},{24,30},{26,28},{32,38},{34,36},{56,62},{58,60},{6,0},... | collective-permute-start | bytes 786440 | tf_op jit(solution)/shard_map/ppermute | solution.py:51
  25.6 13.8 %collective-permute-start.12 = (bf16[8,32,512]{2,1,0:T(8,128)(2,1)S(1)}, bf16[8,32,512]{2,1,0:T(8,128)(2,1)S(1)}, u32[]{:S(2)}, u32[]{:S(2)}) collective-permute-start(bf16[8,32,512]{2,1,0:T(8,128)(2,1)S(1)} %get-tuple-element.71), channel_id=1, source_target_pairs={{0,14},{2,12},{24,22},{26,20},{32,46},{34,44},{56,54},{58,52},{6,8... | collective-permute-start | bytes 786440 | tf_op jit(solution)/shard_map/ppermute | solution.py:51
  32.5 17.5 %collective-permute-start.13 = (bf16[512,512]{1,0:T(8,128)(2,1)S(1)}, bf16[512,512]{1,0:T(8,128)(2,1)S(1)}, u32[]{:S(2)}, u32[]{:S(2)}) collective-permute-start(bf16[512,512]{1,0:T(8,128)(2,1)S(1)} %get-tuple-element.74.refs_11_.refs_9_), channel_id=1, source_target_pairs={{0,2},{2,0},{24,26},{26,24},{32,34},{34,32},{56,58},{58,56},{6,4},... | collective-permute-start | bytes 1572872 | tf_op jit(solution)/shard_map/ppermute | solution.py:51
  34.3 11.5 %collective-permute-start.10 = (bf16[8,32,512]{2,1,0:T(8,128)(2,1)S(1)}, bf16[8,32,512]{2,1,0:T(8,128)(2,1)S(1)}, u32[]{:S(2)}, u32[]{:S(2)}) collective-permute-start(bf16[8,32,512]{2,1,0:T(8,128)(2,1)S(1)} %get-tuple-element.69), channel_id=1, source_target_pairs={{0,110},{2,108},{24,118},{26,116},{32,78},{34,76},{56,86},{58,84},... | collective-permute-start | bytes 786440 | tf_op jit(solution)/shard_map/ppermute | solution.py:51
  36.2 13.8 %collective-permute-start.11 = (bf16[8,32,512]{2,1,0:T(8,128)(2,1)S(1)}, bf16[8,32,512]{2,1,0:T(8,128)(2,1)S(1)}, u32[]{:S(2)}, u32[]{:S(2)}) collective-permute-start(bf16[8,32,512]{2,1,0:T(8,128)(2,1)S(1)} %get-tuple-element.70), channel_id=1, source_target_pairs={{0,102},{2,100},{24,126},{26,124},{32,70},{34,68},{56,94},{58,92},... | collective-permute-start | bytes 786440 | tf_op jit(solution)/shard_map/ppermute | solution.py:51
  38.4 16.0 %collective-permute-start.18 = (bf16[8,32,512]{2,1,0:T(8,128)(2,1)S(1)}, bf16[8,32,512]{2,1,0:T(8,128)(2,1)S(1)}, u32[]{:S(2)}, u32[]{:S(2)}) collective-permute-start(bf16[8,32,512]{2,1,0:T(8,128)(2,1)S(1)} %get-tuple-element.80), channel_id=1, source_target_pairs={{0,104},{2,106},{24,112},{26,114},{32,72},{34,74},{56,80},{58,82},... | collective-permute-start | bytes 786440 | tf_op jit(solution)/shard_map/ppermute | solution.py:51
  39.4 16.4 %collective-permute-start.19 = (bf16[8,32,512]{2,1,0:T(8,128)(2,1)S(1)}, bf16[8,32,512]{2,1,0:T(8,128)(2,1)S(1)}, u32[]{:S(2)}, u32[]{:S(2)}) collective-permute-start(bf16[8,32,512]{2,1,0:T(8,128)(2,1)S(1)} %get-tuple-element.81), channel_id=1, source_target_pairs={{0,8},{2,10},{24,16},{26,18},{32,40},{34,42},{56,48},{58,50},{6,14... | collective-permute-start | bytes 786440 | tf_op jit(solution)/shard_map/ppermute | solution.py:51
  45.8 11.1 %collective-permute-start.20 = (bf16[8,32,512]{2,1,0:T(8,128)(2,1)S(1)}, bf16[8,32,512]{2,1,0:T(8,128)(2,1)S(1)}, u32[]{:S(2)}, u32[]{:S(2)}) collective-permute-start(bf16[8,32,512]{2,1,0:T(8,128)(2,1)S(1)} %get-tuple-element.82), channel_id=1, source_target_pairs={{0,96},{2,98},{24,120},{26,122},{32,64},{34,66},{56,88},{58,90},{6... | collective-permute-start | bytes 786440 | tf_op jit(solution)/shard_map/ppermute | solution.py:51
  50.9 9.3 %collective-permute-start.14 = (bf16[8,32,512]{2,1,0:T(8,128)(2,1)S(1)}, bf16[8,32,512]{2,1,0:T(8,128)(2,1)S(1)}, u32[]{:S(2)}, u32[]{:S(2)}) collective-permute-start(bf16[8,32,512]{2,1,0:T(8,128)(2,1)S(1)} %get-tuple-element.76), channel_id=1, source_target_pairs={{0,110},{2,108},{24,118},{26,116},{32,78},{34,76},{56,86},{58,84},... | collective-permute-start | bytes 786440 | tf_op jit(solution)/shard_map/ppermute | solution.py:51
  51.9 10.4 %collective-permute-start.15 = (bf16[8,32,512]{2,1,0:T(8,128)(2,1)S(1)}, bf16[8,32,512]{2,1,0:T(8,128)(2,1)S(1)}, u32[]{:S(2)}, u32[]{:S(2)}) collective-permute-start(bf16[8,32,512]{2,1,0:T(8,128)(2,1)S(1)} %get-tuple-element.77), channel_id=1, source_target_pairs={{0,102},{2,100},{24,126},{26,124},{32,70},{34,68},{56,94},{58,92},... | collective-permute-start | bytes 786440 | tf_op jit(solution)/shard_map/ppermute | solution.py:51
  54.4 11.7 %collective-permute-start.16 = (bf16[8,32,512]{2,1,0:T(8,128)(2,1)S(1)}, bf16[8,32,512]{2,1,0:T(8,128)(2,1)S(1)}, u32[]{:S(2)}, u32[]{:S(2)}) collective-permute-start(bf16[8,32,512]{2,1,0:T(8,128)(2,1)S(1)} %get-tuple-element.78), channel_id=1, source_target_pairs={{0,14},{2,12},{24,22},{26,20},{32,46},{34,44},{56,54},{58,52},{6,8... | collective-permute-start | bytes 786440 | tf_op jit(solution)/shard_map/ppermute | solution.py:51
  55.8 11.8 %collective-permute-start.17 = (bf16[8,32,512]{2,1,0:T(8,128)(2,1)S(1)}, bf16[8,32,512]{2,1,0:T(8,128)(2,1)S(1)}, u32[]{:S(2)}, u32[]{:S(2)}) collective-permute-start(bf16[8,32,512]{2,1,0:T(8,128)(2,1)S(1)} %get-tuple-element.79), channel_id=1, source_target_pairs={{0,6},{2,4},{24,30},{26,28},{32,38},{34,36},{56,62},{58,60},{6,0},... | collective-permute-start | bytes 786440 | tf_op jit(solution)/shard_map/ppermute | solution.py:51
  57.7 13.1 %collective-permute-start.21 = (bf16[8,32,512]{2,1,0:T(8,128)(2,1)S(1)}, bf16[8,32,512]{2,1,0:T(8,128)(2,1)S(1)}, u32[]{:S(2)}, u32[]{:S(2)}) collective-permute-start(bf16[8,32,512]{2,1,0:T(8,128)(2,1)S(1)} %get-tuple-element.83), channel_id=1, source_target_pairs={{0,104},{2,106},{24,112},{26,114},{32,72},{34,74},{56,80},{58,82},... | collective-permute-start | bytes 786440 | tf_op jit(solution)/shard_map/ppermute | solution.py:51
  60.2 10.6 %collective-permute-start.22 = (bf16[8,32,512]{2,1,0:T(8,128)(2,1)S(1)}, bf16[8,32,512]{2,1,0:T(8,128)(2,1)S(1)}, u32[]{:S(2)}, u32[]{:S(2)}) collective-permute-start(bf16[8,32,512]{2,1,0:T(8,128)(2,1)S(1)} %get-tuple-element.84), channel_id=1, source_target_pairs={{0,8},{2,10},{24,16},{26,18},{32,40},{34,42},{56,48},{58,50},{6,14... | collective-permute-start | bytes 786440 | tf_op jit(solution)/shard_map/ppermute | solution.py:51
  62.2 10.1 %collective-permute-start.23 = (bf16[8,32,512]{2,1,0:T(8,128)(2,1)S(1)}, bf16[8,32,512]{2,1,0:T(8,128)(2,1)S(1)}, u32[]{:S(2)}, u32[]{:S(2)}) collective-permute-start(bf16[8,32,512]{2,1,0:T(8,128)(2,1)S(1)} %get-tuple-element.86), channel_id=1, source_target_pairs={{0,96},{2,98},{24,120},{26,122},{32,64},{34,66},{56,88},{58,90},{6... | collective-permute-start | bytes 786440 | tf_op jit(solution)/shard_map/ppermute | solution.py:51
  72.3 6.2 %copy-start.2 = (f32[2,256]{1,0:T(2,128)S(1)}, f32[2,256]{1,0:T(2,128)}, u32[]{:S(2)}) copy-start(f32[2,256]{1,0:T(2,128)} %hole.1) | copy-start | bytes 6148
  73.8 7.0 %collective-permute-start.24 = (bf16[2048,256]{1,0:T(8,128)(2,1)S(1)}, bf16[2048,256]{1,0:T(8,128)(2,1)S(1)}, u32[]{:S(2)}, u32[]{:S(2)}) collective-permute-start(bf16[2048,256]{1,0:T(8,128)(2,1)S(1)} %final_other.1.refs_1_), channel_id=1, source_target_pairs={{0,1},{1,0},{2,3},{3,2},{4,5},{5,4},{6,7},{7,6},{8,9},{9,8},{10,11... | collective-permute-start | bytes 3145736 | tf_op jit(solution)/shard_map/ppermute | solution.py:47

commit v5 on v4

--- a/solution.py
+++ b/solution.py
@@ -18,7 +18,7 @@
     return (PLACE[bits[0]] * 4 + PLACE[bits[1]]) * 4 + PLACE[bits[2]]
 
 
-HIGH = (1, 0, 1)
+HIGH = (0, 0, 0)
 
 
 def bits_of(core, moved, kept):
@@ -87,10 +87,10 @@
 AWAY = pl.BlockSpec(memory_space=pltpu.HBM)
 WAIT = pl.BlockSpec(memory_space=pl.ANY)
 TILES = 4
-FIRST, THEN = (1, 3), (7, 5, 6, 2, 4)
-BACK = (0, 7, 5, 3, 1), (6, 2, 4)
+FIRST, THEN = (1, 7), (2, 4, 3, 5, 6)
+BACK = (0, 7, 1, 2, 4), (3, 5, 6)
 ORDER = BACK[0] + BACK[1]
-EARLY, LATE = (range(5), range(5, 7)), range(7, 8)
+EARLY, LATE = (range(2), range(2, 5), range(5, 6)), range(6, 8)
 
 
 def tie_kernel(*refs):

time: 82.7 us -> 79.7 us (0.964)
  waiting for transfers between devices: 10.5 us -> 2.79 us
  starting transfers between devices: 40.9 us -> 44.8 us
    ppermute x21, starting transfers between devices: 34.2 us -> 42.7 us  [over(): return lax.ppermute(array, BOTH, flips(moved, kept))]
    ppermute x21, waiting for transfers between devices: 10.3 us -> 2.54 us  [over(): return lax.ppermute(array, BOTH, flips(moved, kept))]
    ppermute x4, starting transfers between devices: 6.77 us -> 2.1 us  [swap(): return lax.ppermute(array, 'dom', [(0, 1), (1, 0)])]
    pallas_call x2 -> x3, Pallas kernels: 4.68 us -> 4.47 us  [folded_call(): pl.pallas_call(functools.partial(folded_kernel, chosen), in_specs=[WHOLE]...]
  transfers between devices with their start and end apart: 25 -> 25, of which waited for: 7 -> 4; matrix products, arithmetic and copies ran while one was open for 0% -> 0% of each run, Pallas kernels for 32% -> 33%
where the time goes in v5:
time: 79.7 us; the launch traced here: 79 us
  starting transfers between devices  44.8 us (56%)
  Pallas kernels  30.9 us (39%)
  waiting for transfers between devices  2.79 us (4%)
    ppermute x21, starting transfers between devices, over(): return lax.ppermute(array, BOTH, flips(moved, kept))  42.7 us
    pallas_call x2, Pallas kernels, ladder_call(): pl.pallas_call(functools.partial(ladder_kernel, tiles), grid_spec=pltpu.P...  5.73 us
    pallas_call x1, Pallas kernels, load_call(): pl.pallas_call(load_kernel, grid_spec=pltpu.PrefetchScalarGridSpec(num_sc...  5.08 us
    pallas_call x3, Pallas kernels, folded_call(): pl.pallas_call(functools.partial(folded_kernel, chosen), in_specs=[WHOLE]...  4.47 us
    pallas_call x2, Pallas kernels, final_call(): pl.pallas_call(functools.partial(final_kernel, chosen, side), grid_spec=p...  4.04 us
    ppermute x21, waiting for transfers between devices, over(): return lax.ppermute(array, BOTH, flips(moved, kept))  2.54 us
    pallas_call x1, Pallas kernels, other_call(): pl.pallas_call(other_kernel, in_specs=[WHOLE] * 10 + [WAIT] * len(waits),...  2.33 us
    pallas_call x1, Pallas kernels, own_call(): pl.pallas_call(own_kernel, in_specs=[WHOLE, WHOLE] + [WAIT] * len(waits),...  2.33 us
  transfers between devices with their start and end apart: 25, of which 4 were waited for; matrix products, arithmetic and copies ran while one was open for 0% of the time, Pallas kernels for 33%

profile of v5, /device:TPU:1, one launch (start us, length us, event | category | flops | bytes accessed | tf_op | source)
XLA Modules:
  0.0 79.0 jit_solution(13317856905738349375)
XLA Ops:
  0.0 1.4 %collective-permute-start = (bf16[2,256,512]{2,1,0:T(8,128)(2,1)}, bf16[2,256,512]{2,1,0:T(8,128)(2,1)S(1)}, u32[]{:S(2)}, u32[]{:S(2)}) collective-permute-start(bf16[2,256,512]{2,1,0:T(8,128)(2,1)} %own.1), channel_id=1, source_target_pairs={{0,1},{1,0},{2,3},{3,2},{4,5},{5,4},{6,7},{7,6},{8,9},{9,8},{10,11... | collective-permute-start | bytes 1572872 | tf_op jit(solution)/shard_map/ppermute | solution.py:47
  1.4 0.0 collective-permute-start.1
  1.4 0.1 pad_add_fusion.sc
  1.5 2.1 %cut.1.refs_0_ = bf16[2,2048,256]{2,1,0:T(8,128)(2,1)S(1)} custom-call(s32[3]{0:T(128)S(1)} %pad_add_fusion.sc, bf16[2,2048,256]{2,1,0:T(8,128)(2,1)} %amplitudes.3, bf16[2,2048,256]{2,1,0:T(8,128)(2,1)} %drive.5), custom_call_target="tpu_custom_call" | custom-call | bytes 4194304 | tf_op jit(solution)/shard_map/cut/pallas_call | solution.py:126
  3.6 0.0 collective-permute-done.1.refs_1_.hole
  3.6 0.0 collective-permute-done.oth
  3.6 1.6 %coupling.1.refs_0_.refs_1_.refs_5_.refs_3_ = bf16[512,512]{1,0:T(8,128)(2,1)S(1)} custom-call(s32[3]{0:T(128)S(1)} %pad_add_fusion.sc, bf16[2,256,512]{2,1,0:T(8,128)(2,1)} %own.1, bf16[2,256,512]{2,1,0:T(8,128)(2,1)S(1)} %collective-permute-done.oth, bf16[2,2048,256]{2,1,0:T(8,128)(2,1)S(1)} %cut.1.refs_0_, f32[2,256]{1,0:T(2,128)S(1)} %collective-permute-done.1.refs_1_.hole), custom_call_target="tpu_custom_call" | custom-call | bytes 1048576 | tf_op jit(solution)/shard_map/coupling/pallas_call | solution.py:245
  5.2 0.6 collective-permute-start.2
  5.8 1.3 %collective-permute-start.7 = (bf16[512,512]{1,0:T(8,128)(2,1)S(1)}, bf16[512,512]{1,0:T(8,128)(2,1)S(1)}, u32[]{:S(2)}, u32[]{:S(2)}) collective-permute-start(bf16[512,512]{1,0:T(8,128)(2,1)S(1)} %coupling.1.refs_0_.refs_1_.refs_5_.refs_3_), channel_id=1, source_target_pairs={{0,6},{6,0},{24,30},{30,24},{96,102},{102,96},{120,126},{126,120},... | collective-permute-start | bytes 1572872 | tf_op jit(solution)/shard_map/ppermute | solution.py:51
  7.1 1.3 %collective-permute-start.6 = (bf16[512,512]{1,0:T(8,128)(2,1)S(1)}, bf16[512,512]{1,0:T(8,128)(2,1)S(1)}, u32[]{:S(2)}, u32[]{:S(2)}) collective-permute-start(bf16[512,512]{1,0:T(8,128)(2,1)S(1)} %coupling.1.refs_0_.refs_1_.refs_5_.refs_3_), channel_id=1, source_target_pairs={{0,24},{6,30},{24,0},{30,6},{96,120},{102,126},{120,96},{126,102},... | collective-permute-start | bytes 1572872 | tf_op jit(solution)/shard_map/ppermute | solution.py:51
  8.4 1.6 %collective-permute-start.5 = (bf16[512,512]{1,0:T(8,128)(2,1)S(1)}, bf16[512,512]{1,0:T(8,128)(2,1)S(1)}, u32[]{:S(2)}, u32[]{:S(2)}) collective-permute-start(bf16[512,512]{1,0:T(8,128)(2,1)S(1)} %coupling.1.refs_0_.refs_1_.refs_5_.refs_3_), channel_id=1, source_target_pairs={{0,96},{6,102},{24,120},{30,126},{96,0},{102,6},{120,24},{126,30},... | collective-permute-start | bytes 1572872 | tf_op jit(solution)/shard_map/ppermute | solution.py:51
  10.0 5.1 %load.1 = (bf16[2048,2048]{1,0:T(8,128)(2,1)S(1)}, bf16[2048,256]{1,0:T(8,128)(2,1)S(1)}) custom-call(s32[3]{0:T(128)S(1)} %pad_add_fusion.sc, bf16[2,2048,2048]{2,1,0:T(8,128)(2,1)} %recouple.1, bf16[2,2048,256]{2,1,0:T(8,128)(2,1)} %amplitudes.3, bf16[512,512]{1,0:T(8,128)(2,1)S(1)} %coupling.1.refs_0_.refs_1_.refs_5_.refs_3_), custom_call_target="tpu_custom_call" | custom-call | bytes 16777216 | tf_op jit(solution)/shard_map/load/pallas_call | solution.py:160
  15.1 0.0 slice-start.2
  15.1 2.3 %recoupled_own.1 = (bf16[8,32,512]{2,1,0:T(8,128)(2,1)S(1)}, bf16[8,32,512]{2,1,0:T(8,128)(2,1)S(1)}, bf16[8,32,512]{2,1,0:T(8,128)(2,1)S(1)}, bf16[8,32,512]{2,...) custom-call(bf16[2048,2048]{1,0:T(8,128)(2,1)S(1)} %get-tuple-elemen, ...), custom_call_target="tpu_custom_call" | custom-call | flops 2147483648 | bytes 8388608 | tf_op jit(solution)/shard_map/recoupled_own/pallas_call | solution.py:194
  17.5 0.0 collective-permute-done.7.refs_2_
  17.5 0.0 collective-permute-done.6.refs_1_
  17.5 0.0 collective-permute-done.5.refs_0_
  17.5 0.2 collective-permute-start.8
  17.8 0.3 collective-permute-start.9
  18.0 0.8 collective-permute-start.10
  18.8 0.0 collective-permute-done.2.pair
  18.8 2.3 %recoupled_other.1 = (bf16[8,32,512]{2,1,0:T(8,128)(2,1)S(1)}, bf16[8,32,512]{2,1,0:T(8,128)(2,1)S(1)}, bf16[8,32,512]{2,1,0:T(8,128)(2,1)S(1)}, bf16[8,32,512]{...) custom-call(bf16[2048,2048]{1,0:T(8,128)(2,1)S(1)} %get-tuple-elemen, ...), custom_call_target="tpu_custom_call", output_to_operand_aliasing={{0}: (2, {}), {1}: (3, {}), {2}: (4, {}), {3}: (5, {}), {4}... | custom-call | flops 2147483648 | bytes 2097152 | tf_op jit(solution)/shard_map/recoupled_other/pallas_call | solution.py:216
  21.1 2.6 %collective-permute-start.4 = (bf16[8,32,512]{2,1,0:T(8,128)(2,1)S(1)}, bf16[8,32,512]{2,1,0:T(8,128)(2,1)S(1)}, u32[]{:S(2)}, u32[]{:S(2)}) collective-permute-start(bf16[8,32,512]{2,1,0:T(8,128)(2,1)S(1)} %get-tuple-element.61), channel_id=1, source_target_pairs={{0,2},{6,4},{24,26},{30,28},{96,98},{102,100},{120,122},{126,124},... | collective-permute-start | bytes 786440 | tf_op jit(solution)/shard_map/ppermute | solution.py:51
  23.7 5.2 %collective-permute-start.3 = (bf16[8,32,512]{2,1,0:T(8,128)(2,1)S(1)}, bf16[8,32,512]{2,1,0:T(8,128)(2,1)S(1)}, u32[]{:S(2)}, u32[]{:S(2)}) collective-permute-start(bf16[8,32,512]{2,1,0:T(8,128)(2,1)S(1)} %get-tuple-element.60), channel_id=1, source_target_pairs={{0,42},{6,44},{24,50},{30,52},{96,74},{102,76},{120,82},{126,84},{... | collective-permute-start | bytes 786440 | tf_op jit(solution)/shard_map/ppermute | solution.py:51
  28.9 1.8 %ladder.2 = (f32[2048,512]{1,0:T(8,128)S(1)}, f32[2048,128]{1,0:T(8,128)S(1)}) custom-call(s32[3]{0:T(128)S(1)} %pad_add_fusion.sc, bf16[2,2048,2048]{2,1,0:T(8,128)(2,1)S(1)} %bitcast.4, bf16[2048,256]{1,0:T(8,128)(2,1)S(1)} %get-tuple-element.47.amp, bf16[2,2048,256]{2,1,0:T(8,128)(2,1)S(1)} %copy-done, ...), custom_call_target="tpu_custom_call" | custom-call | flops 1073741824 | bytes 4194304 | tf_op jit(solution)/shard_map/ladder/pallas_call | solution.py:299
  30.7 0.0 collective-permute-done.8.refs_0_
  30.7 0.0 collective-permute-done.9.refs_1_
  30.7 0.0 collective-permute-done.10.refs_2_
  30.7 0.0 collective-permute-done.4.refs_9_.refs_2_
  30.8 0.1 collective-permute-start.13
  30.9 1.1 %collective-permute-start.11 = (bf16[8,32,512]{2,1,0:T(8,128)(2,1)S(1)}, bf16[8,32,512]{2,1,0:T(8,128)(2,1)S(1)}, u32[]{:S(2)}, u32[]{:S(2)}) collective-permute-start(bf16[8,32,512]{2,1,0:T(8,128)(2,1)S(1)} %get-tuple-element.70), channel_id=1, source_target_pairs={{0,8},{6,14},{24,16},{30,22},{96,104},{102,110},{120,112},{126,118... | collective-permute-start | bytes 786440 | tf_op jit(solution)/shard_map/ppermute | solution.py:51
  32.0 3.2 %collective-permute-start.12 = (bf16[8,32,512]{2,1,0:T(8,128)(2,1)S(1)}, bf16[8,32,512]{2,1,0:T(8,128)(2,1)S(1)}, u32[]{:S(2)}, u32[]{:S(2)}) collective-permute-start(bf16[8,32,512]{2,1,0:T(8,128)(2,1)S(1)} %get-tuple-element.71), channel_id=1, source_target_pairs={{0,32},{6,38},{24,56},{30,62},{96,64},{102,70},{120,88},{126,94},{... | collective-permute-start | bytes 786440 | tf_op jit(solution)/shard_map/ppermute | solution.py:51
  35.1 3.2 %collective-permute-start.18 = (bf16[8,32,512]{2,1,0:T(8,128)(2,1)S(1)}, bf16[8,32,512]{2,1,0:T(8,128)(2,1)S(1)}, u32[]{:S(2)}, u32[]{:S(2)}) collective-permute-start(bf16[8,32,512]{2,1,0:T(8,128)(2,1)S(1)} %get-tuple-element.80), channel_id=1, source_target_pairs={{0,10},{6,12},{24,18},{30,20},{96,106},{102,108},{120,114},{126,11... | collective-permute-start | bytes 786440 | tf_op jit(solution)/shard_map/ppermute | solution.py:51
  38.3 0.1 collective-permute-done.3.refs_1_
  38.4 3.6 %collective-permute-start.19 = (bf16[8,32,512]{2,1,0:T(8,128)(2,1)S(1)}, bf16[8,32,512]{2,1,0:T(8,128)(2,1)S(1)}, u32[]{:S(2)}, u32[]{:S(2)}) collective-permute-start(bf16[8,32,512]{2,1,0:T(8,128)(2,1)S(1)} %get-tuple-element.81), channel_id=1, source_target_pairs={{0,34},{6,36},{24,58},{30,60},{96,66},{102,68},{120,90},{126,92},{... | collective-permute-start | bytes 786440 | tf_op jit(solution)/shard_map/ppermute | solution.py:51
  42.0 3.9 %ladder.3 = (f32[2048,512]{1,0:T(8,128)S(1)}, f32[2048,128]{1,0:T(8,128)S(1)}) custom-call(s32[3]{0:T(128)S(1)} %pad_add_fusion.sc, bf16[2,2048,2048]{2,1,0:T(8,128)(2,1)S(1)} %bitcast.4, bf16[2048,256]{1,0:T(8,128)(2,1)S(1)} %get-tuple-element.47.amp, bf16[2,2048,256]{2,1,0:T(8,128)(2,1)S(1)} %copy-done, ...), custom_call_target="tpu_custom_call", output_to_operand_aliasing={{0}: (6, {}), {1}: (7, {})} | custom-call | flops 3221225472 | bytes 4194304 | tf_op jit(solution)/shard_map/ladder/pallas_call | solution.py:299
  46.0 0.0 collective-permute-done.11.refs_3_
  46.0 3.4 %collective-permute-start.20 = (bf16[8,32,512]{2,1,0:T(8,128)(2,1)S(1)}, bf16[8,32,512]{2,1,0:T(8,128)(2,1)S(1)}, u32[]{:S(2)}, u32[]{:S(2)}) collective-permute-start(bf16[8,32,512]{2,1,0:T(8,128)(2,1)S(1)} %get-tuple-element.82), channel_id=1, source_target_pairs={{0,40},{6,46},{24,48},{30,54},{96,72},{102,78},{120,80},{126,86},{... | collective-permute-start | bytes 786440 | tf_op jit(solution)/shard_map/ppermute | solution.py:51
  49.4 0.0 collective-permute-done.12.refs_4_
  49.4 0.0 collective-permute-done.13.refs_12_.refs_10_
  49.4 0.9 %cycle.2 = (bf16[8,32,512]{2,1,0:T(8,128)(2,1)S(1)}, bf16[8,32,512]{2,1,0:T(8,128)(2,1)S(1)}, bf16[8,32,512]{2,1,0:T(8,128)(2,1)S(1)}, bf16[8,32,512]{2,1,0:T(8,128)(2,1)S(1)}, bf16[8,32,512]{2,1,0:T(8,128)(2,1)S(1)}) custom-call(bf16[8,32,512]{2,1,0:T(8,128)(2,1)S(1)} %get-tuple-element.59.refs_0_, bf16[8,32,512]{2,1,0:T(8,128)(2,1)S(1)} %collective-permute-done.3.refs_1_, ...), custom_call_target="tpu_custom_call" | custom-call | flops 671088640 | bytes 6815744 | tf_op jit(solution)/shard_map/cycle/pallas_call | solution.py:274
  50.2 2.5 %collective-permute-start.14 = (bf16[8,32,512]{2,1,0:T(8,128)(2,1)S(1)}, bf16[8,32,512]{2,1,0:T(8,128)(2,1)S(1)}, u32[]{:S(2)}, u32[]{:S(2)}) collective-permute-start(bf16[8,32,512]{2,1,0:T(8,128)(2,1)S(1)} %get-tuple-element.76), channel_id=1, source_target_pairs={{0,42},{6,44},{24,50},{30,52},{96,74},{102,76},{120,82},{126,84},{... | collective-permute-start | bytes 786440 | tf_op jit(solution)/shard_map/ppermute | solution.py:51
  52.8 1.4 %collective-permute-start.15 = (bf16[8,32,512]{2,1,0:T(8,128)(2,1)S(1)}, bf16[8,32,512]{2,1,0:T(8,128)(2,1)S(1)}, u32[]{:S(2)}, u32[]{:S(2)}) collective-permute-start(bf16[8,32,512]{2,1,0:T(8,128)(2,1)S(1)} %get-tuple-element.77), channel_id=1, source_target_pairs={{0,2},{6,4},{24,26},{30,28},{96,98},{102,100},{120,122},{126,124},... | collective-permute-start | bytes 786440 | tf_op jit(solution)/shard_map/ppermute | solution.py:51
  54.2 0.0 collective-permute-done.18.refs_0_
  54.2 1.3 %collective-permute-start.16 = (bf16[8,32,512]{2,1,0:T(8,128)(2,1)S(1)}, bf16[8,32,512]{2,1,0:T(8,128)(2,1)S(1)}, u32[]{:S(2)}, u32[]{:S(2)}) collective-permute-start(bf16[8,32,512]{2,1,0:T(8,128)(2,1)S(1)} %get-tuple-element.78), channel_id=1, source_target_pairs={{0,8},{6,14},{24,16},{30,22},{96,104},{102,110},{120,112},{126,118... | collective-permute-start | bytes 786440 | tf_op jit(solution)/shard_map/ppermute | solution.py:51
  55.5 0.0 collective-permute-done.19.refs_1_
  55.5 2.4 %collective-permute-start.17 = (bf16[8,32,512]{2,1,0:T(8,128)(2,1)S(1)}, bf16[8,32,512]{2,1,0:T(8,128)(2,1)S(1)}, u32[]{:S(2)}, u32[]{:S(2)}) collective-permute-start(bf16[8,32,512]{2,1,0:T(8,128)(2,1)S(1)} %get-tuple-element.79), channel_id=1, source_target_pairs={{0,32},{6,38},{24,56},{30,62},{96,64},{102,70},{120,88},{126,94},{... | collective-permute-start | bytes 786440 | tf_op jit(solution)/shard_map/ppermute | solution.py:51
  57.9 0.0 collective-permute-done.20.refs_2_
  57.9 0.8 %cycle.3 = (bf16[8,32,512]{2,1,0:T(8,128)(2,1)S(1)}, bf16[8,32,512]{2,1,0:T(8,128)(2,1)S(1)}, bf16[8,32,512]{2,1,0:T(8,128)(2,1)S(1)}) custom-call(bf16[8,32,512]{2,1,0:T(8,128)(2,1)S(1)} %collective-permute-done.18.refs_0_, bf16[8,32,512]{2,1,0:T(8,128)(2,1)S(1)} %collective-permute-done.19.refs_1_, ...), custom_call_target="tpu_custom_call" | custom-call | flops 402653184 | bytes 5767168 | tf_op jit(solution)/shard_map/cycle/pallas_call | solution.py:274
  58.8 2.4 %collective-permute-start.21 = (bf16[8,32,512]{2,1,0:T(8,128)(2,1)S(1)}, bf16[8,32,512]{2,1,0:T(8,128)(2,1)S(1)}, u32[]{:S(2)}, u32[]{:S(2)}) collective-permute-start(bf16[8,32,512]{2,1,0:T(8,128)(2,1)S(1)} %get-tuple-element.83), channel_id=1, source_target_pairs={{0,10},{6,12},{24,18},{30,20},{96,106},{102,108},{120,114},{126,11... | collective-permute-start | bytes 786440 | tf_op jit(solution)/shard_map/ppermute | solution.py:51
  61.1 2.4 %collective-permute-start.22 = (bf16[8,32,512]{2,1,0:T(8,128)(2,1)S(1)}, bf16[8,32,512]{2,1,0:T(8,128)(2,1)S(1)}, u32[]{:S(2)}, u32[]{:S(2)}) collective-permute-start(bf16[8,32,512]{2,1,0:T(8,128)(2,1)S(1)} %get-tuple-element.85), channel_id=1, source_target_pairs={{0,34},{6,36},{24,58},{30,60},{96,66},{102,68},{120,90},{126,92},{... | collective-permute-start | bytes 786440 | tf_op jit(solution)/shard_map/ppermute | solution.py:51
  63.6 2.5 %collective-permute-start.23 = (bf16[8,32,512]{2,1,0:T(8,128)(2,1)S(1)}, bf16[8,32,512]{2,1,0:T(8,128)(2,1)S(1)}, u32[]{:S(2)}, u32[]{:S(2)}) collective-permute-start(bf16[8,32,512]{2,1,0:T(8,128)(2,1)S(1)} %get-tuple-element.86), channel_id=1, source_target_pairs={{0,40},{6,46},{24,48},{30,54},{96,72},{102,78},{120,80},{126,86},{... | collective-permute-start | bytes 786440 | tf_op jit(solution)/shard_map/ppermute | solution.py:51
  66.0 1.5 %folded.3.ladder = f32[2048,512]{1,0:T(8,128)S(1)} custom-call(bf16[2048,2048]{1,0:T(8,128)(2,1)S(1)} %get-tuple-element.46.rows, f32[2048,512]{1,0:T(8,128)S(1)} %get-tuple-element.50.refs_13_.ladder.refs_11_, bf16[8,32,512]{2,1,0:T(8,128)(2,1)S(1)} %get-tuple-element.75.refs_0_, ...), custom_call_target="tpu_custom_call", output_to_operand_aliasing={{}: (1, {})} | custom-call | flops 1073741824 | bytes 6291456 | tf_op jit(solution)/shard_map/folded/pallas_call | solution.py:339
  67.5 0.0 collective-permute-done.16.refs_1_
  67.6 0.0 collective-permute-done.17.refs_2_
  67.6 2.1 %folded.4.ladder = f32[2048,512]{1,0:T(8,128)S(1)} custom-call(bf16[2048,2048]{1,0:T(8,128)(2,1)S(1)} %get-tuple-element.46.rows, f32[2048,512]{1,0:T(8,128)S(1)} %folded.3.ladder, bf16[8,32,512]{2,1,0:T(8,128)(2,1)S(1)} %collective-permute-done.15.refs_0_, bf16[8,32,512]{2,1,0:T(8,128)(2,1)S(1)} %collective-permute-done.16.refs_1_, ...), custom_call_target="tpu_custom_call", output_to_operand_aliasing={{}: (1, {})} | custom-call | flops 1610612736 | bytes 6291456 | tf_op jit(solution)/shard_map/folded/pallas_call | solution.py:339
  69.7 0.9 %folded.5.ladder = f32[2048,512]{1,0:T(8,128)S(1)} custom-call(bf16[2048,2048]{1,0:T(8,128)(2,1)S(1)} %get-tuple-element.46.rows, f32[2048,512]{1,0:T(8,128)S(1)} %folded.4.ladder, bf16[8,32,512]{2,1,0:T(8,128)(2,1)S(1)} %collective-permute-done.21.refs_0_), custom_call_target="tpu_custom_call", output_to_operand_aliasing={{}: (1, {})} | custom-call | flops 536870912 | bytes 6291456 | tf_op jit(solution)/shard_map/folded/pallas_call | solution.py:339
  70.5 0.4 collective-permute-done.22.refs_0_
  70.9 2.0 %collective-permute-done.23.refs_1_ = bf16[8,32,512]{2,1,0:T(8,128)(2,1)S(1)} collective-permute-done((bf16[8,32,512]{2,1,0:T(8,128)(2,1)S(1)}, bf16[8,32,512]{2,1,0:T(8,128)(2,1)S(1)}, u32[]{:S(2)}, u32[]{:S(2)}) %collective-permute-start.23) | collective-permute-done | bytes 262176 | tf_op jit(solution)/shard_map/ppermute | solution.py:51
  72.9 1.7 %final_other.1.refs_2_ = bf16[2048,256]{1,0:T(8,128)(2,1)S(1)} custom-call(s32[3]{0:T(128)S(1)} %pad_add_fusion.sc, bf16[2048,2048]{1,0:T(8,128)(2,1)S(1)} %get-tuple-element.46.rows, f32[2048,512]{1,0:T(8,128)S(1)} %folded.5.ladder, f32[2048,128]{1,0:T(8,128)S(1)} %get-tuple-element.84.part, f32[2,256]{1,0:T(2,128)S(1)} %collective-permute-done.1.refs_1_.hole, ...), custom_call_target="tpu_custom_call" | custom-call | flops 2147483648 | bytes 3145728 | tf_op jit(solution)/shard_map/final_other/pallas_call | solution.py:378
  74.6 0.1 collective-permute-start.24
  74.7 2.4 %final_own.1.given = bf16[2,2048,256]{2,1,0:T(8,128)(2,1)} custom-call(s32[3]{0:T(128)S(1)} %pad_add_fusion.sc, bf16[2048,2048]{1,0:T(8,128)(2,1)S(1)} %get-tuple-element.46.rows, f32[2048,512]{1,0:T(8,128)S(1)} %folded.5.ladder, f32[2048,128]{1,0:T(8,128)S(1)} %get-tuple-element.84.part, f32[2,256]{1,0:T(2,128)S(1)} %copy-done.2, ...), custom_call_target="tpu_custom_call" | custom-call | flops 2147483648 | bytes 3145728 | tf_op jit(solution)/shard_map/final_own/pallas_call | solution.py:378
  77.1 0.2 collective-permute-done.24.arrived
  77.3 1.5 %place.1 = bf16[2,2048,256]{2,1,0:T(8,128)(2,1)} custom-call(s32[3]{0:T(128)S(1)} %pad_add_fusion.sc, bf16[2048,256]{1,0:T(8,128)(2,1)S(1)} %collective-permute-done.24.arrived, bf16[2,2048,256]{2,1,0:T(8,128)(2,1)} %final_own.1.given), custom_call_target="tpu_custom_call", output_to_operand_aliasing={{}: (2, {})} | custom-call | bytes 2097152 | tf_op jit(solution)/shard_map/place/pallas_call | solution.py:422
  (20 shorter events, 0.0 us)
Async XLA Ops:
  0.0 3.6 %collective-permute-start = (bf16[2,256,512]{2,1,0:T(8,128)(2,1)}, bf16[2,256,512]{2,1,0:T(8,128)(2,1)S(1)}, u32[]{:S(2)}, u32[]{:S(2)}) collective-permute-start(bf16[2,256,512]{2,1,0:T(8,128)(2,1)} %own.1), channel_id=1, source_target_pairs={{0,1},{1,0},{2,3},{3,2},{4,5},{5,4},{6,7},{7,6},{8,9},{9,8},{10,11... | collective-permute-start | bytes 1572872 | tf_op jit(solution)/shard_map/ppermute | solution.py:47
  1.4 2.2 %collective-permute-start.1 = (f32[2,256]{1,0:T(2,128)}, f32[2,256]{1,0:T(2,128)S(1)}, u32[]{:S(2)}, u32[]{:S(2)}) collective-permute-start(f32[2,256]{1,0:T(2,128)} %hole.1), channel_id=1, source_target_pairs={{0,1},{1,0},{2,3},{3,2},{4,5},{5,4},{6,7},{7,6},{8,9},{9,8},{10,11... | collective-permute-start | bytes 6152 | tf_op jit(solution)/shard_map/ppermute | solution.py:47
  5.2 13.6 %collective-permute-start.2 = (bf16[2,2048,256]{2,1,0:T(8,128)(2,1)S(1)}, bf16[2,2048,256]{2,1,0:T(8,128)(2,1)S(1)}, u32[]{:S(2)}, u32[]{:S(2)}) collective-permute-start(bf16[2,2048,256]{2,1,0:T(8,128)(2,1)S(1)} %tie.3), channel_id=1, source_target_pairs={{0,1},{1,0},{2,3},{3,2},{4,5},{5,4},{6,7},{7,6},{8,9},{9,8},{10,11... | collective-permute-start | bytes 6291464 | tf_op jit(solution)/shard_map/ppermute | solution.py:47
  5.8 11.7 %collective-permute-start.7 = (bf16[512,512]{1,0:T(8,128)(2,1)S(1)}, bf16[512,512]{1,0:T(8,128)(2,1)S(1)}, u32[]{:S(2)}, u32[]{:S(2)}) collective-permute-start(bf16[512,512]{1,0:T(8,128)(2,1)S(1)} %coupling.1.refs_0_.refs_1_.refs_5_.refs_3_), channel_id=1, source_target_pairs={{0,6},{6,0},{24,30},{30,24},{96,102},{102,96},{120,126},{126,120},... | collective-permute-start | bytes 1572872 | tf_op jit(solution)/shard_map/ppermute | solution.py:51
  7.1 10.4 %collective-permute-start.6 = (bf16[512,512]{1,0:T(8,128)(2,1)S(1)}, bf16[512,512]{1,0:T(8,128)(2,1)S(1)}, u32[]{:S(2)}, u32[]{:S(2)}) collective-permute-start(bf16[512,512]{1,0:T(8,128)(2,1)S(1)} %coupling.1.refs_0_.refs_1_.refs_5_.refs_3_), channel_id=1, source_target_pairs={{0,24},{6,30},{24,0},{30,6},{96,120},{102,126},{120,96},{126,102},... | collective-permute-start | bytes 1572872 | tf_op jit(solution)/shard_map/ppermute | solution.py:51
  8.4 9.1 %collective-permute-start.5 = (bf16[512,512]{1,0:T(8,128)(2,1)S(1)}, bf16[512,512]{1,0:T(8,128)(2,1)S(1)}, u32[]{:S(2)}, u32[]{:S(2)}) collective-permute-start(bf16[512,512]{1,0:T(8,128)(2,1)S(1)} %coupling.1.refs_0_.refs_1_.refs_5_.refs_3_), channel_id=1, source_target_pairs={{0,96},{6,102},{24,120},{30,126},{96,0},{102,6},{120,24},{126,30},... | collective-permute-start | bytes 1572872 | tf_op jit(solution)/shard_map/ppermute | solution.py:51
  10.0 18.9 %slice-start = ((s8[16777216]{0:T(1024)(128)(4,1)}), s8[4194304]{0:T(1024)(128)(4,1)S(1)}, s32[]{:S(2)}) async-start(s8[16777216]{0:T(1024)(128)(4,1)} %bitcast.3), calls=%async_computation | async-start | bytes 8388608
  10.0 18.9 %slice-start.1 = ((s8[16777216]{0:T(1024)(128)(4,1)}), s8[4194304]{0:T(1024)(128)(4,1)S(1)}, s32[]{:S(2)}) async-start(s8[16777216]{0:T(1024)(128)(4,1)} %bitcast.3), calls=%async_computation.1 | async-start | bytes 8388608
  15.1 13.8 %slice-start.2 = ((s8[16777216]{0:T(1024)(128)(4,1)}), s8[4194304]{0:T(1024)(128)(4,1)S(1)}, s32[]{:S(2)}) async-start(s8[16777216]{0:T(1024)(128)(4,1)} %bitcast.3), calls=%async_computation.2 | async-start | bytes 8388608
  17.5 13.2 %collective-permute-start.8 = (bf16[512,512]{1,0:T(8,128)(2,1)S(1)}, bf16[512,512]{1,0:T(8,128)(2,1)S(1)}, u32[]{:S(2)}, u32[]{:S(2)}) collective-permute-start(bf16[512,512]{1,0:T(8,128)(2,1)S(1)} %get-tuple-element.62.refs_9_.refs_7_), channel_id=1, source_target_pairs={{0,24},{6,30},{24,0},{30,6},{96,120},{102,126},{120,96},{126,102},... | collective-permute-start | bytes 1572872 | tf_op jit(solution)/shard_map/ppermute | solution.py:51
  17.8 13.0 %collective-permute-start.9 = (bf16[512,512]{1,0:T(8,128)(2,1)S(1)}, bf16[512,512]{1,0:T(8,128)(2,1)S(1)}, u32[]{:S(2)}, u32[]{:S(2)}) collective-permute-start(bf16[512,512]{1,0:T(8,128)(2,1)S(1)} %get-tuple-element.63.refs_7_.refs_5_), channel_id=1, source_target_pairs={{0,6},{6,0},{24,30},{30,24},{96,102},{102,96},{120,126},{126,120},... | collective-permute-start | bytes 1572872 | tf_op jit(solution)/shard_map/ppermute | solution.py:51
  18.0 12.7 %collective-permute-start.10 = (bf16[512,512]{1,0:T(8,128)(2,1)S(1)}, bf16[512,512]{1,0:T(8,128)(2,1)S(1)}, u32[]{:S(2)}, u32[]{:S(2)}) collective-permute-start(bf16[512,512]{1,0:T(8,128)(2,1)S(1)} %get-tuple-element.64.refs_6_.refs_4_), channel_id=1, source_target_pairs={{0,96},{6,102},{24,120},{30,126},{96,0},{102,6},{120,24},{126,30},... | collective-permute-start | bytes 1572872 | tf_op jit(solution)/shard_map/ppermute | solution.py:51
  18.8 10.1 %slice-start.3 = ((s8[16777216]{0:T(1024)(128)(4,1)}), s8[4194304]{0:T(1024)(128)(4,1)S(1)}, s32[]{:S(2)}) async-start(s8[16777216]{0:T(1024)(128)(4,1)} %bitcast.3), calls=%async_computation.3 | async-start | bytes 8388608
  18.8 10.1 %copy-start = (bf16[2,2048,256]{2,1,0:T(8,128)(2,1)S(1)}, bf16[2,2048,256]{2,1,0:T(8,128)(2,1)}, u32[]{:S(2)}) copy-start(bf16[2,2048,256]{2,1,0:T(8,128)(2,1)} %drive.5) | copy-start | bytes 6291460
  18.8 10.1 %copy-start.1 = (f32[2,2048]{1,0:T(2,128)S(1)}, f32[2,2048]{1,0:T(2,128)}, u32[]{:S(2)}) copy-start(f32[2,2048]{1,0:T(2,128)} %part.3) | copy-start | bytes 49156
  21.1 9.6 %collective-permute-start.4 = (bf16[8,32,512]{2,1,0:T(8,128)(2,1)S(1)}, bf16[8,32,512]{2,1,0:T(8,128)(2,1)S(1)}, u32[]{:S(2)}, u32[]{:S(2)}) collective-permute-start(bf16[8,32,512]{2,1,0:T(8,128)(2,1)S(1)} %get-tuple-element.61), channel_id=1, source_target_pairs={{0,2},{6,4},{24,26},{30,28},{96,98},{102,100},{120,122},{126,124},... | collective-permute-start | bytes 786440 | tf_op jit(solution)/shard_map/ppermute | solution.py:51
  23.7 14.8 %collective-permute-start.3 = (bf16[8,32,512]{2,1,0:T(8,128)(2,1)S(1)}, bf16[8,32,512]{2,1,0:T(8,128)(2,1)S(1)}, u32[]{:S(2)}, u32[]{:S(2)}) collective-permute-start(bf16[8,32,512]{2,1,0:T(8,128)(2,1)S(1)} %get-tuple-element.60), channel_id=1, source_target_pairs={{0,42},{6,44},{24,50},{30,52},{96,74},{102,76},{120,82},{126,84},{... | collective-permute-start | bytes 786440 | tf_op jit(solution)/shard_map/ppermute | solution.py:51
  30.8 18.6 %collective-permute-start.13 = (bf16[512,512]{1,0:T(8,128)(2,1)S(1)}, bf16[512,512]{1,0:T(8,128)(2,1)S(1)}, u32[]{:S(2)}, u32[]{:S(2)}) collective-permute-start(bf16[512,512]{1,0:T(8,128)(2,1)S(1)} %get-tuple-element.74.refs_11_.refs_9_), channel_id=1, source_target_pairs={{0,6},{6,0},{24,30},{30,24},{96,102},{102,96},{120,126},{126,120},... | collective-permute-start | bytes 1572872 | tf_op jit(solution)/shard_map/ppermute | solution.py:51
  30.9 15.1 %collective-permute-start.11 = (bf16[8,32,512]{2,1,0:T(8,128)(2,1)S(1)}, bf16[8,32,512]{2,1,0:T(8,128)(2,1)S(1)}, u32[]{:S(2)}, u32[]{:S(2)}) collective-permute-start(bf16[8,32,512]{2,1,0:T(8,128)(2,1)S(1)} %get-tuple-element.70), channel_id=1, source_target_pairs={{0,8},{6,14},{24,16},{30,22},{96,104},{102,110},{120,112},{126,118... | collective-permute-start | bytes 786440 | tf_op jit(solution)/shard_map/ppermute | solution.py:51
  32.0 17.4 %collective-permute-start.12 = (bf16[8,32,512]{2,1,0:T(8,128)(2,1)S(1)}, bf16[8,32,512]{2,1,0:T(8,128)(2,1)S(1)}, u32[]{:S(2)}, u32[]{:S(2)}) collective-permute-start(bf16[8,32,512]{2,1,0:T(8,128)(2,1)S(1)} %get-tuple-element.71), channel_id=1, source_target_pairs={{0,32},{6,38},{24,56},{30,62},{96,64},{102,70},{120,88},{126,94},{... | collective-permute-start | bytes 786440 | tf_op jit(solution)/shard_map/ppermute | solution.py:51
  35.1 19.1 %collective-permute-start.18 = (bf16[8,32,512]{2,1,0:T(8,128)(2,1)S(1)}, bf16[8,32,512]{2,1,0:T(8,128)(2,1)S(1)}, u32[]{:S(2)}, u32[]{:S(2)}) collective-permute-start(bf16[8,32,512]{2,1,0:T(8,128)(2,1)S(1)} %get-tuple-element.80), channel_id=1, source_target_pairs={{0,10},{6,12},{24,18},{30,20},{96,106},{102,108},{120,114},{126,11... | collective-permute-start | bytes 786440 | tf_op jit(solution)/shard_map/ppermute | solution.py:51
  38.4 17.0 %collective-permute-start.19 = (bf16[8,32,512]{2,1,0:T(8,128)(2,1)S(1)}, bf16[8,32,512]{2,1,0:T(8,128)(2,1)S(1)}, u32[]{:S(2)}, u32[]{:S(2)}) collective-permute-start(bf16[8,32,512]{2,1,0:T(8,128)(2,1)S(1)} %get-tuple-element.81), channel_id=1, source_target_pairs={{0,34},{6,36},{24,58},{30,60},{96,66},{102,68},{120,90},{126,92},{... | collective-permute-start | bytes 786440 | tf_op jit(solution)/shard_map/ppermute | solution.py:51
  46.0 12.0 %collective-permute-start.20 = (bf16[8,32,512]{2,1,0:T(8,128)(2,1)S(1)}, bf16[8,32,512]{2,1,0:T(8,128)(2,1)S(1)}, u32[]{:S(2)}, u32[]{:S(2)}) collective-permute-start(bf16[8,32,512]{2,1,0:T(8,128)(2,1)S(1)} %get-tuple-element.82), channel_id=1, source_target_pairs={{0,40},{6,46},{24,48},{30,54},{96,72},{102,78},{120,80},{126,86},{... | collective-permute-start | bytes 786440 | tf_op jit(solution)/shard_map/ppermute | solution.py:51
  50.2 10.9 %collective-permute-start.14 = (bf16[8,32,512]{2,1,0:T(8,128)(2,1)S(1)}, bf16[8,32,512]{2,1,0:T(8,128)(2,1)S(1)}, u32[]{:S(2)}, u32[]{:S(2)}) collective-permute-start(bf16[8,32,512]{2,1,0:T(8,128)(2,1)S(1)} %get-tuple-element.76), channel_id=1, source_target_pairs={{0,42},{6,44},{24,50},{30,52},{96,74},{102,76},{120,82},{126,84},{... | collective-permute-start | bytes 786440 | tf_op jit(solution)/shard_map/ppermute | solution.py:51
  52.8 10.8 %collective-permute-start.15 = (bf16[8,32,512]{2,1,0:T(8,128)(2,1)S(1)}, bf16[8,32,512]{2,1,0:T(8,128)(2,1)S(1)}, u32[]{:S(2)}, u32[]{:S(2)}) collective-permute-start(bf16[8,32,512]{2,1,0:T(8,128)(2,1)S(1)} %get-tuple-element.77), channel_id=1, source_target_pairs={{0,2},{6,4},{24,26},{30,28},{96,98},{102,100},{120,122},{126,124},... | collective-permute-start | bytes 786440 | tf_op jit(solution)/shard_map/ppermute | solution.py:51
  54.2 13.4 %collective-permute-start.16 = (bf16[8,32,512]{2,1,0:T(8,128)(2,1)S(1)}, bf16[8,32,512]{2,1,0:T(8,128)(2,1)S(1)}, u32[]{:S(2)}, u32[]{:S(2)}) collective-permute-start(bf16[8,32,512]{2,1,0:T(8,128)(2,1)S(1)} %get-tuple-element.78), channel_id=1, source_target_pairs={{0,8},{6,14},{24,16},{30,22},{96,104},{102,110},{120,112},{126,118... | collective-permute-start | bytes 786440 | tf_op jit(solution)/shard_map/ppermute | solution.py:51
  55.5 12.1 %collective-permute-start.17 = (bf16[8,32,512]{2,1,0:T(8,128)(2,1)S(1)}, bf16[8,32,512]{2,1,0:T(8,128)(2,1)S(1)}, u32[]{:S(2)}, u32[]{:S(2)}) collective-permute-start(bf16[8,32,512]{2,1,0:T(8,128)(2,1)S(1)} %get-tuple-element.79), channel_id=1, source_target_pairs={{0,32},{6,38},{24,56},{30,62},{96,64},{102,70},{120,88},{126,94},{... | collective-permute-start | bytes 786440 | tf_op jit(solution)/shard_map/ppermute | solution.py:51
  58.8 10.9 %collective-permute-start.21 = (bf16[8,32,512]{2,1,0:T(8,128)(2,1)S(1)}, bf16[8,32,512]{2,1,0:T(8,128)(2,1)S(1)}, u32[]{:S(2)}, u32[]{:S(2)}) collective-permute-start(bf16[8,32,512]{2,1,0:T(8,128)(2,1)S(1)} %get-tuple-element.83), channel_id=1, source_target_pairs={{0,10},{6,12},{24,18},{30,20},{96,106},{102,108},{120,114},{126,11... | collective-permute-start | bytes 786440 | tf_op jit(solution)/shard_map/ppermute | solution.py:51
  61.1 9.8 %collective-permute-start.22 = (bf16[8,32,512]{2,1,0:T(8,128)(2,1)S(1)}, bf16[8,32,512]{2,1,0:T(8,128)(2,1)S(1)}, u32[]{:S(2)}, u32[]{:S(2)}) collective-permute-start(bf16[8,32,512]{2,1,0:T(8,128)(2,1)S(1)} %get-tuple-element.85), channel_id=1, source_target_pairs={{0,34},{6,36},{24,58},{30,60},{96,66},{102,68},{120,90},{126,92},{... | collective-permute-start | bytes 786440 | tf_op jit(solution)/shard_map/ppermute | solution.py:51
  63.6 9.4 %collective-permute-start.23 = (bf16[8,32,512]{2,1,0:T(8,128)(2,1)S(1)}, bf16[8,32,512]{2,1,0:T(8,128)(2,1)S(1)}, u32[]{:S(2)}, u32[]{:S(2)}) collective-permute-start(bf16[8,32,512]{2,1,0:T(8,128)(2,1)S(1)} %get-tuple-element.86), channel_id=1, source_target_pairs={{0,40},{6,46},{24,48},{30,54},{96,72},{102,78},{120,80},{126,86},{... | collective-permute-start | bytes 786440 | tf_op jit(solution)/shard_map/ppermute | solution.py:51
  72.9 1.8 %copy-start.2 = (f32[2,256]{1,0:T(2,128)S(1)}, f32[2,256]{1,0:T(2,128)}, u32[]{:S(2)}) copy-start(f32[2,256]{1,0:T(2,128)} %hole.1) | copy-start | bytes 6148
  74.6 2.7 %collective-permute-start.24 = (bf16[2048,256]{1,0:T(8,128)(2,1)S(1)}, bf16[2048,256]{1,0:T(8,128)(2,1)S(1)}, u32[]{:S(2)}, u32[]{:S(2)}) collective-permute-start(bf16[2048,256]{1,0:T(8,128)(2,1)S(1)} %final_other.1.refs_2_), channel_id=1, source_target_pairs={{0,1},{1,0},{2,3},{3,2},{4,5},{5,4},{6,7},{7,6},{8,9},{9,8},{10,11... | collective-permute-start | bytes 3145736 | tf_op jit(solution)/shard_map/ppermute | solution.py:47

commit v6 on v5

--- a/solution.py
+++ b/solution.py
@@ -88,7 +88,7 @@
 WAIT = pl.BlockSpec(memory_space=pl.ANY)
 TILES = 4
 FIRST, THEN = (1, 7), (2, 4, 3, 5, 6)
-BACK = (0, 7, 1, 2, 4), (3, 5, 6)
+BACK = (0, 1, 2, 4, 7), (3, 5, 6)
 ORDER = BACK[0] + BACK[1]
 EARLY, LATE = (range(2), range(2, 5), range(5, 6)), range(6, 8)
 

time: 79.7 us -> 79.3 us (level)
  no operation moved by 1% of the time
where the time goes in v6:
time: 79.3 us; the launch traced here: 79.1 us
  starting transfers between devices  44.7 us (56%)
  Pallas kernels  30.9 us (39%)
  waiting for transfers between devices  2.94 us (4%)
    ppermute x21, starting transfers between devices, over(): return lax.ppermute(array, BOTH, flips(moved, kept))  42.6 us
    pallas_call x2, Pallas kernels, ladder_call(): pl.pallas_call(functools.partial(ladder_kernel, tiles), grid_spec=pltpu.P...  5.73 us
    pallas_call x1, Pallas kernels, load_call(): pl.pallas_call(load_kernel, grid_spec=pltpu.PrefetchScalarGridSpec(num_sc...  5.08 us
    pallas_call x3, Pallas kernels, folded_call(): pl.pallas_call(functools.partial(folded_kernel, chosen), in_specs=[WHOLE]...  4.47 us
    pallas_call x2, Pallas kernels, final_call(): pl.pallas_call(functools.partial(final_kernel, chosen, side), grid_spec=p...  4.05 us
    ppermute x21, waiting for transfers between devices, over(): return lax.ppermute(array, BOTH, flips(moved, kept))  2.7 us
    pallas_call x1, Pallas kernels, other_call(): pl.pallas_call(other_kernel, in_specs=[WHOLE] * 10 + [WAIT] * len(waits),...  2.33 us
    pallas_call x1, Pallas kernels, own_call(): pl.pallas_call(own_kernel, in_specs=[WHOLE, WHOLE] + [WAIT] * len(waits),...  2.33 us
  transfers between devices with their start and end apart: 25, of which 4 were waited for; matrix products, arithmetic and copies ran while one was open for 0% of the time, Pallas kernels for 33%

profile of v6, /device:TPU:1, one launch (start us, length us, event | category | flops | bytes accessed | tf_op | source)
XLA Modules:
  0.0 79.1 jit_solution(10909824508228703809)
XLA Ops:
  0.0 1.4 %collective-permute-start = (bf16[2,256,512]{2,1,0:T(8,128)(2,1)}, bf16[2,256,512]{2,1,0:T(8,128)(2,1)S(1)}, u32[]{:S(2)}, u32[]{:S(2)}) collective-permute-start(bf16[2,256,512]{2,1,0:T(8,128)(2,1)} %own.1), channel_id=1, source_target_pairs={{0,1},{1,0},{2,3},{3,2},{4,5},{5,4},{6,7},{7,6},{8,9},{9,8},{10,11... | collective-permute-start | bytes 1572872 | tf_op jit(solution)/shard_map/ppermute | solution.py:47
  1.4 0.0 collective-permute-start.1
  1.4 0.1 pad_add_fusion.sc
  1.5 2.1 %cut.1.refs_0_ = bf16[2,2048,256]{2,1,0:T(8,128)(2,1)S(1)} custom-call(s32[3]{0:T(128)S(1)} %pad_add_fusion.sc, bf16[2,2048,256]{2,1,0:T(8,128)(2,1)} %amplitudes.3, bf16[2,2048,256]{2,1,0:T(8,128)(2,1)} %drive.5), custom_call_target="tpu_custom_call" | custom-call | bytes 4194304 | tf_op jit(solution)/shard_map/cut/pallas_call | solution.py:126
  3.6 0.0 collective-permute-done.1.refs_1_.hole
  3.6 0.0 collective-permute-done.oth
  3.6 1.6 %coupling.1.refs_0_.refs_1_.refs_5_.refs_3_ = bf16[512,512]{1,0:T(8,128)(2,1)S(1)} custom-call(s32[3]{0:T(128)S(1)} %pad_add_fusion.sc, bf16[2,256,512]{2,1,0:T(8,128)(2,1)} %own.1, bf16[2,256,512]{2,1,0:T(8,128)(2,1)S(1)} %collective-permute-done.oth, bf16[2,2048,256]{2,1,0:T(8,128)(2,1)S(1)} %cut.1.refs_0_, f32[2,256]{1,0:T(2,128)S(1)} %collective-permute-done.1.refs_1_.hole), custom_call_target="tpu_custom_call" | custom-call | bytes 1048576 | tf_op jit(solution)/shard_map/coupling/pallas_call | solution.py:245
  5.2 0.6 collective-permute-start.2
  5.8 1.3 %collective-permute-start.6 = (bf16[512,512]{1,0:T(8,128)(2,1)S(1)}, bf16[512,512]{1,0:T(8,128)(2,1)S(1)}, u32[]{:S(2)}, u32[]{:S(2)}) collective-permute-start(bf16[512,512]{1,0:T(8,128)(2,1)S(1)} %coupling.1.refs_0_.refs_1_.refs_5_.refs_3_), channel_id=1, source_target_pairs={{0,6},{6,0},{24,30},{30,24},{96,102},{102,96},{120,126},{126,120},... | collective-permute-start | bytes 1572872 | tf_op jit(solution)/shard_map/ppermute | solution.py:51
  7.1 1.3 %collective-permute-start.5 = (bf16[512,512]{1,0:T(8,128)(2,1)S(1)}, bf16[512,512]{1,0:T(8,128)(2,1)S(1)}, u32[]{:S(2)}, u32[]{:S(2)}) collective-permute-start(bf16[512,512]{1,0:T(8,128)(2,1)S(1)} %coupling.1.refs_0_.refs_1_.refs_5_.refs_3_), channel_id=1, source_target_pairs={{0,24},{6,30},{24,0},{30,6},{96,120},{102,126},{120,96},{126,102},... | collective-permute-start | bytes 1572872 | tf_op jit(solution)/shard_map/ppermute | solution.py:51
  8.4 1.6 %collective-permute-start.4 = (bf16[512,512]{1,0:T(8,128)(2,1)S(1)}, bf16[512,512]{1,0:T(8,128)(2,1)S(1)}, u32[]{:S(2)}, u32[]{:S(2)}) collective-permute-start(bf16[512,512]{1,0:T(8,128)(2,1)S(1)} %coupling.1.refs_0_.refs_1_.refs_5_.refs_3_), channel_id=1, source_target_pairs={{0,96},{6,102},{24,120},{30,126},{96,0},{102,6},{120,24},{126,30},... | collective-permute-start | bytes 1572872 | tf_op jit(solution)/shard_map/ppermute | solution.py:51
  10.0 5.1 %load.1 = (bf16[2048,2048]{1,0:T(8,128)(2,1)S(1)}, bf16[2048,256]{1,0:T(8,128)(2,1)S(1)}) custom-call(s32[3]{0:T(128)S(1)} %pad_add_fusion.sc, bf16[2,2048,2048]{2,1,0:T(8,128)(2,1)} %recouple.1, bf16[2,2048,256]{2,1,0:T(8,128)(2,1)} %amplitudes.3, bf16[512,512]{1,0:T(8,128)(2,1)S(1)} %coupling.1.refs_0_.refs_1_.refs_5_.refs_3_), custom_call_target="tpu_custom_call" | custom-call | bytes 16777216 | tf_op jit(solution)/shard_map/load/pallas_call | solution.py:160
  15.1 0.0 slice-start.2
  15.1 2.3 %recoupled_own.1 = (bf16[8,32,512]{2,1,0:T(8,128)(2,1)S(1)}, bf16[8,32,512]{2,1,0:T(8,128)(2,1)S(1)}, bf16[8,32,512]{2,1,0:T(8,128)(2,1)S(1)}, bf16[8,32,512]{2,...) custom-call(bf16[2048,2048]{1,0:T(8,128)(2,1)S(1)} %get-tuple-elemen, ...), custom_call_target="tpu_custom_call" | custom-call | flops 2147483648 | bytes 8388608 | tf_op jit(solution)/shard_map/recoupled_own/pallas_call | solution.py:194
  17.5 0.0 collective-permute-done.6.refs_2_
  17.5 0.0 collective-permute-done.5.refs_1_
  17.5 0.0 collective-permute-done.4.refs_0_
  17.5 0.2 collective-permute-start.7
  17.8 0.3 collective-permute-start.8
  18.0 0.8 collective-permute-start.9
  18.8 0.0 collective-permute-done.2.pair
  18.8 2.3 %recoupled_other.1 = (bf16[8,32,512]{2,1,0:T(8,128)(2,1)S(1)}, bf16[8,32,512]{2,1,0:T(8,128)(2,1)S(1)}, bf16[8,32,512]{2,1,0:T(8,128)(2,1)S(1)}, bf16[8,32,512]{...) custom-call(bf16[2048,2048]{1,0:T(8,128)(2,1)S(1)} %get-tuple-elemen, ...), custom_call_target="tpu_custom_call", output_to_operand_aliasing={{0}: (2, {}), {1}: (3, {}), {2}: (4, {}), {3}: (5, {}), {4}... | custom-call | flops 2147483648 | bytes 2097152 | tf_op jit(solution)/shard_map/recoupled_other/pallas_call | solution.py:216
  21.1 2.6 %collective-permute-start.3 = (bf16[8,32,512]{2,1,0:T(8,128)(2,1)S(1)}, bf16[8,32,512]{2,1,0:T(8,128)(2,1)S(1)}, u32[]{:S(2)}, u32[]{:S(2)}) collective-permute-start(bf16[8,32,512]{2,1,0:T(8,128)(2,1)S(1)} %get-tuple-element.60), channel_id=1, source_target_pairs={{0,2},{6,4},{24,26},{30,28},{96,98},{102,100},{120,122},{126,124},... | collective-permute-start | bytes 786440 | tf_op jit(solution)/shard_map/ppermute | solution.py:51
  23.7 5.2 %collective-permute-start.12 = (bf16[8,32,512]{2,1,0:T(8,128)(2,1)S(1)}, bf16[8,32,512]{2,1,0:T(8,128)(2,1)S(1)}, u32[]{:S(2)}, u32[]{:S(2)}) collective-permute-start(bf16[8,32,512]{2,1,0:T(8,128)(2,1)S(1)} %get-tuple-element.71), channel_id=1, source_target_pairs={{0,42},{6,44},{24,50},{30,52},{96,74},{102,76},{120,82},{126,84},{... | collective-permute-start | bytes 786440 | tf_op jit(solution)/shard_map/ppermute | solution.py:51
  28.9 1.8 %ladder.2 = (f32[2048,512]{1,0:T(8,128)S(1)}, f32[2048,128]{1,0:T(8,128)S(1)}) custom-call(s32[3]{0:T(128)S(1)} %pad_add_fusion.sc, bf16[2,2048,2048]{2,1,0:T(8,128)(2,1)S(1)} %bitcast.4, bf16[2048,256]{1,0:T(8,128)(2,1)S(1)} %get-tuple-element.47.amp, bf16[2,2048,256]{2,1,0:T(8,128)(2,1)S(1)} %copy-done, ...), custom_call_target="tpu_custom_call" | custom-call | flops 1073741824 | bytes 4194304 | tf_op jit(solution)/shard_map/ladder/pallas_call | solution.py:299
  30.7 0.0 collective-permute-done.7.refs_0_
  30.7 0.0 collective-permute-done.8.refs_1_
  30.7 0.0 collective-permute-done.9.refs_2_
  30.7 0.0 collective-permute-done.3.refs_9_.refs_1_
  30.8 0.1 collective-permute-start.13
  30.9 1.1 %collective-permute-start.10 = (bf16[8,32,512]{2,1,0:T(8,128)(2,1)S(1)}, bf16[8,32,512]{2,1,0:T(8,128)(2,1)S(1)}, u32[]{:S(2)}, u32[]{:S(2)}) collective-permute-start(bf16[8,32,512]{2,1,0:T(8,128)(2,1)S(1)} %get-tuple-element.69), channel_id=1, source_target_pairs={{0,8},{6,14},{24,16},{30,22},{96,104},{102,110},{120,112},{126,118... | collective-permute-start | bytes 786440 | tf_op jit(solution)/shard_map/ppermute | solution.py:51
  32.0 3.2 %collective-permute-start.11 = (bf16[8,32,512]{2,1,0:T(8,128)(2,1)S(1)}, bf16[8,32,512]{2,1,0:T(8,128)(2,1)S(1)}, u32[]{:S(2)}, u32[]{:S(2)}) collective-permute-start(bf16[8,32,512]{2,1,0:T(8,128)(2,1)S(1)} %get-tuple-element.70), channel_id=1, source_target_pairs={{0,32},{6,38},{24,56},{30,62},{96,64},{102,70},{120,88},{126,94},{... | collective-permute-start | bytes 786440 | tf_op jit(solution)/shard_map/ppermute | solution.py:51
  35.1 3.2 %collective-permute-start.18 = (bf16[8,32,512]{2,1,0:T(8,128)(2,1)S(1)}, bf16[8,32,512]{2,1,0:T(8,128)(2,1)S(1)}, u32[]{:S(2)}, u32[]{:S(2)}) collective-permute-start(bf16[8,32,512]{2,1,0:T(8,128)(2,1)S(1)} %get-tuple-element.80), channel_id=1, source_target_pairs={{0,10},{6,12},{24,18},{30,20},{96,106},{102,108},{120,114},{126,11... | collective-permute-start | bytes 786440 | tf_op jit(solution)/shard_map/ppermute | solution.py:51
  38.3 0.1 collective-permute-done.12.refs_4_
  38.4 3.6 %collective-permute-start.19 = (bf16[8,32,512]{2,1,0:T(8,128)(2,1)S(1)}, bf16[8,32,512]{2,1,0:T(8,128)(2,1)S(1)}, u32[]{:S(2)}, u32[]{:S(2)}) collective-permute-start(bf16[8,32,512]{2,1,0:T(8,128)(2,1)S(1)} %get-tuple-element.81), channel_id=1, source_target_pairs={{0,34},{6,36},{24,58},{30,60},{96,66},{102,68},{120,90},{126,92},{... | collective-permute-start | bytes 786440 | tf_op jit(solution)/shard_map/ppermute | solution.py:51
  42.0 3.9 %ladder.3 = (f32[2048,512]{1,0:T(8,128)S(1)}, f32[2048,128]{1,0:T(8,128)S(1)}) custom-call(s32[3]{0:T(128)S(1)} %pad_add_fusion.sc, bf16[2,2048,2048]{2,1,0:T(8,128)(2,1)S(1)} %bitcast.4, bf16[2048,256]{1,0:T(8,128)(2,1)S(1)} %get-tuple-element.47.amp, bf16[2,2048,256]{2,1,0:T(8,128)(2,1)S(1)} %copy-done, ...), custom_call_target="tpu_custom_call", output_to_operand_aliasing={{0}: (6, {}), {1}: (7, {})} | custom-call | flops 3221225472 | bytes 4194304 | tf_op jit(solution)/shard_map/ladder/pallas_call | solution.py:299
  46.0 0.0 collective-permute-done.10.refs_2_
  46.0 3.4 %collective-permute-start.20 = (bf16[8,32,512]{2,1,0:T(8,128)(2,1)S(1)}, bf16[8,32,512]{2,1,0:T(8,128)(2,1)S(1)}, u32[]{:S(2)}, u32[]{:S(2)}) collective-permute-start(bf16[8,32,512]{2,1,0:T(8,128)(2,1)S(1)} %get-tuple-element.82), channel_id=1, source_target_pairs={{0,40},{6,46},{24,48},{30,54},{96,72},{102,78},{120,80},{126,86},{... | collective-permute-start | bytes 786440 | tf_op jit(solution)/shard_map/ppermute | solution.py:51
  49.4 0.0 collective-permute-done.11.refs_3_
  49.4 0.0 collective-permute-done.13.refs_12_.refs_10_
  49.4 0.9 %cycle.2 = (bf16[8,32,512]{2,1,0:T(8,128)(2,1)S(1)}, bf16[8,32,512]{2,1,0:T(8,128)(2,1)S(1)}, bf16[8,32,512]{2,1,0:T(8,128)(2,1)S(1)}, bf16[8,32,512]{2,1,0:T(8,128)(2,1)S(1)}, bf16[8,32,512]{2,1,0:T(8,128)(2,1)S(1)}) custom-call(bf16[8,32,512]{2,1,0:T(8,128)(2,1)S(1)} %get-tuple-element.59.refs_0_, ...), custom_call_target="tpu_custom_call" | custom-call | flops 671088640 | bytes 6815744 | tf_op jit(solution)/shard_map/cycle/pallas_call | solution.py:274
  50.2 0.5 collective-permute-start.14
  50.7 2.4 %collective-permute-start.15 = (bf16[8,32,512]{2,1,0:T(8,128)(2,1)S(1)}, bf16[8,32,512]{2,1,0:T(8,128)(2,1)S(1)}, u32[]{:S(2)}, u32[]{:S(2)}) collective-permute-start(bf16[8,32,512]{2,1,0:T(8,128)(2,1)S(1)} %get-tuple-element.77), channel_id=1, source_target_pairs={{0,8},{6,14},{24,16},{30,22},{96,104},{102,110},{120,112},{126,118... | collective-permute-start | bytes 786440 | tf_op jit(solution)/shard_map/ppermute | solution.py:51
  53.2 0.0 collective-permute-done.18.refs_0_
  53.2 0.2 collective-permute-start.16
  53.4 0.0 collective-permute-done.19.refs_1_
  53.4 4.5 %collective-permute-start.17 = (bf16[8,32,512]{2,1,0:T(8,128)(2,1)S(1)}, bf16[8,32,512]{2,1,0:T(8,128)(2,1)S(1)}, u32[]{:S(2)}, u32[]{:S(2)}) collective-permute-start(bf16[8,32,512]{2,1,0:T(8,128)(2,1)S(1)} %get-tuple-element.79), channel_id=1, source_target_pairs={{0,42},{6,44},{24,50},{30,52},{96,74},{102,76},{120,82},{126,84},{... | collective-permute-start | bytes 786440 | tf_op jit(solution)/shard_map/ppermute | solution.py:51
  57.9 0.0 collective-permute-done.20.refs_2_
  57.9 0.8 %cycle.3 = (bf16[8,32,512]{2,1,0:T(8,128)(2,1)S(1)}, bf16[8,32,512]{2,1,0:T(8,128)(2,1)S(1)}, bf16[8,32,512]{2,1,0:T(8,128)(2,1)S(1)}) custom-call(bf16[8,32,512]{2,1,0:T(8,128)(2,1)S(1)} %collective-permute-done.18.refs_0_, bf16[8,32,512]{2,1,0:T(8,128)(2,1)S(1)} %collective-permute-done.19.refs_1_, ...), custom_call_target="tpu_custom_call" | custom-call | flops 402653184 | bytes 5767168 | tf_op jit(solution)/shard_map/cycle/pallas_call | solution.py:274
  58.7 2.6 %collective-permute-start.21 = (bf16[8,32,512]{2,1,0:T(8,128)(2,1)S(1)}, bf16[8,32,512]{2,1,0:T(8,128)(2,1)S(1)}, u32[]{:S(2)}, u32[]{:S(2)}) collective-permute-start(bf16[8,32,512]{2,1,0:T(8,128)(2,1)S(1)} %get-tuple-element.83), channel_id=1, source_target_pairs={{0,10},{6,12},{24,18},{30,20},{96,106},{102,108},{120,114},{126,11... | collective-permute-start | bytes 786440 | tf_op jit(solution)/shard_map/ppermute | solution.py:51
  61.2 2.4 %collective-permute-start.22 = (bf16[8,32,512]{2,1,0:T(8,128)(2,1)S(1)}, bf16[8,32,512]{2,1,0:T(8,128)(2,1)S(1)}, u32[]{:S(2)}, u32[]{:S(2)}) collective-permute-start(bf16[8,32,512]{2,1,0:T(8,128)(2,1)S(1)} %get-tuple-element.85), channel_id=1, source_target_pairs={{0,34},{6,36},{24,58},{30,60},{96,66},{102,68},{120,90},{126,92},{... | collective-permute-start | bytes 786440 | tf_op jit(solution)/shard_map/ppermute | solution.py:51
  63.6 2.3 %collective-permute-start.23 = (bf16[8,32,512]{2,1,0:T(8,128)(2,1)S(1)}, bf16[8,32,512]{2,1,0:T(8,128)(2,1)S(1)}, u32[]{:S(2)}, u32[]{:S(2)}) collective-permute-start(bf16[8,32,512]{2,1,0:T(8,128)(2,1)S(1)} %get-tuple-element.86), channel_id=1, source_target_pairs={{0,40},{6,46},{24,48},{30,54},{96,72},{102,78},{120,80},{126,86},{... | collective-permute-start | bytes 786440 | tf_op jit(solution)/shard_map/ppermute | solution.py:51
  65.9 1.5 %folded.3.ladder = f32[2048,512]{1,0:T(8,128)S(1)} custom-call(bf16[2048,2048]{1,0:T(8,128)(2,1)S(1)} %get-tuple-element.46.rows, f32[2048,512]{1,0:T(8,128)S(1)} %get-tuple-element.50.refs_13_.ladder.refs_11_, bf16[8,32,512]{2,1,0:T(8,128)(2,1)S(1)} %get-tuple-element.75.refs_0_, ...), custom_call_target="tpu_custom_call", output_to_operand_aliasing={{}: (1, {})} | custom-call | flops 1073741824 | bytes 6291456 | tf_op jit(solution)/shard_map/folded/pallas_call | solution.py:339
  67.5 0.0 collective-permute-done.16.refs_1_
  67.5 2.1 %folded.4.ladder = f32[2048,512]{1,0:T(8,128)S(1)} custom-call(bf16[2048,2048]{1,0:T(8,128)(2,1)S(1)} %get-tuple-element.46.rows, f32[2048,512]{1,0:T(8,128)S(1)} %folded.3.ladder, bf16[8,32,512]{2,1,0:T(8,128)(2,1)S(1)} %collective-permute-done.15.refs_0_, bf16[8,32,512]{2,1,0:T(8,128)(2,1)S(1)} %collective-permute-done.16.refs_1_, ...), custom_call_target="tpu_custom_call", output_to_operand_aliasing={{}: (1, {})} | custom-call | flops 1610612736 | bytes 6291456 | tf_op jit(solution)/shard_map/folded/pallas_call | solution.py:339
  69.6 0.0 collective-permute-done.21.refs_0_
  69.6 0.9 %folded.5.ladder = f32[2048,512]{1,0:T(8,128)S(1)} custom-call(bf16[2048,2048]{1,0:T(8,128)(2,1)S(1)} %get-tuple-element.46.rows, f32[2048,512]{1,0:T(8,128)S(1)} %folded.4.ladder, bf16[8,32,512]{2,1,0:T(8,128)(2,1)S(1)} %collective-permute-done.21.refs_0_), custom_call_target="tpu_custom_call", output_to_operand_aliasing={{}: (1, {})} | custom-call | flops 536870912 | bytes 6291456 | tf_op jit(solution)/shard_map/folded/pallas_call | solution.py:339
  70.5 0.5 collective-permute-done.22.refs_0_
  71.0 2.0 %collective-permute-done.23.refs_1_ = bf16[8,32,512]{2,1,0:T(8,128)(2,1)S(1)} collective-permute-done((bf16[8,32,512]{2,1,0:T(8,128)(2,1)S(1)}, bf16[8,32,512]{2,1,0:T(8,128)(2,1)S(1)}, u32[]{:S(2)}, u32[]{:S(2)}) %collective-permute-start.23) | collective-permute-done | bytes 262176 | tf_op jit(solution)/shard_map/ppermute | solution.py:51
  73.0 1.7 %final_other.1.refs_2_ = bf16[2048,256]{1,0:T(8,128)(2,1)S(1)} custom-call(s32[3]{0:T(128)S(1)} %pad_add_fusion.sc, bf16[2048,2048]{1,0:T(8,128)(2,1)S(1)} %get-tuple-element.46.rows, f32[2048,512]{1,0:T(8,128)S(1)} %folded.5.ladder, f32[2048,128]{1,0:T(8,128)S(1)} %get-tuple-element.84.part, f32[2,256]{1,0:T(2,128)S(1)} %collective-permute-done.1.refs_1_.hole, ...), custom_call_target="tpu_custom_call" | custom-call | flops 2147483648 | bytes 3145728 | tf_op jit(solution)/shard_map/final_other/pallas_call | solution.py:378
  74.7 0.1 collective-permute-start.24
  74.8 2.4 %final_own.1.given = bf16[2,2048,256]{2,1,0:T(8,128)(2,1)} custom-call(s32[3]{0:T(128)S(1)} %pad_add_fusion.sc, bf16[2048,2048]{1,0:T(8,128)(2,1)S(1)} %get-tuple-element.46.rows, f32[2048,512]{1,0:T(8,128)S(1)} %folded.5.ladder, f32[2048,128]{1,0:T(8,128)S(1)} %get-tuple-element.84.part, f32[2,256]{1,0:T(2,128)S(1)} %copy-done.2, ...), custom_call_target="tpu_custom_call" | custom-call | flops 2147483648 | bytes 3145728 | tf_op jit(solution)/shard_map/final_own/pallas_call | solution.py:378
  77.2 0.2 collective-permute-done.24.arrived
  77.4 1.5 %place.1 = bf16[2,2048,256]{2,1,0:T(8,128)(2,1)} custom-call(s32[3]{0:T(128)S(1)} %pad_add_fusion.sc, bf16[2048,256]{1,0:T(8,128)(2,1)S(1)} %collective-permute-done.24.arrived, bf16[2,2048,256]{2,1,0:T(8,128)(2,1)} %final_own.1.given), custom_call_target="tpu_custom_call", output_to_operand_aliasing={{}: (2, {})} | custom-call | bytes 2097152 | tf_op jit(solution)/shard_map/place/pallas_call | solution.py:422
  (20 shorter events, 0.0 us)
Async XLA Ops:
  0.0 3.6 %collective-permute-start = (bf16[2,256,512]{2,1,0:T(8,128)(2,1)}, bf16[2,256,512]{2,1,0:T(8,128)(2,1)S(1)}, u32[]{:S(2)}, u32[]{:S(2)}) collective-permute-start(bf16[2,256,512]{2,1,0:T(8,128)(2,1)} %own.1), channel_id=1, source_target_pairs={{0,1},{1,0},{2,3},{3,2},{4,5},{5,4},{6,7},{7,6},{8,9},{9,8},{10,11... | collective-permute-start | bytes 1572872 | tf_op jit(solution)/shard_map/ppermute | solution.py:47
  1.4 2.2 %collective-permute-start.1 = (f32[2,256]{1,0:T(2,128)}, f32[2,256]{1,0:T(2,128)S(1)}, u32[]{:S(2)}, u32[]{:S(2)}) collective-permute-start(f32[2,256]{1,0:T(2,128)} %hole.1), channel_id=1, source_target_pairs={{0,1},{1,0},{2,3},{3,2},{4,5},{5,4},{6,7},{7,6},{8,9},{9,8},{10,11... | collective-permute-start | bytes 6152 | tf_op jit(solution)/shard_map/ppermute | solution.py:47
  5.2 13.6 %collective-permute-start.2 = (bf16[2,2048,256]{2,1,0:T(8,128)(2,1)S(1)}, bf16[2,2048,256]{2,1,0:T(8,128)(2,1)S(1)}, u32[]{:S(2)}, u32[]{:S(2)}) collective-permute-start(bf16[2,2048,256]{2,1,0:T(8,128)(2,1)S(1)} %tie.3), channel_id=1, source_target_pairs={{0,1},{1,0},{2,3},{3,2},{4,5},{5,4},{6,7},{7,6},{8,9},{9,8},{10,11... | collective-permute-start | bytes 6291464 | tf_op jit(solution)/shard_map/ppermute | solution.py:47
  5.8 11.7 %collective-permute-start.6 = (bf16[512,512]{1,0:T(8,128)(2,1)S(1)}, bf16[512,512]{1,0:T(8,128)(2,1)S(1)}, u32[]{:S(2)}, u32[]{:S(2)}) collective-permute-start(bf16[512,512]{1,0:T(8,128)(2,1)S(1)} %coupling.1.refs_0_.refs_1_.refs_5_.refs_3_), channel_id=1, source_target_pairs={{0,6},{6,0},{24,30},{30,24},{96,102},{102,96},{120,126},{126,120},... | collective-permute-start | bytes 1572872 | tf_op jit(solution)/shard_map/ppermute | solution.py:51
  7.1 10.4 %collective-permute-start.5 = (bf16[512,512]{1,0:T(8,128)(2,1)S(1)}, bf16[512,512]{1,0:T(8,128)(2,1)S(1)}, u32[]{:S(2)}, u32[]{:S(2)}) collective-permute-start(bf16[512,512]{1,0:T(8,128)(2,1)S(1)} %coupling.1.refs_0_.refs_1_.refs_5_.refs_3_), channel_id=1, source_target_pairs={{0,24},{6,30},{24,0},{30,6},{96,120},{102,126},{120,96},{126,102},... | collective-permute-start | bytes 1572872 | tf_op jit(solution)/shard_map/ppermute | solution.py:51
  8.4 9.1 %collective-permute-start.4 = (bf16[512,512]{1,0:T(8,128)(2,1)S(1)}, bf16[512,512]{1,0:T(8,128)(2,1)S(1)}, u32[]{:S(2)}, u32[]{:S(2)}) collective-permute-start(bf16[512,512]{1,0:T(8,128)(2,1)S(1)} %coupling.1.refs_0_.refs_1_.refs_5_.refs_3_), channel_id=1, source_target_pairs={{0,96},{6,102},{24,120},{30,126},{96,0},{102,6},{120,24},{126,30},... | collective-permute-start | bytes 1572872 | tf_op jit(solution)/shard_map/ppermute | solution.py:51
  10.0 18.9 %slice-start = ((s8[16777216]{0:T(1024)(128)(4,1)}), s8[4194304]{0:T(1024)(128)(4,1)S(1)}, s32[]{:S(2)}) async-start(s8[16777216]{0:T(1024)(128)(4,1)} %bitcast.3), calls=%async_computation | async-start | bytes 8388608
  10.0 18.9 %slice-start.1 = ((s8[16777216]{0:T(1024)(128)(4,1)}), s8[4194304]{0:T(1024)(128)(4,1)S(1)}, s32[]{:S(2)}) async-start(s8[16777216]{0:T(1024)(128)(4,1)} %bitcast.3), calls=%async_computation.1 | async-start | bytes 8388608
  15.1 13.8 %slice-start.2 = ((s8[16777216]{0:T(1024)(128)(4,1)}), s8[4194304]{0:T(1024)(128)(4,1)S(1)}, s32[]{:S(2)}) async-start(s8[16777216]{0:T(1024)(128)(4,1)} %bitcast.3), calls=%async_computation.2 | async-start | bytes 8388608
  17.5 13.2 %collective-permute-start.7 = (bf16[512,512]{1,0:T(8,128)(2,1)S(1)}, bf16[512,512]{1,0:T(8,128)(2,1)S(1)}, u32[]{:S(2)}, u32[]{:S(2)}) collective-permute-start(bf16[512,512]{1,0:T(8,128)(2,1)S(1)} %get-tuple-element.61.refs_9_.refs_7_), channel_id=1, source_target_pairs={{0,24},{6,30},{24,0},{30,6},{96,120},{102,126},{120,96},{126,102},... | collective-permute-start | bytes 1572872 | tf_op jit(solution)/shard_map/ppermute | solution.py:51
  17.8 13.0 %collective-permute-start.8 = (bf16[512,512]{1,0:T(8,128)(2,1)S(1)}, bf16[512,512]{1,0:T(8,128)(2,1)S(1)}, u32[]{:S(2)}, u32[]{:S(2)}) collective-permute-start(bf16[512,512]{1,0:T(8,128)(2,1)S(1)} %get-tuple-element.62.refs_7_.refs_5_), channel_id=1, source_target_pairs={{0,6},{6,0},{24,30},{30,24},{96,102},{102,96},{120,126},{126,120},... | collective-permute-start | bytes 1572872 | tf_op jit(solution)/shard_map/ppermute | solution.py:51
  18.0 12.7 %collective-permute-start.9 = (bf16[512,512]{1,0:T(8,128)(2,1)S(1)}, bf16[512,512]{1,0:T(8,128)(2,1)S(1)}, u32[]{:S(2)}, u32[]{:S(2)}) collective-permute-start(bf16[512,512]{1,0:T(8,128)(2,1)S(1)} %get-tuple-element.63.refs_6_.refs_4_), channel_id=1, source_target_pairs={{0,96},{6,102},{24,120},{30,126},{96,0},{102,6},{120,24},{126,30},... | collective-permute-start | bytes 1572872 | tf_op jit(solution)/shard_map/ppermute | solution.py:51
  18.8 10.1 %slice-start.3 = ((s8[16777216]{0:T(1024)(128)(4,1)}), s8[4194304]{0:T(1024)(128)(4,1)S(1)}, s32[]{:S(2)}) async-start(s8[16777216]{0:T(1024)(128)(4,1)} %bitcast.3), calls=%async_computation.3 | async-start | bytes 8388608
  18.8 10.1 %copy-start = (bf16[2,2048,256]{2,1,0:T(8,128)(2,1)S(1)}, bf16[2,2048,256]{2,1,0:T(8,128)(2,1)}, u32[]{:S(2)}) copy-start(bf16[2,2048,256]{2,1,0:T(8,128)(2,1)} %drive.5) | copy-start | bytes 6291460
  18.8 10.1 %copy-start.1 = (f32[2,2048]{1,0:T(2,128)S(1)}, f32[2,2048]{1,0:T(2,128)}, u32[]{:S(2)}) copy-start(f32[2,2048]{1,0:T(2,128)} %part.3) | copy-start | bytes 49156
  21.1 9.6 %collective-permute-start.3 = (bf16[8,32,512]{2,1,0:T(8,128)(2,1)S(1)}, bf16[8,32,512]{2,1,0:T(8,128)(2,1)S(1)}, u32[]{:S(2)}, u32[]{:S(2)}) collective-permute-start(bf16[8,32,512]{2,1,0:T(8,128)(2,1)S(1)} %get-tuple-element.60), channel_id=1, source_target_pairs={{0,2},{6,4},{24,26},{30,28},{96,98},{102,100},{120,122},{126,124},... | collective-permute-start | bytes 786440 | tf_op jit(solution)/shard_map/ppermute | solution.py:51
  23.7 14.8 %collective-permute-start.12 = (bf16[8,32,512]{2,1,0:T(8,128)(2,1)S(1)}, bf16[8,32,512]{2,1,0:T(8,128)(2,1)S(1)}, u32[]{:S(2)}, u32[]{:S(2)}) collective-permute-start(bf16[8,32,512]{2,1,0:T(8,128)(2,1)S(1)} %get-tuple-element.71), channel_id=1, source_target_pairs={{0,42},{6,44},{24,50},{30,52},{96,74},{102,76},{120,82},{126,84},{... | collective-permute-start | bytes 786440 | tf_op jit(solution)/shard_map/ppermute | solution.py:51
  30.8 18.6 %collective-permute-start.13 = (bf16[512,512]{1,0:T(8,128)(2,1)S(1)}, bf16[512,512]{1,0:T(8,128)(2,1)S(1)}, u32[]{:S(2)}, u32[]{:S(2)}) collective-permute-start(bf16[512,512]{1,0:T(8,128)(2,1)S(1)} %get-tuple-element.74.refs_11_.refs_9_), channel_id=1, source_target_pairs={{0,6},{6,0},{24,30},{30,24},{96,102},{102,96},{120,126},{126,120},... | collective-permute-start | bytes 1572872 | tf_op jit(solution)/shard_map/ppermute | solution.py:51
  30.9 15.1 %collective-permute-start.10 = (bf16[8,32,512]{2,1,0:T(8,128)(2,1)S(1)}, bf16[8,32,512]{2,1,0:T(8,128)(2,1)S(1)}, u32[]{:S(2)}, u32[]{:S(2)}) collective-permute-start(bf16[8,32,512]{2,1,0:T(8,128)(2,1)S(1)} %get-tuple-element.69), channel_id=1, source_target_pairs={{0,8},{6,14},{24,16},{30,22},{96,104},{102,110},{120,112},{126,118... | collective-permute-start | bytes 786440 | tf_op jit(solution)/shard_map/ppermute | solution.py:51
  32.0 17.4 %collective-permute-start.11 = (bf16[8,32,512]{2,1,0:T(8,128)(2,1)S(1)}, bf16[8,32,512]{2,1,0:T(8,128)(2,1)S(1)}, u32[]{:S(2)}, u32[]{:S(2)}) collective-permute-start(bf16[8,32,512]{2,1,0:T(8,128)(2,1)S(1)} %get-tuple-element.70), channel_id=1, source_target_pairs={{0,32},{6,38},{24,56},{30,62},{96,64},{102,70},{120,88},{126,94},{... | collective-permute-start | bytes 786440 | tf_op jit(solution)/shard_map/ppermute | solution.py:51
  35.1 18.0 %collective-permute-start.18 = (bf16[8,32,512]{2,1,0:T(8,128)(2,1)S(1)}, bf16[8,32,512]{2,1,0:T(8,128)(2,1)S(1)}, u32[]{:S(2)}, u32[]{:S(2)}) collective-permute-start(bf16[8,32,512]{2,1,0:T(8,128)(2,1)S(1)} %get-tuple-element.80), channel_id=1, source_target_pairs={{0,10},{6,12},{24,18},{30,20},{96,106},{102,108},{120,114},{126,11... | collective-permute-start | bytes 786440 | tf_op jit(solution)/shard_map/ppermute | solution.py:51
  38.4 14.9 %collective-permute-start.19 = (bf16[8,32,512]{2,1,0:T(8,128)(2,1)S(1)}, bf16[8,32,512]{2,1,0:T(8,128)(2,1)S(1)}, u32[]{:S(2)}, u32[]{:S(2)}) collective-permute-start(bf16[8,32,512]{2,1,0:T(8,128)(2,1)S(1)} %get-tuple-element.81), channel_id=1, source_target_pairs={{0,34},{6,36},{24,58},{30,60},{96,66},{102,68},{120,90},{126,92},{... | collective-permute-start | bytes 786440 | tf_op jit(solution)/shard_map/ppermute | solution.py:51
  46.0 11.9 %collective-permute-start.20 = (bf16[8,32,512]{2,1,0:T(8,128)(2,1)S(1)}, bf16[8,32,512]{2,1,0:T(8,128)(2,1)S(1)}, u32[]{:S(2)}, u32[]{:S(2)}) collective-permute-start(bf16[8,32,512]{2,1,0:T(8,128)(2,1)S(1)} %get-tuple-element.82), channel_id=1, source_target_pairs={{0,40},{6,46},{24,48},{30,54},{96,72},{102,78},{120,80},{126,86},{... | collective-permute-start | bytes 786440 | tf_op jit(solution)/shard_map/ppermute | solution.py:51
  50.2 11.0 %collective-permute-start.14 = (bf16[8,32,512]{2,1,0:T(8,128)(2,1)S(1)}, bf16[8,32,512]{2,1,0:T(8,128)(2,1)S(1)}, u32[]{:S(2)}, u32[]{:S(2)}) collective-permute-start(bf16[8,32,512]{2,1,0:T(8,128)(2,1)S(1)} %get-tuple-element.76), channel_id=1, source_target_pairs={{0,2},{6,4},{24,26},{30,28},{96,98},{102,100},{120,122},{126,124},... | collective-permute-start | bytes 786440 | tf_op jit(solution)/shard_map/ppermute | solution.py:51
  50.7 12.9 %collective-permute-start.15 = (bf16[8,32,512]{2,1,0:T(8,128)(2,1)S(1)}, bf16[8,32,512]{2,1,0:T(8,128)(2,1)S(1)}, u32[]{:S(2)}, u32[]{:S(2)}) collective-permute-start(bf16[8,32,512]{2,1,0:T(8,128)(2,1)S(1)} %get-tuple-element.77), channel_id=1, source_target_pairs={{0,8},{6,14},{24,16},{30,22},{96,104},{102,110},{120,112},{126,118... | collective-permute-start | bytes 786440 | tf_op jit(solution)/shard_map/ppermute | solution.py:51
  53.2 14.3 %collective-permute-start.16 = (bf16[8,32,512]{2,1,0:T(8,128)(2,1)S(1)}, bf16[8,32,512]{2,1,0:T(8,128)(2,1)S(1)}, u32[]{:S(2)}, u32[]{:S(2)}) collective-permute-start(bf16[8,32,512]{2,1,0:T(8,128)(2,1)S(1)} %get-tuple-element.78), channel_id=1, source_target_pairs={{0,32},{6,38},{24,56},{30,62},{96,64},{102,70},{120,88},{126,94},{... | collective-permute-start | bytes 786440 | tf_op jit(solution)/shard_map/ppermute | solution.py:51
  53.4 14.1 %collective-permute-start.17 = (bf16[8,32,512]{2,1,0:T(8,128)(2,1)S(1)}, bf16[8,32,512]{2,1,0:T(8,128)(2,1)S(1)}, u32[]{:S(2)}, u32[]{:S(2)}) collective-permute-start(bf16[8,32,512]{2,1,0:T(8,128)(2,1)S(1)} %get-tuple-element.79), channel_id=1, source_target_pairs={{0,42},{6,44},{24,50},{30,52},{96,74},{102,76},{120,82},{126,84},{... | collective-permute-start | bytes 786440 | tf_op jit(solution)/shard_map/ppermute | solution.py:51
  58.7 10.9 %collective-permute-start.21 = (bf16[8,32,512]{2,1,0:T(8,128)(2,1)S(1)}, bf16[8,32,512]{2,1,0:T(8,128)(2,1)S(1)}, u32[]{:S(2)}, u32[]{:S(2)}) collective-permute-start(bf16[8,32,512]{2,1,0:T(8,128)(2,1)S(1)} %get-tuple-element.83), channel_id=1, source_target_pairs={{0,10},{6,12},{24,18},{30,20},{96,106},{102,108},{120,114},{126,11... | collective-permute-start | bytes 786440 | tf_op jit(solution)/shard_map/ppermute | solution.py:51
  61.2 9.8 %collective-permute-start.22 = (bf16[8,32,512]{2,1,0:T(8,128)(2,1)S(1)}, bf16[8,32,512]{2,1,0:T(8,128)(2,1)S(1)}, u32[]{:S(2)}, u32[]{:S(2)}) collective-permute-start(bf16[8,32,512]{2,1,0:T(8,128)(2,1)S(1)} %get-tuple-element.85), channel_id=1, source_target_pairs={{0,34},{6,36},{24,58},{30,60},{96,66},{102,68},{120,90},{126,92},{... | collective-permute-start | bytes 786440 | tf_op jit(solution)/shard_map/ppermute | solution.py:51
  63.6 9.4 %collective-permute-start.23 = (bf16[8,32,512]{2,1,0:T(8,128)(2,1)S(1)}, bf16[8,32,512]{2,1,0:T(8,128)(2,1)S(1)}, u32[]{:S(2)}, u32[]{:S(2)}) collective-permute-start(bf16[8,32,512]{2,1,0:T(8,128)(2,1)S(1)} %get-tuple-element.86), channel_id=1, source_target_pairs={{0,40},{6,46},{24,48},{30,54},{96,72},{102,78},{120,80},{126,86},{... | collective-permute-start | bytes 786440 | tf_op jit(solution)/shard_map/ppermute | solution.py:51
  73.0 1.8 %copy-start.2 = (f32[2,256]{1,0:T(2,128)S(1)}, f32[2,256]{1,0:T(2,128)}, u32[]{:S(2)}) copy-start(f32[2,256]{1,0:T(2,128)} %hole.1) | copy-start | bytes 6148
  74.7 2.7 %collective-permute-start.24 = (bf16[2048,256]{1,0:T(8,128)(2,1)S(1)}, bf16[2048,256]{1,0:T(8,128)(2,1)S(1)}, u32[]{:S(2)}, u32[]{:S(2)}) collective-permute-start(bf16[2048,256]{1,0:T(8,128)(2,1)S(1)} %final_other.1.refs_2_), channel_id=1, source_target_pairs={{0,1},{1,0},{2,3},{3,2},{4,5},{5,4},{6,7},{7,6},{8,9},{9,8},{10,11... | collective-permute-start | bytes 3145736 | tf_op jit(solution)/shard_map/ppermute | solution.py:47

commit v7 on v6

--- a/solution.py
+++ b/solution.py
@@ -90,7 +90,7 @@
 FIRST, THEN = (1, 7), (2, 4, 3, 5, 6)
 BACK = (0, 1, 2, 4, 7), (3, 5, 6)
 ORDER = BACK[0] + BACK[1]
-EARLY, LATE = (range(2), range(2, 5), range(5, 6)), range(6, 8)
+EARLY, LATE = (range(5), range(5, 6)), range(6, 8)
 
 
 def tie_kernel(*refs):

time: 79.3 us -> 79.3 us (level)
    pallas_call x3 -> x2, Pallas kernels: 4.47 us -> 4.04 us  [folded_call(): pl.pallas_call(functools.partial(folded_kernel, chosen), in_specs=[WHOLE]...]
  transfers between devices with their start and end apart: 25 -> 25, of which waited for: 4 -> 4; matrix products, arithmetic and copies ran while one was open for 0% -> 0% of each run, Pallas kernels for 33% -> 32%
where the time goes in v7:
time: 79.3 us; the launch traced here: 79.1 us
  starting transfers between devices  44.7 us (56%)
  Pallas kernels  30.4 us (38%)
  waiting for transfers between devices  3.4 us (4%)
    ppermute x21, starting transfers between devices, over(): return lax.ppermute(array, BOTH, flips(moved, kept))  42.6 us
    pallas_call x2, Pallas kernels, ladder_call(): pl.pallas_call(functools.partial(ladder_kernel, tiles), grid_spec=pltpu.P...  5.73 us
    pallas_call x1, Pallas kernels, load_call(): pl.pallas_call(load_kernel, grid_spec=pltpu.PrefetchScalarGridSpec(num_sc...  5.08 us
    pallas_call x2, Pallas kernels, final_call(): pl.pallas_call(functools.partial(final_kernel, chosen, side), grid_spec=p...  4.05 us
    pallas_call x2, Pallas kernels, folded_call(): pl.pallas_call(functools.partial(folded_kernel, chosen), in_specs=[WHOLE]...  4.04 us
    ppermute x21, waiting for transfers between devices, over(): return lax.ppermute(array, BOTH, flips(moved, kept))  3.16 us
    pallas_call x1, Pallas kernels, other_call(): pl.pallas_call(other_kernel, in_specs=[WHOLE] * 10 + [WAIT] * len(waits),...  2.33 us
    pallas_call x1, Pallas kernels, own_call(): pl.pallas_call(own_kernel, in_specs=[WHOLE, WHOLE] + [WAIT] * len(waits),...  2.33 us
  transfers between devices with their start and end apart: 25, of which 4 were waited for; matrix products, arithmetic and copies ran while one was open for 0% of the time, Pallas kernels for 32%

profile of v7, /device:TPU:1, one launch (start us, length us, event | category | flops | bytes accessed | tf_op | source)
XLA Modules:
  0.0 79.1 jit_solution(16215541028450296802)
XLA Ops:
  0.0 1.4 %collective-permute-start = (bf16[2,256,512]{2,1,0:T(8,128)(2,1)}, bf16[2,256,512]{2,1,0:T(8,128)(2,1)S(1)}, u32[]{:S(2)}, u32[]{:S(2)}) collective-permute-start(bf16[2,256,512]{2,1,0:T(8,128)(2,1)} %own.1), channel_id=1, source_target_pairs={{0,1},{1,0},{2,3},{3,2},{4,5},{5,4},{6,7},{7,6},{8,9},{9,8},{10,11... | collective-permute-start | bytes 1572872 | tf_op jit(solution)/shard_map/ppermute | solution.py:47
  1.4 0.0 collective-permute-start.1
  1.4 0.1 pad_add_fusion.sc
  1.5 2.1 %cut.1.refs_0_ = bf16[2,2048,256]{2,1,0:T(8,128)(2,1)S(1)} custom-call(s32[3]{0:T(128)S(1)} %pad_add_fusion.sc, bf16[2,2048,256]{2,1,0:T(8,128)(2,1)} %amplitudes.3, bf16[2,2048,256]{2,1,0:T(8,128)(2,1)} %drive.5), custom_call_target="tpu_custom_call" | custom-call | bytes 4194304 | tf_op jit(solution)/shard_map/cut/pallas_call | solution.py:126
  3.6 0.0 collective-permute-done.1.refs_1_.hole
  3.6 0.0 collective-permute-done.oth
  3.6 1.6 %coupling.1.refs_0_.refs_1_.refs_5_.refs_3_ = bf16[512,512]{1,0:T(8,128)(2,1)S(1)} custom-call(s32[3]{0:T(128)S(1)} %pad_add_fusion.sc, bf16[2,256,512]{2,1,0:T(8,128)(2,1)} %own.1, bf16[2,256,512]{2,1,0:T(8,128)(2,1)S(1)} %collective-permute-done.oth, bf16[2,2048,256]{2,1,0:T(8,128)(2,1)S(1)} %cut.1.refs_0_, f32[2,256]{1,0:T(2,128)S(1)} %collective-permute-done.1.refs_1_.hole), custom_call_target="tpu_custom_call" | custom-call | bytes 1048576 | tf_op jit(solution)/shard_map/coupling/pallas_call | solution.py:245
  5.2 0.6 collective-permute-start.2
  5.8 1.3 %collective-permute-start.6 = (bf16[512,512]{1,0:T(8,128)(2,1)S(1)}, bf16[512,512]{1,0:T(8,128)(2,1)S(1)}, u32[]{:S(2)}, u32[]{:S(2)}) collective-permute-start(bf16[512,512]{1,0:T(8,128)(2,1)S(1)} %coupling.1.refs_0_.refs_1_.refs_5_.refs_3_), channel_id=1, source_target_pairs={{0,6},{6,0},{24,30},{30,24},{96,102},{102,96},{120,126},{126,120},... | collective-permute-start | bytes 1572872 | tf_op jit(solution)/shard_map/ppermute | solution.py:51
  7.1 1.3 %collective-permute-start.5 = (bf16[512,512]{1,0:T(8,128)(2,1)S(1)}, bf16[512,512]{1,0:T(8,128)(2,1)S(1)}, u32[]{:S(2)}, u32[]{:S(2)}) collective-permute-start(bf16[512,512]{1,0:T(8,128)(2,1)S(1)} %coupling.1.refs_0_.refs_1_.refs_5_.refs_3_), channel_id=1, source_target_pairs={{0,24},{6,30},{24,0},{30,6},{96,120},{102,126},{120,96},{126,102},... | collective-permute-start | bytes 1572872 | tf_op jit(solution)/shard_map/ppermute | solution.py:51
  8.4 1.6 %collective-permute-start.4 = (bf16[512,512]{1,0:T(8,128)(2,1)S(1)}, bf16[512,512]{1,0:T(8,128)(2,1)S(1)}, u32[]{:S(2)}, u32[]{:S(2)}) collective-permute-start(bf16[512,512]{1,0:T(8,128)(2,1)S(1)} %coupling.1.refs_0_.refs_1_.refs_5_.refs_3_), channel_id=1, source_target_pairs={{0,96},{6,102},{24,120},{30,126},{96,0},{102,6},{120,24},{126,30},... | collective-permute-start | bytes 1572872 | tf_op jit(solution)/shard_map/ppermute | solution.py:51
  10.0 5.1 %load.1 = (bf16[2048,2048]{1,0:T(8,128)(2,1)S(1)}, bf16[2048,256]{1,0:T(8,128)(2,1)S(1)}) custom-call(s32[3]{0:T(128)S(1)} %pad_add_fusion.sc, bf16[2,2048,2048]{2,1,0:T(8,128)(2,1)} %recouple.1, bf16[2,2048,256]{2,1,0:T(8,128)(2,1)} %amplitudes.3, bf16[512,512]{1,0:T(8,128)(2,1)S(1)} %coupling.1.refs_0_.refs_1_.refs_5_.refs_3_), custom_call_target="tpu_custom_call" | custom-call | bytes 16777216 | tf_op jit(solution)/shard_map/load/pallas_call | solution.py:160
  15.1 0.0 slice-start.2
  15.1 2.3 %recoupled_own.1 = (bf16[8,32,512]{2,1,0:T(8,128)(2,1)S(1)}, bf16[8,32,512]{2,1,0:T(8,128)(2,1)S(1)}, bf16[8,32,512]{2,1,0:T(8,128)(2,1)S(1)}, bf16[8,32,512]{2,...) custom-call(bf16[2048,2048]{1,0:T(8,128)(2,1)S(1)} %get-tuple-elemen, ...), custom_call_target="tpu_custom_call" | custom-call | flops 2147483648 | bytes 8388608 | tf_op jit(solution)/shard_map/recoupled_own/pallas_call | solution.py:194
  17.5 0.0 collective-permute-done.6.refs_2_
  17.5 0.0 collective-permute-done.5.refs_1_
  17.5 0.0 collective-permute-done.4.refs_0_
  17.5 0.2 collective-permute-start.7
  17.8 0.3 collective-permute-start.8
  18.0 0.8 collective-permute-start.9
  18.8 0.0 collective-permute-done.2.pair
  18.8 2.3 %recoupled_other.1 = (bf16[8,32,512]{2,1,0:T(8,128)(2,1)S(1)}, bf16[8,32,512]{2,1,0:T(8,128)(2,1)S(1)}, bf16[8,32,512]{2,1,0:T(8,128)(2,1)S(1)}, bf16[8,32,512]{...) custom-call(bf16[2048,2048]{1,0:T(8,128)(2,1)S(1)} %get-tuple-elemen, ...), custom_call_target="tpu_custom_call", output_to_operand_aliasing={{0}: (2, {}), {1}: (3, {}), {2}: (4, {}), {3}: (5, {}), {4}... | custom-call | flops 2147483648 | bytes 2097152 | tf_op jit(solution)/shard_map/recoupled_other/pallas_call | solution.py:216
  21.1 2.6 %collective-permute-start.3 = (bf16[8,32,512]{2,1,0:T(8,128)(2,1)S(1)}, bf16[8,32,512]{2,1,0:T(8,128)(2,1)S(1)}, u32[]{:S(2)}, u32[]{:S(2)}) collective-permute-start(bf16[8,32,512]{2,1,0:T(8,128)(2,1)S(1)} %get-tuple-element.60), channel_id=1, source_target_pairs={{0,2},{6,4},{24,26},{30,28},{96,98},{102,100},{120,122},{126,124},... | collective-permute-start | bytes 786440 | tf_op jit(solution)/shard_map/ppermute | solution.py:51
  23.7 5.2 %collective-permute-start.12 = (bf16[8,32,512]{2,1,0:T(8,128)(2,1)S(1)}, bf16[8,32,512]{2,1,0:T(8,128)(2,1)S(1)}, u32[]{:S(2)}, u32[]{:S(2)}) collective-permute-start(bf16[8,32,512]{2,1,0:T(8,128)(2,1)S(1)} %get-tuple-element.71), channel_id=1, source_target_pairs={{0,42},{6,44},{24,50},{30,52},{96,74},{102,76},{120,82},{126,84},{... | collective-permute-start | bytes 786440 | tf_op jit(solution)/shard_map/ppermute | solution.py:51
  28.9 1.8 %ladder.2 = (f32[2048,512]{1,0:T(8,128)S(1)}, f32[2048,128]{1,0:T(8,128)S(1)}) custom-call(s32[3]{0:T(128)S(1)} %pad_add_fusion.sc, bf16[2,2048,2048]{2,1,0:T(8,128)(2,1)S(1)} %bitcast.4, bf16[2048,256]{1,0:T(8,128)(2,1)S(1)} %get-tuple-element.47.amp, bf16[2,2048,256]{2,1,0:T(8,128)(2,1)S(1)} %copy-done, ...), custom_call_target="tpu_custom_call" | custom-call | flops 1073741824 | bytes 4194304 | tf_op jit(solution)/shard_map/ladder/pallas_call | solution.py:299
  30.7 0.0 collective-permute-done.7.refs_0_
  30.7 0.0 collective-permute-done.8.refs_1_
  30.7 0.0 collective-permute-done.9.refs_2_
  30.7 0.0 collective-permute-done.3.refs_9_.refs_1_
  30.8 0.1 collective-permute-start.13
  30.9 1.1 %collective-permute-start.10 = (bf16[8,32,512]{2,1,0:T(8,128)(2,1)S(1)}, bf16[8,32,512]{2,1,0:T(8,128)(2,1)S(1)}, u32[]{:S(2)}, u32[]{:S(2)}) collective-permute-start(bf16[8,32,512]{2,1,0:T(8,128)(2,1)S(1)} %get-tuple-element.69), channel_id=1, source_target_pairs={{0,8},{6,14},{24,16},{30,22},{96,104},{102,110},{120,112},{126,118... | collective-permute-start | bytes 786440 | tf_op jit(solution)/shard_map/ppermute | solution.py:51
  32.0 3.2 %collective-permute-start.11 = (bf16[8,32,512]{2,1,0:T(8,128)(2,1)S(1)}, bf16[8,32,512]{2,1,0:T(8,128)(2,1)S(1)}, u32[]{:S(2)}, u32[]{:S(2)}) collective-permute-start(bf16[8,32,512]{2,1,0:T(8,128)(2,1)S(1)} %get-tuple-element.70), channel_id=1, source_target_pairs={{0,32},{6,38},{24,56},{30,62},{96,64},{102,70},{120,88},{126,94},{... | collective-permute-start | bytes 786440 | tf_op jit(solution)/shard_map/ppermute | solution.py:51
  35.1 3.2 %collective-permute-start.18 = (bf16[8,32,512]{2,1,0:T(8,128)(2,1)S(1)}, bf16[8,32,512]{2,1,0:T(8,128)(2,1)S(1)}, u32[]{:S(2)}, u32[]{:S(2)}) collective-permute-start(bf16[8,32,512]{2,1,0:T(8,128)(2,1)S(1)} %get-tuple-element.80), channel_id=1, source_target_pairs={{0,10},{6,12},{24,18},{30,20},{96,106},{102,108},{120,114},{126,11... | collective-permute-start | bytes 786440 | tf_op jit(solution)/shard_map/ppermute | solution.py:51
  38.3 0.1 collective-permute-done.12.refs_4_
  38.4 3.6 %collective-permute-start.19 = (bf16[8,32,512]{2,1,0:T(8,128)(2,1)S(1)}, bf16[8,32,512]{2,1,0:T(8,128)(2,1)S(1)}, u32[]{:S(2)}, u32[]{:S(2)}) collective-permute-start(bf16[8,32,512]{2,1,0:T(8,128)(2,1)S(1)} %get-tuple-element.81), channel_id=1, source_target_pairs={{0,34},{6,36},{24,58},{30,60},{96,66},{102,68},{120,90},{126,92},{... | collective-permute-start | bytes 786440 | tf_op jit(solution)/shard_map/ppermute | solution.py:51
  42.0 3.9 %ladder.3 = (f32[2048,512]{1,0:T(8,128)S(1)}, f32[2048,128]{1,0:T(8,128)S(1)}) custom-call(s32[3]{0:T(128)S(1)} %pad_add_fusion.sc, bf16[2,2048,2048]{2,1,0:T(8,128)(2,1)S(1)} %bitcast.4, bf16[2048,256]{1,0:T(8,128)(2,1)S(1)} %get-tuple-element.47.amp, bf16[2,2048,256]{2,1,0:T(8,128)(2,1)S(1)} %copy-done, ...), custom_call_target="tpu_custom_call", output_to_operand_aliasing={{0}: (6, {}), {1}: (7, {})} | custom-call | flops 3221225472 | bytes 4194304 | tf_op jit(solution)/shard_map/ladder/pallas_call | solution.py:299
  46.0 0.0 collective-permute-done.10.refs_2_
  46.0 3.4 %collective-permute-start.20 = (bf16[8,32,512]{2,1,0:T(8,128)(2,1)S(1)}, bf16[8,32,512]{2,1,0:T(8,128)(2,1)S(1)}, u32[]{:S(2)}, u32[]{:S(2)}) collective-permute-start(bf16[8,32,512]{2,1,0:T(8,128)(2,1)S(1)} %get-tuple-element.82), channel_id=1, source_target_pairs={{0,40},{6,46},{24,48},{30,54},{96,72},{102,78},{120,80},{126,86},{... | collective-permute-start | bytes 786440 | tf_op jit(solution)/shard_map/ppermute | solution.py:51
  49.4 0.0 collective-permute-done.11.refs_3_
  49.4 0.0 collective-permute-done.13.refs_12_.refs_10_
  49.4 0.9 %cycle.2 = (bf16[8,32,512]{2,1,0:T(8,128)(2,1)S(1)}, bf16[8,32,512]{2,1,0:T(8,128)(2,1)S(1)}, bf16[8,32,512]{2,1,0:T(8,128)(2,1)S(1)}, bf16[8,32,512]{2,1,0:T(8,128)(2,1)S(1)}, bf16[8,32,512]{2,1,0:T(8,128)(2,1)S(1)}) custom-call(bf16[8,32,512]{2,1,0:T(8,128)(2,1)S(1)} %get-tuple-element.59.refs_0_, ...), custom_call_target="tpu_custom_call" | custom-call | flops 671088640 | bytes 6815744 | tf_op jit(solution)/shard_map/cycle/pallas_call | solution.py:274
  50.2 0.5 collective-permute-start.14
  50.7 2.4 %collective-permute-start.15 = (bf16[8,32,512]{2,1,0:T(8,128)(2,1)S(1)}, bf16[8,32,512]{2,1,0:T(8,128)(2,1)S(1)}, u32[]{:S(2)}, u32[]{:S(2)}) collective-permute-start(bf16[8,32,512]{2,1,0:T(8,128)(2,1)S(1)} %get-tuple-element.77), channel_id=1, source_target_pairs={{0,8},{6,14},{24,16},{30,22},{96,104},{102,110},{120,112},{126,118... | collective-permute-start | bytes 786440 | tf_op jit(solution)/shard_map/ppermute | solution.py:51
  53.2 0.0 collective-permute-done.18.refs_0_
  53.2 0.2 collective-permute-start.16
  53.4 0.0 collective-permute-done.19.refs_1_
  53.4 4.5 %collective-permute-start.17 = (bf16[8,32,512]{2,1,0:T(8,128)(2,1)S(1)}, bf16[8,32,512]{2,1,0:T(8,128)(2,1)S(1)}, u32[]{:S(2)}, u32[]{:S(2)}) collective-permute-start(bf16[8,32,512]{2,1,0:T(8,128)(2,1)S(1)} %get-tuple-element.79), channel_id=1, source_target_pairs={{0,42},{6,44},{24,50},{30,52},{96,74},{102,76},{120,82},{126,84},{... | collective-permute-start | bytes 786440 | tf_op jit(solution)/shard_map/ppermute | solution.py:51
  57.9 0.0 collective-permute-done.20.refs_2_
  57.9 0.8 %cycle.3 = (bf16[8,32,512]{2,1,0:T(8,128)(2,1)S(1)}, bf16[8,32,512]{2,1,0:T(8,128)(2,1)S(1)}, bf16[8,32,512]{2,1,0:T(8,128)(2,1)S(1)}) custom-call(bf16[8,32,512]{2,1,0:T(8,128)(2,1)S(1)} %collective-permute-done.18.refs_0_, bf16[8,32,512]{2,1,0:T(8,128)(2,1)S(1)} %collective-permute-done.19.refs_1_, ...), custom_call_target="tpu_custom_call" | custom-call | flops 402653184 | bytes 5767168 | tf_op jit(solution)/shard_map/cycle/pallas_call | solution.py:274
  58.7 2.6 %collective-permute-start.21 = (bf16[8,32,512]{2,1,0:T(8,128)(2,1)S(1)}, bf16[8,32,512]{2,1,0:T(8,128)(2,1)S(1)}, u32[]{:S(2)}, u32[]{:S(2)}) collective-permute-start(bf16[8,32,512]{2,1,0:T(8,128)(2,1)S(1)} %get-tuple-element.83), channel_id=1, source_target_pairs={{0,10},{6,12},{24,18},{30,20},{96,106},{102,108},{120,114},{126,11... | collective-permute-start | bytes 786440 | tf_op jit(solution)/shard_map/ppermute | solution.py:51
  61.2 0.0 collective-permute-done.14.refs_1_
  61.2 2.4 %collective-permute-start.22 = (bf16[8,32,512]{2,1,0:T(8,128)(2,1)S(1)}, bf16[8,32,512]{2,1,0:T(8,128)(2,1)S(1)}, u32[]{:S(2)}, u32[]{:S(2)}) collective-permute-start(bf16[8,32,512]{2,1,0:T(8,128)(2,1)S(1)} %get-tuple-element.85), channel_id=1, source_target_pairs={{0,34},{6,36},{24,58},{30,60},{96,66},{102,68},{120,90},{126,92},{... | collective-permute-start | bytes 786440 | tf_op jit(solution)/shard_map/ppermute | solution.py:51
  63.6 2.3 %collective-permute-start.23 = (bf16[8,32,512]{2,1,0:T(8,128)(2,1)S(1)}, bf16[8,32,512]{2,1,0:T(8,128)(2,1)S(1)}, u32[]{:S(2)}, u32[]{:S(2)}) collective-permute-start(bf16[8,32,512]{2,1,0:T(8,128)(2,1)S(1)} %get-tuple-element.86), channel_id=1, source_target_pairs={{0,40},{6,46},{24,48},{30,54},{96,72},{102,78},{120,80},{126,86},{... | collective-permute-start | bytes 786440 | tf_op jit(solution)/shard_map/ppermute | solution.py:51
  65.9 0.0 collective-permute-done.16.refs_3_
  65.9 0.0 collective-permute-done.17.refs_4_
  65.9 3.2 %folded.2.ladder = f32[2048,512]{1,0:T(8,128)S(1)} custom-call(bf16[2048,2048]{1,0:T(8,128)(2,1)S(1)} %get-tuple-element.46.rows, f32[2048,512]{1,0:T(8,128)S(1)} %get-tuple-element.50.refs_13_.ladder.refs_11_, bf16[8,32,512]{2,1,0:T(8,128)(2,1)S(1)} %get-tuple-element.75.refs_0_, ...), custom_call_target="tpu_custom_call", output_to_operand_aliasing={{}: (1, {})} | custom-call | flops 2684354560 | bytes 6291456 | tf_op jit(solution)/shard_map/folded/pallas_call | solution.py:339
  69.1 0.9 %folded.3.ladder = f32[2048,512]{1,0:T(8,128)S(1)} custom-call(bf16[2048,2048]{1,0:T(8,128)(2,1)S(1)} %get-tuple-element.46.rows, f32[2048,512]{1,0:T(8,128)S(1)} %folded.2.ladder, bf16[8,32,512]{2,1,0:T(8,128)(2,1)S(1)} %collective-permute-done.21.refs_0_), custom_call_target="tpu_custom_call", output_to_operand_aliasing={{}: (1, {})} | custom-call | flops 536870912 | bytes 6291456 | tf_op jit(solution)/shard_map/folded/pallas_call | solution.py:339
  70.0 1.0 %collective-permute-done.22.refs_0_ = bf16[8,32,512]{2,1,0:T(8,128)(2,1)S(1)} collective-permute-done((bf16[8,32,512]{2,1,0:T(8,128)(2,1)S(1)}, bf16[8,32,512]{2,1,0:T(8,128)(2,1)S(1)}, u32[]{:S(2)}, u32[]{:S(2)}) %collective-permute-start.22) | collective-permute-done | bytes 262176 | tf_op jit(solution)/shard_map/ppermute | solution.py:51
  71.0 2.0 %collective-permute-done.23.refs_1_ = bf16[8,32,512]{2,1,0:T(8,128)(2,1)S(1)} collective-permute-done((bf16[8,32,512]{2,1,0:T(8,128)(2,1)S(1)}, bf16[8,32,512]{2,1,0:T(8,128)(2,1)S(1)}, u32[]{:S(2)}, u32[]{:S(2)}) %collective-permute-start.23) | collective-permute-done | bytes 262176 | tf_op jit(solution)/shard_map/ppermute | solution.py:51
  73.0 1.7 %final_other.1.refs_2_ = bf16[2048,256]{1,0:T(8,128)(2,1)S(1)} custom-call(s32[3]{0:T(128)S(1)} %pad_add_fusion.sc, bf16[2048,2048]{1,0:T(8,128)(2,1)S(1)} %get-tuple-element.46.rows, f32[2048,512]{1,0:T(8,128)S(1)} %folded.3.ladder, f32[2048,128]{1,0:T(8,128)S(1)} %get-tuple-element.84.part, f32[2,256]{1,0:T(2,128)S(1)} %collective-permute-done.1.refs_1_.hole, ...), custom_call_target="tpu_custom_call" | custom-call | flops 2147483648 | bytes 3145728 | tf_op jit(solution)/shard_map/final_other/pallas_call | solution.py:378
  74.7 0.1 collective-permute-start.24
  74.8 2.4 %final_own.1.given = bf16[2,2048,256]{2,1,0:T(8,128)(2,1)} custom-call(s32[3]{0:T(128)S(1)} %pad_add_fusion.sc, bf16[2048,2048]{1,0:T(8,128)(2,1)S(1)} %get-tuple-element.46.rows, f32[2048,512]{1,0:T(8,128)S(1)} %folded.3.ladder, f32[2048,128]{1,0:T(8,128)S(1)} %get-tuple-element.84.part, f32[2,256]{1,0:T(2,128)S(1)} %copy-done.2, ...), custom_call_target="tpu_custom_call" | custom-call | flops 2147483648 | bytes 3145728 | tf_op jit(solution)/shard_map/final_own/pallas_call | solution.py:378
  77.2 0.2 collective-permute-done.24.arrived
  77.4 1.5 %place.1 = bf16[2,2048,256]{2,1,0:T(8,128)(2,1)} custom-call(s32[3]{0:T(128)S(1)} %pad_add_fusion.sc, bf16[2048,256]{1,0:T(8,128)(2,1)S(1)} %collective-permute-done.24.arrived, bf16[2,2048,256]{2,1,0:T(8,128)(2,1)} %final_own.1.given), custom_call_target="tpu_custom_call", output_to_operand_aliasing={{}: (2, {})} | custom-call | bytes 2097152 | tf_op jit(solution)/shard_map/place/pallas_call | solution.py:422
  (19 shorter events, 0.0 us)
Async XLA Ops:
  0.0 3.6 %collective-permute-start = (bf16[2,256,512]{2,1,0:T(8,128)(2,1)}, bf16[2,256,512]{2,1,0:T(8,128)(2,1)S(1)}, u32[]{:S(2)}, u32[]{:S(2)}) collective-permute-start(bf16[2,256,512]{2,1,0:T(8,128)(2,1)} %own.1), channel_id=1, source_target_pairs={{0,1},{1,0},{2,3},{3,2},{4,5},{5,4},{6,7},{7,6},{8,9},{9,8},{10,11... | collective-permute-start | bytes 1572872 | tf_op jit(solution)/shard_map/ppermute | solution.py:47
  1.4 2.2 %collective-permute-start.1 = (f32[2,256]{1,0:T(2,128)}, f32[2,256]{1,0:T(2,128)S(1)}, u32[]{:S(2)}, u32[]{:S(2)}) collective-permute-start(f32[2,256]{1,0:T(2,128)} %hole.1), channel_id=1, source_target_pairs={{0,1},{1,0},{2,3},{3,2},{4,5},{5,4},{6,7},{7,6},{8,9},{9,8},{10,11... | collective-permute-start | bytes 6152 | tf_op jit(solution)/shard_map/ppermute | solution.py:47
  5.2 13.6 %collective-permute-start.2 = (bf16[2,2048,256]{2,1,0:T(8,128)(2,1)S(1)}, bf16[2,2048,256]{2,1,0:T(8,128)(2,1)S(1)}, u32[]{:S(2)}, u32[]{:S(2)}) collective-permute-start(bf16[2,2048,256]{2,1,0:T(8,128)(2,1)S(1)} %tie.3), channel_id=1, source_target_pairs={{0,1},{1,0},{2,3},{3,2},{4,5},{5,4},{6,7},{7,6},{8,9},{9,8},{10,11... | collective-permute-start | bytes 6291464 | tf_op jit(solution)/shard_map/ppermute | solution.py:47
  5.8 11.7 %collective-permute-start.6 = (bf16[512,512]{1,0:T(8,128)(2,1)S(1)}, bf16[512,512]{1,0:T(8,128)(2,1)S(1)}, u32[]{:S(2)}, u32[]{:S(2)}) collective-permute-start(bf16[512,512]{1,0:T(8,128)(2,1)S(1)} %coupling.1.refs_0_.refs_1_.refs_5_.refs_3_), channel_id=1, source_target_pairs={{0,6},{6,0},{24,30},{30,24},{96,102},{102,96},{120,126},{126,120},... | collective-permute-start | bytes 1572872 | tf_op jit(solution)/shard_map/ppermute | solution.py:51
  7.1 10.4 %collective-permute-start.5 = (bf16[512,512]{1,0:T(8,128)(2,1)S(1)}, bf16[512,512]{1,0:T(8,128)(2,1)S(1)}, u32[]{:S(2)}, u32[]{:S(2)}) collective-permute-start(bf16[512,512]{1,0:T(8,128)(2,1)S(1)} %coupling.1.refs_0_.refs_1_.refs_5_.refs_3_), channel_id=1, source_target_pairs={{0,24},{6,30},{24,0},{30,6},{96,120},{102,126},{120,96},{126,102},... | collective-permute-start | bytes 1572872 | tf_op jit(solution)/shard_map/ppermute | solution.py:51
  8.4 9.1 %collective-permute-start.4 = (bf16[512,512]{1,0:T(8,128)(2,1)S(1)}, bf16[512,512]{1,0:T(8,128)(2,1)S(1)}, u32[]{:S(2)}, u32[]{:S(2)}) collective-permute-start(bf16[512,512]{1,0:T(8,128)(2,1)S(1)} %coupling.1.refs_0_.refs_1_.refs_5_.refs_3_), channel_id=1, source_target_pairs={{0,96},{6,102},{24,120},{30,126},{96,0},{102,6},{120,24},{126,30},... | collective-permute-start | bytes 1572872 | tf_op jit(solution)/shard_map/ppermute | solution.py:51
  10.0 18.9 %slice-start = ((s8[16777216]{0:T(1024)(128)(4,1)}), s8[4194304]{0:T(1024)(128)(4,1)S(1)}, s32[]{:S(2)}) async-start(s8[16777216]{0:T(1024)(128)(4,1)} %bitcast.3), calls=%async_computation | async-start | bytes 8388608
  10.0 18.9 %slice-start.1 = ((s8[16777216]{0:T(1024)(128)(4,1)}), s8[4194304]{0:T(1024)(128)(4,1)S(1)}, s32[]{:S(2)}) async-start(s8[16777216]{0:T(1024)(128)(4,1)} %bitcast.3), calls=%async_computation.1 | async-start | bytes 8388608
  15.1 13.8 %slice-start.2 = ((s8[16777216]{0:T(1024)(128)(4,1)}), s8[4194304]{0:T(1024)(128)(4,1)S(1)}, s32[]{:S(2)}) async-start(s8[16777216]{0:T(1024)(128)(4,1)} %bitcast.3), calls=%async_computation.2 | async-start | bytes 8388608
  17.5 13.2 %collective-permute-start.7 = (bf16[512,512]{1,0:T(8,128)(2,1)S(1)}, bf16[512,512]{1,0:T(8,128)(2,1)S(1)}, u32[]{:S(2)}, u32[]{:S(2)}) collective-permute-start(bf16[512,512]{1,0:T(8,128)(2,1)S(1)} %get-tuple-element.61.refs_9_.refs_7_), channel_id=1, source_target_pairs={{0,24},{6,30},{24,0},{30,6},{96,120},{102,126},{120,96},{126,102},... | collective-permute-start | bytes 1572872 | tf_op jit(solution)/shard_map/ppermute | solution.py:51
  17.8 13.0 %collective-permute-start.8 = (bf16[512,512]{1,0:T(8,128)(2,1)S(1)}, bf16[512,512]{1,0:T(8,128)(2,1)S(1)}, u32[]{:S(2)}, u32[]{:S(2)}) collective-permute-start(bf16[512,512]{1,0:T(8,128)(2,1)S(1)} %get-tuple-element.62.refs_7_.refs_5_), channel_id=1, source_target_pairs={{0,6},{6,0},{24,30},{30,24},{96,102},{102,96},{120,126},{126,120},... | collective-permute-start | bytes 1572872 | tf_op jit(solution)/shard_map/ppermute | solution.py:51
  18.0 12.7 %collective-permute-start.9 = (bf16[512,512]{1,0:T(8,128)(2,1)S(1)}, bf16[512,512]{1,0:T(8,128)(2,1)S(1)}, u32[]{:S(2)}, u32[]{:S(2)}) collective-permute-start(bf16[512,512]{1,0:T(8,128)(2,1)S(1)} %get-tuple-element.63.refs_6_.refs_4_), channel_id=1, source_target_pairs={{0,96},{6,102},{24,120},{30,126},{96,0},{102,6},{120,24},{126,30},... | collective-permute-start | bytes 1572872 | tf_op jit(solution)/shard_map/ppermute | solution.py:51
  18.8 10.1 %slice-start.3 = ((s8[16777216]{0:T(1024)(128)(4,1)}), s8[4194304]{0:T(1024)(128)(4,1)S(1)}, s32[]{:S(2)}) async-start(s8[16777216]{0:T(1024)(128)(4,1)} %bitcast.3), calls=%async_computation.3 | async-start | bytes 8388608
  18.8 10.1 %copy-start = (bf16[2,2048,256]{2,1,0:T(8,128)(2,1)S(1)}, bf16[2,2048,256]{2,1,0:T(8,128)(2,1)}, u32[]{:S(2)}) copy-start(bf16[2,2048,256]{2,1,0:T(8,128)(2,1)} %drive.5) | copy-start | bytes 6291460
  18.8 10.1 %copy-start.1 = (f32[2,2048]{1,0:T(2,128)S(1)}, f32[2,2048]{1,0:T(2,128)}, u32[]{:S(2)}) copy-start(f32[2,2048]{1,0:T(2,128)} %part.3) | copy-start | bytes 49156
  21.1 9.6 %collective-permute-start.3 = (bf16[8,32,512]{2,1,0:T(8,128)(2,1)S(1)}, bf16[8,32,512]{2,1,0:T(8,128)(2,1)S(1)}, u32[]{:S(2)}, u32[]{:S(2)}) collective-permute-start(bf16[8,32,512]{2,1,0:T(8,128)(2,1)S(1)} %get-tuple-element.60), channel_id=1, source_target_pairs={{0,2},{6,4},{24,26},{30,28},{96,98},{102,100},{120,122},{126,124},... | collective-permute-start | bytes 786440 | tf_op jit(solution)/shard_map/ppermute | solution.py:51
  23.7 14.8 %collective-permute-start.12 = (bf16[8,32,512]{2,1,0:T(8,128)(2,1)S(1)}, bf16[8,32,512]{2,1,0:T(8,128)(2,1)S(1)}, u32[]{:S(2)}, u32[]{:S(2)}) collective-permute-start(bf16[8,32,512]{2,1,0:T(8,128)(2,1)S(1)} %get-tuple-element.71), channel_id=1, source_target_pairs={{0,42},{6,44},{24,50},{30,52},{96,74},{102,76},{120,82},{126,84},{... | collective-permute-start | bytes 786440 | tf_op jit(solution)/shard_map/ppermute | solution.py:51
  30.8 18.6 %collective-permute-start.13 = (bf16[512,512]{1,0:T(8,128)(2,1)S(1)}, bf16[512,512]{1,0:T(8,128)(2,1)S(1)}, u32[]{:S(2)}, u32[]{:S(2)}) collective-permute-start(bf16[512,512]{1,0:T(8,128)(2,1)S(1)} %get-tuple-element.74.refs_11_.refs_9_), channel_id=1, source_target_pairs={{0,6},{6,0},{24,30},{30,24},{96,102},{102,96},{120,126},{126,120},... | collective-permute-start | bytes 1572872 | tf_op jit(solution)/shard_map/ppermute | solution.py:51
  30.9 15.1 %collective-permute-start.10 = (bf16[8,32,512]{2,1,0:T(8,128)(2,1)S(1)}, bf16[8,32,512]{2,1,0:T(8,128)(2,1)S(1)}, u32[]{:S(2)}, u32[]{:S(2)}) collective-permute-start(bf16[8,32,512]{2,1,0:T(8,128)(2,1)S(1)} %get-tuple-element.69), channel_id=1, source_target_pairs={{0,8},{6,14},{24,16},{30,22},{96,104},{102,110},{120,112},{126,118... | collective-permute-start | bytes 786440 | tf_op jit(solution)/shard_map/ppermute | solution.py:51
  32.0 17.4 %collective-permute-start.11 = (bf16[8,32,512]{2,1,0:T(8,128)(2,1)S(1)}, bf16[8,32,512]{2,1,0:T(8,128)(2,1)S(1)}, u32[]{:S(2)}, u32[]{:S(2)}) collective-permute-start(bf16[8,32,512]{2,1,0:T(8,128)(2,1)S(1)} %get-tuple-element.70), channel_id=1, source_target_pairs={{0,32},{6,38},{24,56},{30,62},{96,64},{102,70},{120,88},{126,94},{... | collective-permute-start | bytes 786440 | tf_op jit(solution)/shard_map/ppermute | solution.py:51
  35.1 18.0 %collective-permute-start.18 = (bf16[8,32,512]{2,1,0:T(8,128)(2,1)S(1)}, bf16[8,32,512]{2,1,0:T(8,128)(2,1)S(1)}, u32[]{:S(2)}, u32[]{:S(2)}) collective-permute-start(bf16[8,32,512]{2,1,0:T(8,128)(2,1)S(1)} %get-tuple-element.80), channel_id=1, source_target_pairs={{0,10},{6,12},{24,18},{30,20},{96,106},{102,108},{120,114},{126,11... | collective-permute-start | bytes 786440 | tf_op jit(solution)/shard_map/ppermute | solution.py:51
  38.4 14.9 %collective-permute-start.19 = (bf16[8,32,512]{2,1,0:T(8,128)(2,1)S(1)}, bf16[8,32,512]{2,1,0:T(8,128)(2,1)S(1)}, u32[]{:S(2)}, u32[]{:S(2)}) collective-permute-start(bf16[8,32,512]{2,1,0:T(8,128)(2,1)S(1)} %get-tuple-element.81), channel_id=1, source_target_pairs={{0,34},{6,36},{24,58},{30,60},{96,66},{102,68},{120,90},{126,92},{... | collective-permute-start | bytes 786440 | tf_op jit(solution)/shard_map/ppermute | solution.py:51
  46.0 11.9 %collective-permute-start.20 = (bf16[8,32,512]{2,1,0:T(8,128)(2,1)S(1)}, bf16[8,32,512]{2,1,0:T(8,128)(2,1)S(1)}, u32[]{:S(2)}, u32[]{:S(2)}) collective-permute-start(bf16[8,32,512]{2,1,0:T(8,128)(2,1)S(1)} %get-tuple-element.82), channel_id=1, source_target_pairs={{0,40},{6,46},{24,48},{30,54},{96,72},{102,78},{120,80},{126,86},{... | collective-permute-start | bytes 786440 | tf_op jit(solution)/shard_map/ppermute | solution.py:51
  50.2 11.0 %collective-permute-start.14 = (bf16[8,32,512]{2,1,0:T(8,128)(2,1)S(1)}, bf16[8,32,512]{2,1,0:T(8,128)(2,1)S(1)}, u32[]{:S(2)}, u32[]{:S(2)}) collective-permute-start(bf16[8,32,512]{2,1,0:T(8,128)(2,1)S(1)} %get-tuple-element.76), channel_id=1, source_target_pairs={{0,2},{6,4},{24,26},{30,28},{96,98},{102,100},{120,122},{126,124},... | collective-permute-start | bytes 786440 | tf_op jit(solution)/shard_map/ppermute | solution.py:51
  50.7 12.9 %collective-permute-start.15 = (bf16[8,32,512]{2,1,0:T(8,128)(2,1)S(1)}, bf16[8,32,512]{2,1,0:T(8,128)(2,1)S(1)}, u32[]{:S(2)}, u32[]{:S(2)}) collective-permute-start(bf16[8,32,512]{2,1,0:T(8,128)(2,1)S(1)} %get-tuple-element.77), channel_id=1, source_target_pairs={{0,8},{6,14},{24,16},{30,22},{96,104},{102,110},{120,112},{126,118... | collective-permute-start | bytes 786440 | tf_op jit(solution)/shard_map/ppermute | solution.py:51
  53.2 12.8 %collective-permute-start.16 = (bf16[8,32,512]{2,1,0:T(8,128)(2,1)S(1)}, bf16[8,32,512]{2,1,0:T(8,128)(2,1)S(1)}, u32[]{:S(2)}, u32[]{:S(2)}) collective-permute-start(bf16[8,32,512]{2,1,0:T(8,128)(2,1)S(1)} %get-tuple-element.78), channel_id=1, source_target_pairs={{0,32},{6,38},{24,56},{30,62},{96,64},{102,70},{120,88},{126,94},{... | collective-permute-start | bytes 786440 | tf_op jit(solution)/shard_map/ppermute | solution.py:51
  53.4 12.6 %collective-permute-start.17 = (bf16[8,32,512]{2,1,0:T(8,128)(2,1)S(1)}, bf16[8,32,512]{2,1,0:T(8,128)(2,1)S(1)}, u32[]{:S(2)}, u32[]{:S(2)}) collective-permute-start(bf16[8,32,512]{2,1,0:T(8,128)(2,1)S(1)} %get-tuple-element.79), channel_id=1, source_target_pairs={{0,42},{6,44},{24,50},{30,52},{96,74},{102,76},{120,82},{126,84},{... | collective-permute-start | bytes 786440 | tf_op jit(solution)/shard_map/ppermute | solution.py:51
  58.7 10.4 %collective-permute-start.21 = (bf16[8,32,512]{2,1,0:T(8,128)(2,1)S(1)}, bf16[8,32,512]{2,1,0:T(8,128)(2,1)S(1)}, u32[]{:S(2)}, u32[]{:S(2)}) collective-permute-start(bf16[8,32,512]{2,1,0:T(8,128)(2,1)S(1)} %get-tuple-element.83), channel_id=1, source_target_pairs={{0,10},{6,12},{24,18},{30,20},{96,106},{102,108},{120,114},{126,11... | collective-permute-start | bytes 786440 | tf_op jit(solution)/shard_map/ppermute | solution.py:51
  61.2 9.8 %collective-permute-start.22 = (bf16[8,32,512]{2,1,0:T(8,128)(2,1)S(1)}, bf16[8,32,512]{2,1,0:T(8,128)(2,1)S(1)}, u32[]{:S(2)}, u32[]{:S(2)}) collective-permute-start(bf16[8,32,512]{2,1,0:T(8,128)(2,1)S(1)} %get-tuple-element.85), channel_id=1, source_target_pairs={{0,34},{6,36},{24,58},{30,60},{96,66},{102,68},{120,90},{126,92},{... | collective-permute-start | bytes 786440 | tf_op jit(solution)/shard_map/ppermute | solution.py:51
  63.6 9.4 %collective-permute-start.23 = (bf16[8,32,512]{2,1,0:T(8,128)(2,1)S(1)}, bf16[8,32,512]{2,1,0:T(8,128)(2,1)S(1)}, u32[]{:S(2)}, u32[]{:S(2)}) collective-permute-start(bf16[8,32,512]{2,1,0:T(8,128)(2,1)S(1)} %get-tuple-element.86), channel_id=1, source_target_pairs={{0,40},{6,46},{24,48},{30,54},{96,72},{102,78},{120,80},{126,86},{... | collective-permute-start | bytes 786440 | tf_op jit(solution)/shard_map/ppermute | solution.py:51
  73.0 1.8 %copy-start.2 = (f32[2,256]{1,0:T(2,128)S(1)}, f32[2,256]{1,0:T(2,128)}, u32[]{:S(2)}) copy-start(f32[2,256]{1,0:T(2,128)} %hole.1) | copy-start | bytes 6148
  74.7 2.7 %collective-permute-start.24 = (bf16[2048,256]{1,0:T(8,128)(2,1)S(1)}, bf16[2048,256]{1,0:T(8,128)(2,1)S(1)}, u32[]{:S(2)}, u32[]{:S(2)}) collective-permute-start(bf16[2048,256]{1,0:T(8,128)(2,1)S(1)} %final_other.1.refs_2_), channel_id=1, source_target_pairs={{0,1},{1,0},{2,3},{3,2},{4,5},{5,4},{6,7},{7,6},{8,9},{9,8},{10,11... | collective-permute-start | bytes 3145736 | tf_op jit(solution)/shard_map/ppermute | solution.py:47
